TPU v7x, 128 devices: a whole 4x4x4 slice. The times are simulated.
128 devices in a mesh: grp: 16 (over x, y), tp: 8 (over z, core).
Axes of the slice: x: 4, y: 4, z: 4, core: 2. Of those that a mesh axis runs over, the one named last changes fastest.
Arguments:
- sel_hidden: bfloat16 [32, 320, 4096], P('grp'), may hold values from -6 to 6
- norm_gain: float32 [4096], replicated, may hold values from 0.25 to 1.75
- w_query: bfloat16 [4096, 4096], P(None, 'tp'), may hold values from -0.09375 to 0.09375
- w_key: bfloat16 [4096, 1024], P(None, 'tp'), may hold values from -0.1875 to 0.1875
- w_value: bfloat16 [4096, 1024], P(None, 'tp'), may hold values from -0.09375 to 0.09375
- w_out: bfloat16 [4096, 4096], P(None, 'tp'), may hold values from -0.09375 to 0.09375
- doc_cache: bfloat16 [256, 2, 512, 1024], P('grp', None, None, 'tp'), may hold values from -250 to 250
- home: int32 [256], replicated, may hold values from 0 to 255, as said below
- doc_ids: int32 [32, 8], replicated, may hold values from 0 to 255, as said below
- doc_len: int32 [256], replicated, may hold values from 128 to 512, as said below
- positions: int32 [32, 320], P('grp'), may hold values from 0 to 4095, as said below
Outputs:
- mixed: bfloat16 [32, 320, 4096], P('grp', None, 'tp')
Inputs may be any that keep to these rules, and one draw needn't show every extreme that they name: `home`: a permutation: every location holds one document; the owner of location l along grp is l // 16. `doc_ids`: requests g * 2 .. (g + 1) * 2 - 1 form serving group g; the 16 documents of one group all differ, no owner holds more than 2 of them, and in every group at least one owner holds exactly 2. `doc_len`: documents doc_ids[0, 0] and doc_ids[0, 7] have length 512 (others may too). positions: each row rises; for each j it holds 40 positions j * 512 + t with t below the length of document doc_ids[r, j].
All inputs are finite; a program needn't handle non-finite values.
Results may differ from a plain program's by a relative error of at most 0.006.
The roundings to bfloat16 on the way count: a program that leaves them out, or rounds other values in their place, can miss the bound.
Values may be sent and summed in bfloat16 or wider, within the bound.
No kernel may reach another device: no remote copies, remote signals or barrier semaphores. Data moves between devices by JAX's collectives and lax.ppermute only.
A program may use at most 192 MiB of HBM per device.

v0:
```python
import jax
import jax.numpy as jnp
from jax import lax
from jax.sharding import PartitionSpec as P

H = 32
KVH = 8
HD = 128
CAP = 2


def body(
    sel_hidden,
    norm_gain,
    w_query,
    w_key,
    w_value,
    w_out,
    doc_cache,
    home,
    doc_ids,
    doc_len,
    positions,
):
    groups = lax.axis_size("grp")
    me = lax.axis_index("grp")
    stored = doc_cache.shape[0]
    doc_rows = doc_cache.shape[2]
    width = doc_cache.shape[3]
    group = H // KVH
    scale = HD ** (-0.5)
    served = sel_hidden.shape[0]
    tokens = sel_hidden.shape[1]
    retrieved = doc_ids.shape[1]
    per_group = served * retrieved
    picks = tokens // retrieved
    location = home[doc_ids].reshape(groups, per_group)
    owner = location // stored
    slot_index = location % stored
    slots = jnp.arange(per_group, dtype=jnp.int32)
    earlier = (owner[:, :, None] == owner[:, None, :]) & (
        slots[None, None, :] < slots[None, :, None]
    )
    rank = jnp.sum(earlier.astype(jnp.int32), axis=2)
    match = (owner == me)[:, :, None] & (
        rank[:, :, None] == jnp.arange(CAP, dtype=jnp.int32)[None, None, :]
    )
    chosen = jnp.sum(jnp.where(match, slot_index[:, :, None], 0), axis=1)
    outgoing = doc_cache[chosen]
    incoming = lax.all_to_all(outgoing, "grp", split_axis=0, concat_axis=0, tiled=True)
    own_owner = owner[me]
    own_rank = rank[me]
    flat = incoming.reshape((groups * CAP,) + incoming.shape[2:])
    context = flat[own_owner * CAP + own_rank].reshape((served, retrieved) + flat.shape[1:])
    xf = sel_hidden.astype(jnp.float32)
    normed = (xf * lax.rsqrt(jnp.mean(xf * xf, axis=-1, keepdims=True) + 1e-05) * norm_gain).astype(
        jnp.bfloat16
    )
    normed_rows = normed.reshape(served * tokens, normed.shape[2])
    query = (
        jnp.dot(normed_rows, w_query, preferred_element_type=jnp.float32)
        .astype(jnp.bfloat16)
        .reshape(served, tokens, w_query.shape[1])
    )
    key_new = (
        jnp.dot(normed_rows, w_key, preferred_element_type=jnp.float32)
        .astype(jnp.bfloat16)
        .reshape(served, tokens, width)
    )
    value_new = (
        jnp.dot(normed_rows, w_value, preferred_element_type=jnp.float32)
        .astype(jnp.bfloat16)
        .reshape(served, tokens, width)
    )
    total_rows = retrieved * doc_rows
    keys_old = context[:, :, 0].reshape(served, total_rows, width)
    values_old = context[:, :, 1].reshape(served, total_rows, width)
    doc_rows_at = (
        jnp.arange(retrieved, dtype=jnp.int32)[:, None] * doc_rows
        + jnp.arange(doc_rows, dtype=jnp.int32)[None, :]
    )
    per_doc = positions.reshape(served, retrieved, picks)
    replaced = jnp.any(per_doc[:, :, :, None] == doc_rows_at[None, :, None, :], axis=2).reshape(
        served, total_rows
    )
    lengths = doc_len[doc_ids.reshape(groups, served, retrieved)[me]]
    valid = (jnp.arange(doc_rows, dtype=jnp.int32)[None, None, :] < lengths[:, :, None]).reshape(
        served, total_rows
    )
    keep_old = valid & jnp.logical_not(replaced)
    visible_old = keep_old[:, None, :] & (
        jnp.arange(total_rows, dtype=jnp.int32)[None, None, :] <= positions[:, :, None]
    )
    visible_new = positions[:, None, :] <= positions[:, :, None]
    query_h = query.reshape(served, tokens, group, HD)
    scores_old = (
        jnp.einsum("rqgd,rkd->rgqk", query_h, keys_old, preferred_element_type=jnp.float32) * scale
    )
    scores_old = jnp.where(visible_old[:, None], scores_old, -1e30)
    scores_new = (
        jnp.einsum("rqgd,rkd->rgqk", query_h, key_new, preferred_element_type=jnp.float32) * scale
    )
    scores_new = jnp.where(visible_new[:, None], scores_new, -1e30)
    top = jnp.maximum(
        jnp.max(scores_old, axis=-1, keepdims=True), jnp.max(scores_new, axis=-1, keepdims=True)
    )
    expo_old = jnp.exp(scores_old - top)
    expo_new = jnp.exp(scores_new - top)
    total = jnp.sum(expo_old, axis=-1, keepdims=True) + jnp.sum(expo_new, axis=-1, keepdims=True)
    weights_old = (expo_old / total).astype(jnp.bfloat16)
    weights_new = (expo_new / total).astype(jnp.bfloat16)
    attn = jnp.einsum("rgqk,rkd->rqgd", weights_old, values_old, preferred_element_type=jnp.float32)
    attn = attn + jnp.einsum(
        "rgqk,rkd->rqgd", weights_new, value_new, preferred_element_type=jnp.float32
    )
    outputs = attn.astype(jnp.bfloat16).reshape(served * tokens, group * HD)
    mixed = jnp.dot(
        lax.all_gather(outputs, "tp", axis=1, tiled=True), w_out, preferred_element_type=jnp.float32
    )
    return mixed.astype(jnp.bfloat16).reshape(served, tokens, w_out.shape[1])


def solution(mesh):
    return jax.shard_map(
        body,
        mesh=mesh,
        in_specs=(
            P("grp", None, None),
            P(),
            P(None, "tp"),
            P(None, "tp"),
            P(None, "tp"),
            P(None, "tp"),
            P("grp", None, None, "tp"),
            P(),
            P(),
            P(),
            P("grp", None),
        ),
        out_specs=P("grp", None, "tp"),
        check_vma=False,
    )
```

profile of v0, /device:TPU:1, one launch (start us, length us, event | category | flops | bytes accessed | tf_op | source)
XLA Modules:
  0.0 307.0 jit_solution(3321386081842237147)
XLA Ops:
  6.5 0.8 compare_select_fusion
  7.5 1.9 gather_fusion
  10.3 7.1 %gather_fusion.1 = bf16[32,2,512,128]{3,2,1,0:T(8,128)(2,1)} fusion(bf16[16,2,512,128]{3,2,1,0:T(8,128)(2,1)} %param.17, s32[1024]{0:T(1024)S(1)} %pad_clamp_fusion.2), kind=kCustom, calls=%fused_computation.1 | custom fusion | bytes 16777344 | tf_op jit(solution)/shard_map/gather | solution.py:49
  17.5 7.7 %all-to-all-start = ((bf16[16,2,2,512,128]{4,3,2,1,0:T(8,128)(2,1)}), bf16[16,2,2,512,128]{4,3,2,1,0:T(8,128)(2,1)}, u32[]{:S(2)}, u32[]{:S(2)}) async-start(bf16[16,2,2,512,128]{4,3,2,1,0:T(8,128)(2,1)} %bitcast.94), calls=%async_computation | async-start | bytes 16777216 | tf_op jit(solution)/shard_map/all_to_all | solution.py:50
  26.0 0.7 gather_fusion.3
  26.9 3.6 %fusion.3 = f32[2,320]{1,0:T(2,128)S(1)} fusion(bf16[2,320,4096]{2,1,0:T(8,128)(2,1)} %param.11), kind=kLoop, calls=%fused_computation.12 | loop fusion | flops 7863680 | bytes 5245440 | tf_op jit(solution)/shard_map/reduce_sum | solution.py:56
  30.5 4.5 %fusion.5 = bf16[2,320,4096]{2,1,0:T(8,128)(2,1)S(1)} fusion(bf16[2,320,4096]{2,1,0:T(8,128)(2,1)} %param.11, f32[4096]{0:T(1024)S(1)} %copy-done.6, f32[2,320]{1,0:T(2,128)S(1)} %add_rsqrt_fusion), kind=kLoop, calls=%fused_computation.14 | loop fusion | flops 10485760 | bytes 10504704 | tf_op jit(solution)/shard_map/convert_element_type | solution.py:56
  35.1 2.3 copy-done.4
  37.4 2.9 convolution_convert_fusion.1
  40.7 4.2 %convolution_convert_fusion.3 = bf16[640,128]{1,0:T(8,128)(2,1)S(1)} fusion(bf16[640,4096]{1,0:T(8,128)(2,1)} %bitcast.97, bf16[4096,128]{1,0:T(8,128)(2,1)S(1)} %copy-done), kind=kOutput, calls=%fused_computation.30 | convolution fusion | flops 671170560 | bytes 6455296 | tf_op jit(solution)/shard_map/dot_general | solution.py:66
  44.9 2.8 fusion.8
  47.6 1.5 convolution_convert_fusion.2
  49.2 4.0 %fusion.6 = pred[2,320,4096]{2,1,0:T(8,128)(4,1)} fusion(s32[2,320]{1,0:T(2,128)S(1)} %copy-done.5, pred[2,4096]{1,0:T(4,128)(4,1)S(1)} %compare_and_fusion), kind=kLoop, calls=%fused_computation.16 | loop fusion | flops 5242880 | bytes 2632192 | tf_op jit(solution)/shard_map/and | solution.py:91
  53.2 118.1 %all-to-all-done = bf16[16,2,2,512,128]{4,3,2,1,0:T(8,128)(2,1)} async-done(((bf16[16,2,2,512,128]{4,3,2,1,0:T(8,128)(2,1)}), bf16[16,2,2,512,128]{4,3,2,1,0:T(8,128)(2,1)}, u32[]{:S(2)}, u32[]{:S(2)}) %all-to-all-start) | async-done | bytes 8388640 | tf_op jit(solution)/shard_map/all_to_all | solution.py:50
  171.3 6.6 %gather_fusion.2 = bf16[16,2,512,128]{3,2,1,0:T(8,128)(2,1)} fusion(bf16[32,2,512,128]{3,2,1,0:T(8,128)(2,1)} %bitcast.2, s32[1024]{0:T(1024)S(1)} %pad_clamp_fusion.1), kind=kCustom, calls=%fused_computation.2 | custom fusion | bytes 8388672 | tf_op jit(solution)/shard_map/gather | solution.py:54
  177.9 4.6 %fusion.27 = (bf16[2,8,1,512,128]{4,3,2,1,0:T(8,128)(2,1)}, bf16[2,8,1,512,128]{4,3,2,1,0:T(8,128)(2,1)}) fusion(bf16[2,8,2,512,128]{4,3,2,1,0:T(8,128)(2,1)} %bitcast.95), kind=kLoop, calls=%fused_computation.75 | loop fusion | bytes 8388608 | tf_op jit(solution)/shard_map/slice | solution.py:77
  182.6 18.9 %fusion.1 = (f32[2,4,320]{2,1,0:T(4,128)S(1)}, f32[2,4096,320,4]{1,2,3,0:T(8,128)}) fusion(pred[2,320,4096]{2,1,0:T(8,128)(4,1)} %fusion.6, bf16[2,4096,128,1]{2,1,3,0:T(8,128)(2,1)} %bitcast.104, bf16[2,320,4,128]{3,2,1,0:T(4,128)(2,1)S(1)} %reshape_reshape.3), kind=kOutput, calls=%fused_computation.8 | convolution fusion | flops 2715809280 | bytes 47327232 | tf_op jit(solution)/shard_map/rqgd,rkd->rgqk/dot_general | solution.py:97
  201.5 3.0 fusion.7
  204.5 21.2 %fusion = f32[2,4,320]{2,1,0:T(4,128)S(1)} fusion(f32[2,4096,320,4]{1,2,3,0:T(8,128)} %get-tuple-element.10, f32[2,4,320]{2,1,0:T(4,128)S(1)} %max.8, pred[2,320,4096]{2,1,0:T(8,128)(4,1)} %fusion.6), kind=kLoop, calls=%fused_computation.7 | loop fusion | flops 41940480 | bytes 44584960 | tf_op jit(solution)/shard_map/reduce_sum | solution.py:109
  225.8 3.5 %fusion.9 = f32[2,128,4,320]{1,3,2,0:T(8,128)S(1)} fusion(bf16[2,320,128,1]{2,1,3,0:T(8,128)(2,1)S(1)} %bitcast.110, f32[2,320,320,4]{2,1,3,0:T(8,128)} %get-tuple-element.12, f32[2,4,320]{2,1,0:T(4,128)S(1)} %add.134, f32[2,4,320]{2,1,0:T(4,128)S(1)} %max.8, pred[2,320,320]{1,2,0:T(8,128)(4,1)S(1)} %broadcast_compare_fusion), kind=kOutput, calls=%fused_computation.22 | convolution fusion | flops 213811200 | bytes 4976640 | tf_op jit(solution)/shard_map/rgqk,rkd->rqgd/dot_general | solution.py:113
  229.2 19.2 %fusion.12 = bf16[2,320,4,128]{3,1,2,0:T(8,128)(2,1)S(1)} fusion(f32[2,128,4,320]{1,3,2,0:T(8,128)S(1)} %fusion.9, bf16[2,4096,128,1]{2,1,3,0:T(8,128)(2,1)} %bitcast.103, f32[2,4096,320,4]{1,2,3,0:T(8,128)} %get-tuple-element.10, f32[2,4,320]{2,1,0:T(4,128)S(1)} %add.134, f32[2,4,320]{2,1,0:T(4,128)S(1)} %max.8, pred[2,320,4096]{2,1,0:T(8,128)(4,1)} %fusion.6), kind=kOutput, calls=%fused_computation.28 | convolution fusion | flops 2737438720 | bytes 48648192 | tf_op jit(solution)/shard_map/rgqk,rkd->rqgd/dot_general | solution.py:112
  248.9 0.9 copy.55
  249.9 42.8 %all-gather.2.cloned.1.call-done = bf16[640,4096]{1,0:T(8,128)(2,1)} async-done(((bf16[640,512]{1,0:T(8,128)(2,1)}), bf16[640,4096]{1,0:T(8,128)(2,1)}) %all-gather.2.cloned.1.call-update) | async-done | bytes 5242896 | tf_op jit(solution)/shard_map/all_gather | solution.py:118
  292.7 7.5 %convolution_convert_fusion = bf16[640,512]{1,0:T(8,128)(2,1)} fusion(bf16[640,4096]{1,0:T(8,128)(2,1)} %all-gather.2.cloned.1.call-done, bf16[4096,512]{1,0:T(8,128)(2,1)} %param.16), kind=kOutput, calls=%fused_computation.24 | convolution fusion | flops 2684682240 | bytes 10092544 | tf_op jit(solution)/shard_map/dot_general | solution.py:117
  (62 shorter events, 3.0 us)
Async XLA Ops:
  6.5 34.1 %copy-start = (bf16[4096,128]{1,0:T(8,128)(2,1)S(1)}, bf16[4096,128]{1,0:T(8,128)(2,1)}, u32[]{:S(2)}) copy-start(bf16[4096,128]{1,0:T(8,128)(2,1)} %param.14) | copy-start | bytes 3145732
  6.5 1.0 copy-start.2
  17.5 7.8 %copy-start.7 = (s32[32,8]{0,1:T(8,128)S(1)}, s32[32,8]{0,1:T(8,128)}, u32[]{:S(2)}) copy-start(s32[32,8]{0,1:T(8,128)} %param.19) | copy-start | bytes 3076
  17.5 7.8 %copy-start.5 = (s32[2,320]{1,0:T(2,128)S(1)}, s32[2,320]{1,0:T(2,128)}, u32[]{:S(2)}) copy-start(s32[2,320]{1,0:T(2,128)} %param.21) | copy-start | bytes 7684
  17.5 8.5 %copy-start.3 = (s32[256]{0:T(256)S(1)}, s32[256]{0:T(256)}, u32[]{:S(2)}) copy-start(s32[256]{0:T(256)} %param.20) | copy-start | bytes 3076
  17.5 153.8 %all-to-all-start = ((bf16[16,2,2,512,128]{4,3,2,1,0:T(8,128)(2,1)}), bf16[16,2,2,512,128]{4,3,2,1,0:T(8,128)(2,1)}, u32[]{:S(2)}, u32[]{:S(2)}) async-start(bf16[16,2,2,512,128]{4,3,2,1,0:T(8,128)(2,1)} %bitcast.94), calls=%async_computation | async-start | bytes 16777216 | tf_op jit(solution)/shard_map/all_to_all | solution.py:50
  25.2 5.3 %copy-start.6 = (f32[4096]{0:T(1024)S(1)}, f32[4096]{0:T(1024)}, u32[]{:S(2)}) copy-start(f32[4096]{0:T(1024)} %param.12) | copy-start | bytes 49156
  25.2 267.5 %all-gather.2.cloned.1.call-start = ((), (), s32[]{:S(2)}) async-start(), calls=%async_computation.1 | async-start | bytes 5898240 | tf_op jit(solution)/shard_map/all_gather | solution.py:118
  30.5 6.9 %copy-start.8 = (bf16[4096,512]{1,0:T(8,128)(2,1)S(1)}, bf16[4096,512]{1,0:T(8,128)(2,1)}, u32[]{:S(2)}) copy-start(bf16[4096,512]{1,0:T(8,128)(2,1)} %param.13) | copy-start | bytes 12582916
  35.1 2.3 copy-start.4
  40.5 7.2 %slice-start = ((s8[5242880]{0:T(1024)(128)(4,1)}), s8[4194304]{0:T(1024)(128)(4,1)S(1)}, s32[]{:S(2)}) async-start(s8[5242880]{0:T(1024)(128)(4,1)} %bitcast.98), calls=%async_computation.2 | async-start | bytes 8388608
  40.7 6.9 %slice-start.1 = ((s8[5242880]{0:T(1024)(128)(4,1)}), s8[1048576]{0:T(1024)(128)(4,1)S(1)}, s32[]{:S(2)}) async-start(s8[5242880]{0:T(1024)(128)(4,1)} %bitcast.98), calls=%async_computation.3 | async-start | bytes 2097152
  44.9 2.8 copy-start.9
  292.6 7.5 %copy-start.1 = (bf16[4096,128]{1,0:T(8,128)(2,1)S(1)}, bf16[4096,128]{1,0:T(8,128)(2,1)}, u32[]{:S(2)}) copy-start(bf16[4096,128]{1,0:T(8,128)(2,1)} %param.14) | copy-start | bytes 3145732
Sparse Core Ops, SparseCore 0:
  250.0 42.6 all-gather.1
where the time goes:
time: 308 us; the launch traced here: 307 us
  waiting for transfers between devices  161 us (52%)
  matrix products  60.4 us (20%)
  other arithmetic  38.5 us (12%)
  local copies, waits for them, and re-layouts  25.8 us (8%)
  between operations  13.7 us (4%)
  starting transfers between devices  7.72 us (3%)
    all_to_all x1, waiting for transfers between devices, body(): lax.all_to_all(outgoing, 'grp', split_axis=0, concat_axis=0, tiled=True)  118 us
    all_gather x1, waiting for transfers between devices, body(): lax.all_gather(outputs, 'tp', axis=1, tiled=True)  42.8 us
    reduce_sum x1, other arithmetic, body(): jnp.sum(expo_old, axis=-1, keepdims=True)  21.2 us
    dot_general x1, matrix products, body(): jnp.einsum('rgqk,rkd->rqgd', weights_old, values_old, preferred_element_t...  19.2 us
    dot_general x1, matrix products, body(): jnp.einsum('rqgd,rkd->rgqk', query_h, keys_old, preferred_element_type=jn...  18.9 us
    all_to_all x1, starting transfers between devices, body(): lax.all_to_all(outgoing, 'grp', split_axis=0, concat_axis=0, tiled=True)  7.67 us
    dot_general x1, matrix products, body(): jnp.dot(lax.all_gather(outputs, 'tp', axis=1, tiled=True), w_out, preferr...  7.53 us
    gather x1, local copies, waits for them, and re-layouts, body(): outgoing = doc_cache[chosen]  7.14 us
  transfers between devices with their start and end apart: 2, of which 2 were waited for; matrix products, arithmetic and copies ran while one was open for 8% of the time, Pallas kernels for 0%

commit v1 on v0

v1 whole, which is shorter than its diff:
```python
import functools
import math

import jax
import jax.numpy as jnp
from jax import lax
from jax.experimental import pallas as pl
from jax.experimental.pallas import tpu as pltpu
from jax.sharding import PartitionSpec as P

H = 32
KVH = 8
HD = 128
CAP = 2
GROUP = H // KVH
SIDE = 4
GROUPS = 16
DOC = 512
TOKENS = 320
RETRIEVED = 8
TILES = 4
SUB = TOKENS // TILES
ROWS = SUB * GROUP
PADDED = 384
FAR = 2**30
EXP2 = HD ** (-0.5) * math.log2(math.e)

NEAR = [(1, 0), (3, 0), (0, 1), (0, 3)]
DIAGONAL = [(1, 1), (3, 3), (1, 3), (3, 1)]
TWO = [(2, 0), (0, 2)]
OPPOSITE = [(2, 2)]
KNIGHT = {(0, 1): (2, 1), (0, 3): (2, 3), (1, 0): (1, 2), (3, 0): (3, 2)}
SHIFTS = NEAR + DIAGONAL + TWO + OPPOSITE + [KNIGHT[s] for s in NEAR]

ANY = pl.BlockSpec(memory_space=pl.ANY)
VMEM = pl.BlockSpec(memory_space=pltpu.VMEM)
SMEM = pl.BlockSpec(memory_space=pltpu.SMEM)


def shift(block, by):
    pairs = [
        (x * SIDE + y, (x + by[0]) % SIDE * SIDE + (y + by[1]) % SIDE)
        for x in range(SIDE)
        for y in range(SIDE)
    ]
    return lax.ppermute(block, "grp", pairs)


def pack_kernel(me_ref, chosen_ref, cache_ref, *refs):
    out_refs, sem = refs[: len(SHIFTS)], refs[len(SHIFTS)]
    me = me_ref[0]
    x, y = me // SIDE, me % SIDE

    def each(act):
        for (dx, dy), out in zip(SHIFTS, out_refs):
            g = (x + dx) % SIDE * SIDE + (y + dy) % SIDE
            for k in range(CAP):
                doc = chosen_ref[g * CAP + k]

                @pl.when(doc >= 0)
                def _():
                    act(pltpu.make_async_copy(cache_ref.at[doc], out.at[k], sem))

    each(lambda copy: copy.start())
    each(lambda copy: copy.wait())


def pack(me, chosen, cache):
    return pl.pallas_call(
        pack_kernel,
        out_shape=[jax.ShapeDtypeStruct((CAP, 2, DOC, HD), jnp.bfloat16)] * len(SHIFTS),
        in_specs=[SMEM, SMEM, ANY],
        out_specs=[ANY] * len(SHIFTS),
        scratch_shapes=[pltpu.SemaphoreType.DMA],
        cost_estimate=pl.CostEstimate(flops=0, bytes_accessed=10 << 20, transcendentals=0),
        name="pack",
    )(me, chosen, cache)


def attend_kernel(counts, first, last, table_ref, q_ref, pos_ref, idx_ref, *refs):
    refs = list(refs)
    if first:
        new_idx_ref, new_k_ref, new_v_ref = refs[:3]
        refs = refs[3:]
    else:
        old = refs[:3]
        refs = refs[3:]
    arrays = refs[: len(counts)]
    refs = refs[len(counts) :]
    if last:
        out_ref = refs[0]
        acc, m, l, buf, sem = refs[1:]
    else:
        acc, m, l = refs[:3]
        buf, sem = refs[3:]

    total = sum(min(c, CAP) for c in counts)
    at = 0
    plan = []
    for array, count in zip(arrays, counts):
        for k in range(CAP):
            plan.append((at, array, k, count > CAP))
            at += 1
    for at, array, k, dynamic in plan:

        @pl.when(table_ref[2 * at] >= 0)
        def _(at=at, array=array, k=k, dynamic=dynamic):
            where = table_ref[2 * at + 1] if dynamic else k
            pltpu.make_async_copy(array.at[where], buf.at[at], sem.at[at]).start()

    def tile_queries(tile):
        rows = pl.ds(pl.multiple_of(tile * SUB, SUB), SUB)
        return jnp.concatenate(
            [q_ref[rows, h * HD : (h + 1) * HD] for h in range(GROUP)], axis=0
        )

    def scores(tile, keys, idx):
        s = lax.dot_general(
            tile_queries(tile), keys, (((1,), (1,)), ((), ())), preferred_element_type=jnp.float32
        )
        return jnp.where(idx <= pos_ref[tile], s, -1e30)

    if first:

        def start(tile, carry):
            s = scores(tile, new_k_ref[...], new_idx_ref[...])
            top = jnp.max(s, axis=1, keepdims=True)
            p = jnp.exp2((s - top) * EXP2)
            m[tile] = top
            l[tile] = jnp.sum(p, axis=1, keepdims=True)
            acc[tile] = jnp.dot(
                p.astype(jnp.bfloat16), new_v_ref[...], preferred_element_type=jnp.float32
            )
            return carry

        lax.fori_loop(0, TILES, start, 0)
    else:
        for new, prev in zip((acc, m, l), old):
            new[...] = prev[...]

    def item(at, carry):
        j = table_ref[2 * at]

        @pl.when(j >= 0)
        def _():
            pltpu.make_async_copy(arrays[0].at[0], buf.at[at], sem.at[at]).wait()

            def step(tile, carry):
                s = scores(tile, buf[at, 0], idx_ref[j])
                before = m[tile]
                top = jnp.maximum(before, jnp.max(s, axis=1, keepdims=True))
                p = jnp.exp2((s - top) * EXP2)
                fade = jnp.exp2((before - top) * EXP2)
                m[tile] = top
                l[tile] = l[tile] * fade + jnp.sum(p, axis=1, keepdims=True)
                acc[tile] = acc[tile] * fade + jnp.dot(
                    p.astype(jnp.bfloat16), buf[at, 1], preferred_element_type=jnp.float32
                )
                return carry

            lax.fori_loop(j // 2, TILES, step, 0)

        return carry

    lax.fori_loop(0, total, item, 0)

    if last:
        for tile in range(TILES):
            done = (acc[tile] / l[tile]).astype(jnp.bfloat16)
            for h in range(GROUP):
                out_ref[tile * SUB : (tile + 1) * SUB, h * HD : (h + 1) * HD] = done[
                    h * SUB : (h + 1) * SUB
                ]


def attend(table, query, pos, idx, extra, arrays, first, last):
    counts = [a.shape[0] for a in arrays]
    cands = CAP * len(arrays)
    state = [
        jax.ShapeDtypeStruct((TILES, ROWS, HD), jnp.float32),
        jax.ShapeDtypeStruct((TILES, ROWS, 1), jnp.float32),
        jax.ShapeDtypeStruct((TILES, ROWS, 1), jnp.float32),
    ]
    scratch = [
        pltpu.VMEM((cands, 2, DOC, HD), jnp.bfloat16),
        pltpu.SemaphoreType.DMA((cands,)),
    ]
    if last:
        out_shape = jax.ShapeDtypeStruct((TOKENS, GROUP * HD), jnp.bfloat16)
        scratch = [pltpu.VMEM(s.shape, s.dtype) for s in state] + scratch
        out_specs = VMEM
    else:
        out_shape, out_specs = state, [VMEM] * 3
    return pl.pallas_call(
        functools.partial(attend_kernel, counts, first, last),
        out_shape=out_shape,
        in_specs=[SMEM, VMEM, VMEM, VMEM] + [VMEM] * 3 + [ANY] * len(arrays),
        out_specs=out_specs,
        scratch_shapes=scratch,
        compiler_params=pltpu.CompilerParams(vmem_limit_bytes=40 << 20),
        cost_estimate=pl.CostEstimate(
            flops=2 * 2 * 1280 * 512 * 128 * len(arrays) // 2,
            bytes_accessed=(6 << 20) + len(arrays) * (1 << 18),
            transcendentals=1280 * 512 * len(arrays) // 2,
        ),
        name="attend",
    )(table, query, pos, idx, *extra, *arrays)


def project_kernel(place_ref, *refs):
    parts, w_ref, out_ref = refs[:-2], refs[-2], refs[-1]
    total = None
    for n, part in enumerate(parts):
        rows = pl.ds(pl.multiple_of(place_ref[n] * (GROUP * HD), GROUP * HD), GROUP * HD)
        term = jnp.dot(part[...], w_ref[rows, :], preferred_element_type=jnp.float32)
        total = term if total is None else total + term
    out_ref[...] = total.astype(jnp.bfloat16)


def project(place, parts, w_out):
    return pl.pallas_call(
        project_kernel,
        out_shape=jax.ShapeDtypeStruct((TOKENS, w_out.shape[1]), jnp.bfloat16),
        in_specs=[SMEM] + [VMEM] * (len(parts) + 1),
        out_specs=VMEM,
        compiler_params=pltpu.CompilerParams(vmem_limit_bytes=40 << 20),
        cost_estimate=pl.CostEstimate(
            flops=2 * TOKENS * 4096 * 512, bytes_accessed=7 << 20, transcendentals=0
        ),
        name="project",
    )(place, *parts, w_out)


def ring(block, by):
    return lax.ppermute(block, "tp", [(i, (i + 2 * by) % KVH) for i in range(KVH)])


def other_core(block):
    return lax.ppermute(block, "tp", [(i, i ^ 1) for i in range(KVH)])


def gather(own):
    half = TOKENS // 2
    up, down = ring(own, 1), ring(own, -1)
    far_up, far_down = ring(up[:half], 1), ring(down[half:], -1)
    far = jnp.concatenate([far_up, far_down], axis=0)
    parts = [own, up, down, far]
    return parts + [other_core(p) for p in parts]


def body(
    sel_hidden,
    norm_gain,
    w_query,
    w_key,
    w_value,
    w_out,
    doc_cache,
    home,
    doc_ids,
    doc_len,
    positions,
):
    me = lax.axis_index("grp")
    stored = doc_cache.shape[0]
    served = sel_hidden.shape[0]
    per_group = served * RETRIEVED

    with jax.named_scope("tables"):
        location = home[doc_ids].reshape(GROUPS, per_group)
        owner = location // stored
        slot_index = location % stored
        slots = jnp.arange(per_group, dtype=jnp.int32)
        earlier = (owner[:, :, None] == owner[:, None, :]) & (
            slots[None, None, :] < slots[None, :, None]
        )
        rank = jnp.sum(earlier.astype(jnp.int32), axis=2)
        ranks = jnp.arange(CAP, dtype=jnp.int32)
        match = (owner == me)[:, :, None] & (rank[:, :, None] == ranks)
        chosen = jnp.max(jnp.where(match, slot_index[:, :, None], -1), axis=1).reshape(-1)
    with jax.named_scope("pack"):
        packed = dict(zip(SHIFTS, pack(me.reshape(1), chosen, doc_cache)))
    with jax.named_scope("documents"):
        arrived = {}
        relayed = {s: shift(packed[KNIGHT[s]], s) for s in NEAR}
        for s in NEAR + DIAGONAL:
            arrived[s] = shift(packed[s], s)
        later = TWO + OPPOSITE
        held, _ = lax.optimization_barrier(
            (
                (relayed, {s: packed[s] for s in later}),
                [arrived[s] for s in NEAR + DIAGONAL],
            )
        )
        for s in later:
            arrived[s] = shift(held[1][s], s)
        for s in NEAR:
            arrived[KNIGHT[s]] = shift(held[0][s], (2, 0) if s[0] == 0 else (0, 2))

    with jax.named_scope("receive_tables"):
        x, y = me // SIDE, me % SIDE
        own_owner, own_rank, own_slot = owner[me], rank[me], slot_index[me]

        def table(r, shifts):
            rows = []
            span = slice(r * RETRIEVED, (r + 1) * RETRIEVED)
            sources = jnp.stack(
                [(x - dx) % SIDE * SIDE + (y - dy) % SIDE for dx, dy in shifts]
            )
            hit = (own_owner[span][None, None, :] == sources[:, None, None]) & (
                own_rank[span][None, None, :] == ranks[None, :, None]
            )
            j = jnp.max(
                jnp.where(hit, jnp.arange(RETRIEVED, dtype=jnp.int32), -1), axis=2
            )
            at = jnp.max(jnp.where(hit, own_slot[span][None, None, :], -1), axis=2)
            return jnp.stack([j, at], axis=-1).reshape(-1)

        doc_rows = (
            jnp.arange(RETRIEVED, dtype=jnp.int32)[:, None] * DOC
            + jnp.arange(DOC, dtype=jnp.int32)[None, :]
        )
        per_doc = positions.reshape(served, RETRIEVED, TOKENS // RETRIEVED)
        replaced = jnp.any(per_doc[:, :, :, None] == doc_rows[None, :, None, :], axis=2)
        lengths = doc_len[doc_ids.reshape(GROUPS, served, RETRIEVED)[me]]
        valid = jnp.arange(DOC, dtype=jnp.int32)[None, None, :] < lengths[:, :, None]
        key_index = jnp.where(valid & jnp.logical_not(replaced), doc_rows[None], FAR)[:, :, None, :]
        new_index = jnp.pad(positions, ((0, 0), (0, PADDED - TOKENS)), constant_values=FAR)
        row_pos = jnp.broadcast_to(
            positions.reshape(served, TILES, 1, SUB), (served, TILES, GROUP, SUB)
        ).reshape(served, TILES, ROWS, 1)

    with jax.named_scope("projections"):
        xf = sel_hidden.astype(jnp.float32)
        normed = (
            xf * lax.rsqrt(jnp.mean(xf * xf, axis=-1, keepdims=True) + 1e-05) * norm_gain
        ).astype(jnp.bfloat16)
        normed_rows = normed.reshape(served * TOKENS, normed.shape[2])

        def dot(w):
            out = jnp.dot(normed_rows, w, preferred_element_type=jnp.float32)
            return out.astype(jnp.bfloat16).reshape(served, TOKENS, w.shape[1])

        query, key_new, value_new = dot(w_query), dot(w_key), dot(w_value)
        pad = ((0, 0), (0, PADDED - TOKENS), (0, 0))
        key_new, value_new = jnp.pad(key_new, pad), jnp.pad(value_new, pad)

    with jax.named_scope("attention"):
        stages = [
            [(0, 0)] + NEAR + DIAGONAL,
            TWO + OPPOSITE + [KNIGHT[s] for s in NEAR],
        ]
        arrived[(0, 0)] = doc_cache
        outs = []
        for r in range(served):
            extra = [new_index[r : r + 1], key_new[r], value_new[r]]
            for n, shifts in enumerate(stages):
                extra = attend(
                    table(r, shifts),
                    query[r],
                    row_pos[r],
                    key_index[r],
                    extra,
                    [arrived[s] for s in shifts],
                    n == 0,
                    n == len(stages) - 1,
                )
            outs.append(extra)

    with jax.named_scope("output"):
        tp = lax.axis_index("tp")
        z, core = tp // 2, tp % 2
        planes = jnp.stack([z, (z + 3) % SIDE, (z + 1) % SIDE, (z + 2) % SIDE])
        place = jnp.concatenate([planes * 2 + core, planes * 2 + 1 - core]).astype(jnp.int32)
        mixed = [project(place, gather(o), w_out) for o in outs]
        return jnp.stack(mixed)


def solution(mesh):
    return jax.shard_map(
        body,
        mesh=mesh,
        in_specs=(
            P("grp", None, None),
            P(),
            P(None, "tp"),
            P(None, "tp"),
            P(None, "tp"),
            P(None, "tp"),
            P("grp", None, None, "tp"),
            P(),
            P(),
            P(),
            P("grp", None),
        ),
        out_specs=P("grp", None, "tp"),
        check_vma=False,
    )
```

time: 308 us -> 342 us (1.11)
  Pallas kernels: 0 us -> 160 us
  waiting for transfers between devices: 161 us -> 37.2 us
  starting transfers between devices: 7.72 us -> 110 us
  matrix products: 60.4 us -> 11.2 us
  other arithmetic: 38.5 us -> 11.9 us
  local copies, waits for them, and re-layouts: 25.8 us -> 10.5 us
  between operations: 13.7 us -> 0.69 us
    pallas_call x0 -> x7, Pallas kernels: none -> 160 us  [the longest x1 121 us: pack(): pl.pallas_call(pack_kernel, out_shape=[jax.ShapeDtypeStruct((CAP, 2, DOC,...]
    all_to_all x1 -> x0, waiting for transfers between devices: 118 us -> none  [body(): lax.all_to_all(outgoing, 'grp', split_axis=0, concat_axis=0, tiled=True)]
    ppermute x0 -> x35, starting transfers between devices: none -> 110 us  [the longest x19 87 us: shift(): return lax.ppermute(block, 'grp', pairs)]
    dot_general x8 -> x3, matrix products: 60.4 us -> 11.2 us  [dot(): out = jnp.dot(normed_rows, w, preferred_element_type=jnp.float32)]
    all_gather x1 -> x0, waiting for transfers between devices: 42.8 us -> none  [body(): lax.all_gather(outputs, 'tp', axis=1, tiled=True)]
    ppermute x0 -> x35, waiting for transfers between devices: none -> 37.2 us  [the longest x19 30.3 us: shift(): return lax.ppermute(block, 'grp', pairs)]
    reduce_sum x3 -> x0, other arithmetic: 24.3 us -> none  [the longest x1 21.2 us: body(): jnp.sum(expo_old, axis=-1, keepdims=True)]
    gather x5 -> x4, local copies, waits for them, and re-layouts: 16.5 us -> 2.78 us  [the longest x1 1.94 us: body(): location = home[doc_ids].reshape(GROUPS, per_group)]
  transfers between devices with their start and end apart: 2 -> 35, of which waited for: 2 -> 11; matrix products, arithmetic and copies ran while one was open for 8% -> 7% of each run, Pallas kernels for 0% -> 7%
where the time goes in v1:
time: 342 us; the launch traced here: 341 us
  Pallas kernels  160 us (47%)
  starting transfers between devices  110 us (32%)
  waiting for transfers between devices  37.2 us (11%)
  other arithmetic  11.9 us (3%)
  matrix products  11.2 us (3%)
  local copies, waits for them, and re-layouts  10.5 us (3%)
    pallas_call x1, Pallas kernels, pack(): pl.pallas_call(pack_kernel, out_shape=[jax.ShapeDtypeStruct((CAP, 2, DOC,...  121 us
    ppermute x19, starting transfers between devices, shift(): return lax.ppermute(block, 'grp', pairs)  87 us
    pallas_call x4, Pallas kernels, attend(): pl.pallas_call(functools.partial(attend_kernel, counts, first, last), out...  34.6 us
    ppermute x19, waiting for transfers between devices, shift(): return lax.ppermute(block, 'grp', pairs)  30.3 us
    ppermute x8, starting transfers between devices, other_core(): return lax.ppermute(block, 'tp', [(i, i ^ 1) for i in range(KVH)])  13.9 us
    dot_general x3, matrix products, dot(): out = jnp.dot(normed_rows, w, preferred_element_type=jnp.float32)  11.2 us
    ppermute x8, starting transfers between devices, ring(): lax.ppermute(block, 'tp', [(i, (i + 2 * by) % KVH) for i in range(KVH)])  9.13 us
  transfers between devices with their start and end apart: 35, of which 11 were waited for; matrix products, arithmetic and copies ran while one was open for 7% of the time, Pallas kernels for 7%

profile of v1, /device:TPU:1, one launch (start us, length us, event | category | flops | bytes accessed | tf_op | source)
XLA Modules:
  0.0 341.2 jit_solution(617138398917935730)
XLA Ops:
  5.1 120.9 %pack.1 = (bf16[2,2,512,128]{3,2,1,0:T(8,128)(2,1)}, bf16[2,2,512,128]{3,2,1,0:T(8,128)(2,1)}, bf16[2,2,512,128]{3,2,1,0:T(8,128)(2,1)}, bf16[2,2,512,128]{3,2,1...) custom-call(s32[1]{0:T(128)} %bitcast.35.me_ref, ...), custom_call_target="tpu_custom_call" | custom-call | bytes 10485760 | tf_op jit(solution)/shard_map/pack/pack/pallas_call | solution.py:69
  129.5 25.1 %collective-permute-start.2 = (bf16[2,2,512,128]{3,2,1,0:T(8,128)(2,1)}, bf16[2,2,512,128]{3,2,1,0:T(8,128)(2,1)}, u32[]{:S(2)}, u32[]{:S(2)}) collective-permute-start(bf16[2,2,512,128]{3,2,1,0:T(8,128)(2,1)} %get-tuple-element.35), channel_id=1, source_target_pairs={{0,8},{8,16},{16,24},{24,0},{32,40},{40,48},{48,56},{56,32},{64,72... | collective-permute-start | bytes 1572872 | tf_op jit(solution)/shard_map/documents/ppermute | solution.py:46
  154.7 24.7 %collective-permute-start.4 = (bf16[2,2,512,128]{3,2,1,0:T(8,128)(2,1)}, bf16[2,2,512,128]{3,2,1,0:T(8,128)(2,1)}, u32[]{:S(2)}, u32[]{:S(2)}) collective-permute-start(bf16[2,2,512,128]{3,2,1,0:T(8,128)(2,1)} %get-tuple-element.37), channel_id=1, source_target_pairs={{0,40},{8,48},{16,56},{24,32},{32,72},{40,80},{48,88},{56,64},{64,... | collective-permute-start | bytes 1572872 | tf_op jit(solution)/shard_map/documents/ppermute | solution.py:46
  180.5 3.6 %fusion = f32[2,320]{1,0:T(2,128)S(1)} fusion(bf16[2,320,4096]{2,1,0:T(8,128)(2,1)} %param.11), kind=kLoop, calls=%fused_computation.4 | loop fusion | flops 7863680 | bytes 5245440 | tf_op jit(solution)/shard_map/projections/reduce_sum | solution.py:336
  185.0 4.4 %fusion.2 = bf16[2,320,4096]{2,1,0:T(8,128)(2,1)S(1)} fusion(bf16[2,320,4096]{2,1,0:T(8,128)(2,1)} %param.11, f32[4096]{0:T(1024)S(1)} %copy-done.8, f32[2,320]{1,0:T(2,128)S(1)} %add_rsqrt_fusion), kind=kLoop, calls=%fused_computation.6 | loop fusion | flops 10485760 | bytes 10504704 | tf_op jit(solution)/shard_map/projections/convert_element_type | solution.py:337
  189.5 2.4 convolution_convert_fusion.2
  205.7 11.0 %collective-permute-done.5.refs_9_ = bf16[2,2,512,128]{3,2,1,0:T(8,128)(2,1)} collective-permute-done((bf16[2,2,512,128]{3,2,1,0:T(8,128)(2,1)}, bf16[2,2,512,128]{3,2,1,0:T(8,128)(2,1)}, u32[]{:S(2)}, u32[]{:S(2)}) %collective-permute-start.5) | collective-permute-done | bytes 524320 | tf_op jit(solution)/shard_map/documents/ppermute | solution.py:46
  220.4 6.6 %convolution_convert_fusion = bf16[640,512]{1,0:T(8,128)(2,1)S(1)} fusion(bf16[640,4096]{1,0:T(8,128)(2,1)} %bitcast.73, bf16[4096,512]{1,0:T(8,128)(2,1)} %param.13), kind=kOutput, calls=%fused_computation.7 | convolution fusion | flops 2684682240 | bytes 10092544 | tf_op jit(solution)/shard_map/projections/dot_general | solution.py:341
  228.8 2.9 collective-permute-done.9
  231.8 4.5 %collective-permute-done.11 = bf16[2,2,512,128]{3,2,1,0:T(8,128)(2,1)S(1)} collective-permute-done((bf16[2,2,512,128]{3,2,1,0:T(8,128)(2,1)}, bf16[2,2,512,128]{3,2,1,0:T(8,128)(2,1)S(1)}, u32[]{:S(2)}, u32[]{:S(2)}) %collective-permute-start.11) | collective-permute-done | bytes 524320 | tf_op jit(solution)/shard_map/documents/ppermute | solution.py:46
  237.0 4.7 %collective-permute-start.13 = (bf16[2,2,512,128]{3,2,1,0:T(8,128)(2,1)S(1)}, bf16[2,2,512,128]{3,2,1,0:T(8,128)(2,1)S(1)}, u32[]{:S(2)}, u32[]{:S(2)}) collective-permute-start(bf16[2,2,512,128]{3,2,1,0:T(8,128)(2,1)S(1)} %copy-done.11), channel_id=1, source_target_pairs={{0,16},{8,24},{16,0},{24,8},{32,48},{40,56},{48,32},{56,40},{64,80... | collective-permute-start | bytes 1572872 | tf_op jit(solution)/shard_map/documents/ppermute | solution.py:46
  241.8 2.7 collective-permute-start.14
  244.5 3.0 collective-permute-start.15
  251.3 9.6 %collective-permute-start.18 = (bf16[2,2,512,128]{3,2,1,0:T(8,128)(2,1)S(1)}, bf16[2,2,512,128]{3,2,1,0:T(8,128)(2,1)S(1)}, u32[]{:S(2)}, u32[]{:S(2)}) collective-permute-start(bf16[2,2,512,128]{3,2,1,0:T(8,128)(2,1)S(1)} %collective-permute-done.9), channel_id=1, source_target_pairs={{0,64},{8,72},{16,80},{24,88},{32,96},{40,104},{48,112},{56,120},{... | collective-permute-start | bytes 1572872 | tf_op jit(solution)/shard_map/documents/ppermute | solution.py:46
  260.9 5.9 %attend.6 = (f32[4,320,128]{2,1,0:T(8,128)S(1)}, f32[4,320,1]{2,1,0:T(8,128)S(1)}, f32[4,320,1]{2,1,0:T(8,128)S(1)}) custom-call(s32[36]{0:T(128)S(1)} %reshape.432.table_ref, bf16[320,512]{1,0:T(8,128)(2,1)S(1)} %get-tuple-element.76.q_ref, s32[4,320,1]{2,1,0:T(8,128)S(1)} %broadcast_in_dim.158.pos_ref, s32[8,1,512]{2,1,0:T(1,128)S(1)} %get-tuple-element.82.idx_ref, ...), custom_call_target="tpu_custom_call" | custom-call | flops 1509949440 | bytes 8650752 | tf_op jit(solution)/shard_map/attention/attend/pallas_call | solution.py:194
  266.9 9.0 %attend.4 = (f32[4,320,128]{2,1,0:T(8,128)S(1)}, f32[4,320,1]{2,1,0:T(8,128)S(1)}, f32[4,320,1]{2,1,0:T(8,128)S(1)}) custom-call(s32[36]{0:T(128)S(1)} %reshape.426.table_ref, bf16[320,512]{1,0:T(8,128)(2,1)S(1)} %get-tuple-element.75.q_ref, s32[4,320,1]{2,1,0:T(8,128)S(1)} %broadcast_in_dim.157.pos_ref, s32[8,1,512]{2,1,0:T(1,128)S(1)} %get-tuple-element.81.idx_ref, ...), custom_call_target="tpu_custom_call" | custom-call | flops 1509949440 | bytes 8650752 | tf_op jit(solution)/shard_map/attention/attend/pallas_call | solution.py:194
  275.9 8.0 %collective-permute-done.16.refs_7_ = bf16[2,2,512,128]{3,2,1,0:T(8,128)(2,1)S(1)} collective-permute-done((bf16[2,2,512,128]{3,2,1,0:T(8,128)(2,1)S(1)}, bf16[2,2,512,128]{3,2,1,0:T(8,128)(2,1)S(1)}, u32[]{:S(2)}, u32[]{:S(2)}) %collective-permute-start.16) | collective-permute-done | bytes 524320 | tf_op jit(solution)/shard_map/documents/ppermute | solution.py:46
  283.9 11.4 %attend.7.refs_0_ = bf16[320,512]{1,0:T(8,128)(2,1)S(1)} custom-call(s32[28]{0:T(128)S(1)} %reshape.431.table_ref, bf16[320,512]{1,0:T(8,128)(2,1)S(1)} %get-tuple-element.76.q_ref, s32[4,320,1]{2,1,0:T(8,128)S(1)} %broadcast_in_dim.158.pos_ref, s32[8,1,512]{2,1,0:T(1,128)S(1)} %get-tuple-element.82.idx_ref, f32[4,320,128]{2,1,0:T(8,128)S(1)} %get-tuple-element.58.refs_0_, ...), custom_call_target="tpu_custom_call" | custom-call | flops 1174405120 | bytes 8126464 | tf_op jit(solution)/shard_map/attention/attend/pallas_call | solution.py:194
  297.0 8.3 %attend.5.refs_0_ = bf16[320,512]{1,0:T(8,128)(2,1)S(1)} custom-call(s32[28]{0:T(128)S(1)} %reshape.423.table_ref, bf16[320,512]{1,0:T(8,128)(2,1)S(1)} %get-tuple-element.75.q_ref, s32[4,320,1]{2,1,0:T(8,128)S(1)} %broadcast_in_dim.157.pos_ref, s32[8,1,512]{2,1,0:T(1,128)S(1)} %get-tuple-element.81.idx_ref, f32[4,320,128]{2,1,0:T(8,128)S(1)} %get-tuple-element.41.refs_0_, ...), custom_call_target="tpu_custom_call" | custom-call | flops 1174405120 | bytes 8126464 | tf_op jit(solution)/shard_map/attention/attend/pallas_call | solution.py:194
  309.6 2.9 collective-permute-done.19.refs_1_
  313.3 8.0 %collective-permute-start.31 = (bf16[320,512]{1,0:T(8,128)(2,1)S(1)}, bf16[320,512]{1,0:T(8,128)(2,1)S(1)}, u32[]{:S(2)}, u32[]{:S(2)}) collective-permute-start(bf16[320,512]{1,0:T(8,128)(2,1)S(1)} %attend.7.refs_0_), channel_id=1, source_target_pairs={{0,1},{1,0},{2,3},{3,2},{4,5},{5,4},{6,7},{7,6},{8,9},{9,8},{10,11... | collective-permute-start | bytes 983048 | tf_op jit(solution)/shard_map/output/ppermute | solution.py:239
  321.4 2.3 collective-permute-start.30
  323.8 3.0 collective-permute-start.32
  328.5 2.3 collective-permute-done.22
  (164 shorter events, 53.3 us)
Async XLA Ops:
  126.1 68.0 %collective-permute-start = (bf16[2,2,512,128]{3,2,1,0:T(8,128)(2,1)}, bf16[2,2,512,128]{3,2,1,0:T(8,128)(2,1)S(1)}, u32[]{:S(2)}, u32[]{:S(2)}) collective-permute-start(bf16[2,2,512,128]{3,2,1,0:T(8,128)(2,1)} %get-tuple-element.33), channel_id=1, source_target_pairs={{0,32},{8,40},{16,48},{24,56},{32,64},{40,72},{48,80},{56,88},{64,... | collective-permute-start | bytes 1572872 | tf_op jit(solution)/shard_map/documents/ppermute | solution.py:46
  128.2 67.2 %collective-permute-start.1 = (bf16[2,2,512,128]{3,2,1,0:T(8,128)(2,1)}, bf16[2,2,512,128]{3,2,1,0:T(8,128)(2,1)S(1)}, u32[]{:S(2)}, u32[]{:S(2)}) collective-permute-start(bf16[2,2,512,128]{3,2,1,0:T(8,128)(2,1)} %get-tuple-element.34), channel_id=1, source_target_pairs={{0,96},{8,104},{16,112},{24,120},{32,0},{40,8},{48,16},{56,24},{64... | collective-permute-start | bytes 1572872 | tf_op jit(solution)/shard_map/documents/ppermute | solution.py:46
  129.5 71.5 %collective-permute-start.2 = (bf16[2,2,512,128]{3,2,1,0:T(8,128)(2,1)}, bf16[2,2,512,128]{3,2,1,0:T(8,128)(2,1)}, u32[]{:S(2)}, u32[]{:S(2)}) collective-permute-start(bf16[2,2,512,128]{3,2,1,0:T(8,128)(2,1)} %get-tuple-element.35), channel_id=1, source_target_pairs={{0,8},{8,16},{16,24},{24,0},{32,40},{40,48},{48,56},{56,32},{64,72... | collective-permute-start | bytes 1572872 | tf_op jit(solution)/shard_map/documents/ppermute | solution.py:46
  154.6 48.3 %collective-permute-start.3 = (bf16[2,2,512,128]{3,2,1,0:T(8,128)(2,1)}, bf16[2,2,512,128]{3,2,1,0:T(8,128)(2,1)}, u32[]{:S(2)}, u32[]{:S(2)}) collective-permute-start(bf16[2,2,512,128]{3,2,1,0:T(8,128)(2,1)} %get-tuple-element.36), channel_id=1, source_target_pairs={{0,24},{8,0},{16,8},{24,16},{32,56},{40,32},{48,40},{56,48},{64,88... | collective-permute-start | bytes 1572872 | tf_op jit(solution)/shard_map/documents/ppermute | solution.py:46
  154.7 49.4 %collective-permute-start.4 = (bf16[2,2,512,128]{3,2,1,0:T(8,128)(2,1)}, bf16[2,2,512,128]{3,2,1,0:T(8,128)(2,1)}, u32[]{:S(2)}, u32[]{:S(2)}) collective-permute-start(bf16[2,2,512,128]{3,2,1,0:T(8,128)(2,1)} %get-tuple-element.37), channel_id=1, source_target_pairs={{0,40},{8,48},{16,56},{24,32},{32,72},{40,80},{48,88},{56,64},{64,... | collective-permute-start | bytes 1572872 | tf_op jit(solution)/shard_map/documents/ppermute | solution.py:46
  194.1 22.7 %collective-permute-start.5 = (bf16[2,2,512,128]{3,2,1,0:T(8,128)(2,1)}, bf16[2,2,512,128]{3,2,1,0:T(8,128)(2,1)}, u32[]{:S(2)}, u32[]{:S(2)}) collective-permute-start(bf16[2,2,512,128]{3,2,1,0:T(8,128)(2,1)} %get-tuple-element.38), channel_id=1, source_target_pairs={{0,120},{8,96},{16,104},{24,112},{32,24},{40,0},{48,8},{56,16},{64... | collective-permute-start | bytes 1572872 | tf_op jit(solution)/shard_map/documents/ppermute | solution.py:46
  195.4 22.8 %collective-permute-start.6 = (bf16[2,2,512,128]{3,2,1,0:T(8,128)(2,1)}, bf16[2,2,512,128]{3,2,1,0:T(8,128)(2,1)}, u32[]{:S(2)}, u32[]{:S(2)}) collective-permute-start(bf16[2,2,512,128]{3,2,1,0:T(8,128)(2,1)} %get-tuple-element.39), channel_id=1, source_target_pairs={{0,56},{8,32},{16,40},{24,48},{32,88},{40,64},{48,72},{56,80},{64,... | collective-permute-start | bytes 1572872 | tf_op jit(solution)/shard_map/documents/ppermute | solution.py:46
  201.0 27.8 %collective-permute-start.7 = (bf16[2,2,512,128]{3,2,1,0:T(8,128)(2,1)}, bf16[2,2,512,128]{3,2,1,0:T(8,128)(2,1)S(1)}, u32[]{:S(2)}, u32[]{:S(2)}) collective-permute-start(bf16[2,2,512,128]{3,2,1,0:T(8,128)(2,1)} %get-tuple-element.40), channel_id=1, source_target_pairs={{0,104},{8,112},{16,120},{24,96},{32,8},{40,16},{48,24},{56,0},{64... | collective-permute-start | bytes 1572872 | tf_op jit(solution)/shard_map/documents/ppermute | solution.py:46
  203.0 25.8 %collective-permute-start.8 = (bf16[2,2,512,128]{3,2,1,0:T(8,128)(2,1)}, bf16[2,2,512,128]{3,2,1,0:T(8,128)(2,1)S(1)}, u32[]{:S(2)}, u32[]{:S(2)}) collective-permute-start(bf16[2,2,512,128]{3,2,1,0:T(8,128)(2,1)} %get-tuple-element.44), channel_id=1, source_target_pairs={{0,8},{8,16},{16,24},{24,0},{32,40},{40,48},{48,56},{56,32},{64,72... | collective-permute-start | bytes 1572872 | tf_op jit(solution)/shard_map/documents/ppermute | solution.py:46
  204.1 27.7 %collective-permute-start.9 = (bf16[2,2,512,128]{3,2,1,0:T(8,128)(2,1)}, bf16[2,2,512,128]{3,2,1,0:T(8,128)(2,1)S(1)}, u32[]{:S(2)}, u32[]{:S(2)}) collective-permute-start(bf16[2,2,512,128]{3,2,1,0:T(8,128)(2,1)} %get-tuple-element.45), channel_id=1, source_target_pairs={{0,24},{8,0},{16,8},{24,16},{32,56},{40,32},{48,40},{56,48},{64,88... | collective-permute-start | bytes 1572872 | tf_op jit(solution)/shard_map/documents/ppermute | solution.py:46
  216.7 15.1 %collective-permute-start.10 = (bf16[2,2,512,128]{3,2,1,0:T(8,128)(2,1)}, bf16[2,2,512,128]{3,2,1,0:T(8,128)(2,1)S(1)}, u32[]{:S(2)}, u32[]{:S(2)}) collective-permute-start(bf16[2,2,512,128]{3,2,1,0:T(8,128)(2,1)} %get-tuple-element.46), channel_id=1, source_target_pairs={{0,32},{8,40},{16,48},{24,56},{32,64},{40,72},{48,80},{56,88},{64,... | collective-permute-start | bytes 1572872 | tf_op jit(solution)/shard_map/documents/ppermute | solution.py:46
  218.2 18.1 %collective-permute-start.11 = (bf16[2,2,512,128]{3,2,1,0:T(8,128)(2,1)}, bf16[2,2,512,128]{3,2,1,0:T(8,128)(2,1)S(1)}, u32[]{:S(2)}, u32[]{:S(2)}) collective-permute-start(bf16[2,2,512,128]{3,2,1,0:T(8,128)(2,1)} %get-tuple-element.47), channel_id=1, source_target_pairs={{0,96},{8,104},{16,112},{24,120},{32,0},{40,8},{48,16},{56,24},{64... | collective-permute-start | bytes 1572872 | tf_op jit(solution)/shard_map/documents/ppermute | solution.py:46
  237.0 14.3 %collective-permute-start.13 = (bf16[2,2,512,128]{3,2,1,0:T(8,128)(2,1)S(1)}, bf16[2,2,512,128]{3,2,1,0:T(8,128)(2,1)S(1)}, u32[]{:S(2)}, u32[]{:S(2)}) collective-permute-start(bf16[2,2,512,128]{3,2,1,0:T(8,128)(2,1)S(1)} %copy-done.11), channel_id=1, source_target_pairs={{0,16},{8,24},{16,0},{24,8},{32,48},{40,56},{48,32},{56,40},{64,80... | collective-permute-start | bytes 1572872 | tf_op jit(solution)/shard_map/documents/ppermute | solution.py:46
  241.8 34.1 %collective-permute-start.14 = (bf16[2,2,512,128]{3,2,1,0:T(8,128)(2,1)S(1)}, bf16[2,2,512,128]{3,2,1,0:T(8,128)(2,1)S(1)}, u32[]{:S(2)}, u32[]{:S(2)}) collective-permute-start(bf16[2,2,512,128]{3,2,1,0:T(8,128)(2,1)S(1)} %copy-done.10), channel_id=1, source_target_pairs={{0,80},{8,88},{16,64},{24,72},{32,112},{40,120},{48,96},{56,104},{... | collective-permute-start | bytes 1572872 | tf_op jit(solution)/shard_map/documents/ppermute | solution.py:46
  244.5 31.4 %collective-permute-start.15 = (bf16[2,2,512,128]{3,2,1,0:T(8,128)(2,1)S(1)}, bf16[2,2,512,128]{3,2,1,0:T(8,128)(2,1)S(1)}, u32[]{:S(2)}, u32[]{:S(2)}) collective-permute-start(bf16[2,2,512,128]{3,2,1,0:T(8,128)(2,1)S(1)} %collective-permute-done.10), channel_id=1, source_target_pairs={{0,16},{8,24},{16,0},{24,8},{32,48},{40,56},{48,32},{56,40},{64,80... | collective-permute-start | bytes 1572872 | tf_op jit(solution)/shard_map/documents/ppermute | solution.py:46
  247.5 36.4 %collective-permute-start.16 = (bf16[2,2,512,128]{3,2,1,0:T(8,128)(2,1)S(1)}, bf16[2,2,512,128]{3,2,1,0:T(8,128)(2,1)S(1)}, u32[]{:S(2)}, u32[]{:S(2)}) collective-permute-start(bf16[2,2,512,128]{3,2,1,0:T(8,128)(2,1)S(1)} %collective-permute-done.11), channel_id=1, source_target_pairs={{0,16},{8,24},{16,0},{24,8},{32,48},{40,56},{48,32},{56,40},{64,80... | collective-permute-start | bytes 1572872 | tf_op jit(solution)/shard_map/documents/ppermute | solution.py:46
  247.6 36.3 %collective-permute-start.17 = (bf16[2,2,512,128]{3,2,1,0:T(8,128)(2,1)S(1)}, bf16[2,2,512,128]{3,2,1,0:T(8,128)(2,1)S(1)}, u32[]{:S(2)}, u32[]{:S(2)}) collective-permute-start(bf16[2,2,512,128]{3,2,1,0:T(8,128)(2,1)S(1)} %collective-permute-done.8), channel_id=1, source_target_pairs={{0,64},{8,72},{16,80},{24,88},{32,96},{40,104},{48,112},{56,120},{... | collective-permute-start | bytes 1572872 | tf_op jit(solution)/shard_map/documents/ppermute | solution.py:46
  251.3 32.6 %collective-permute-start.18 = (bf16[2,2,512,128]{3,2,1,0:T(8,128)(2,1)S(1)}, bf16[2,2,512,128]{3,2,1,0:T(8,128)(2,1)S(1)}, u32[]{:S(2)}, u32[]{:S(2)}) collective-permute-start(bf16[2,2,512,128]{3,2,1,0:T(8,128)(2,1)S(1)} %collective-permute-done.9), channel_id=1, source_target_pairs={{0,64},{8,72},{16,80},{24,88},{32,96},{40,104},{48,112},{56,120},{... | collective-permute-start | bytes 1572872 | tf_op jit(solution)/shard_map/documents/ppermute | solution.py:46
  295.3 13.8 %collective-permute-start.27 = (bf16[320,512]{1,0:T(8,128)(2,1)S(1)}, bf16[320,512]{1,0:T(8,128)(2,1)S(1)}, u32[]{:S(2)}, u32[]{:S(2)}) collective-permute-start(bf16[320,512]{1,0:T(8,128)(2,1)S(1)} %attend.7.refs_0_), channel_id=1, source_target_pairs={{0,2},{1,3},{2,4},{3,5},{4,6},{5,7},{6,0},{7,1},{8,10},{9,11},{10,... | collective-permute-start | bytes 983048 | tf_op jit(solution)/shard_map/output/ppermute | solution.py:235
  307.0 14.3 %collective-permute-start.28 = (bf16[320,512]{1,0:T(8,128)(2,1)S(1)}, bf16[320,512]{1,0:T(8,128)(2,1)S(1)}, u32[]{:S(2)}, u32[]{:S(2)}) collective-permute-start(bf16[320,512]{1,0:T(8,128)(2,1)S(1)} %attend.7.refs_0_), channel_id=1, source_target_pairs={{0,6},{1,7},{2,0},{3,1},{4,2},{5,3},{6,4},{7,5},{8,14},{9,15},{10,... | collective-permute-start | bytes 983048 | tf_op jit(solution)/shard_map/output/ppermute | solution.py:235
  308.1 15.6 %collective-permute-start.20 = (bf16[320,512]{1,0:T(8,128)(2,1)S(1)}, bf16[320,512]{1,0:T(8,128)(2,1)S(1)}, u32[]{:S(2)}, u32[]{:S(2)}) collective-permute-start(bf16[320,512]{1,0:T(8,128)(2,1)S(1)} %attend.5.refs_0_), channel_id=1, source_target_pairs={{0,6},{1,7},{2,0},{3,1},{4,2},{5,3},{6,4},{7,5},{8,14},{9,15},{10,... | collective-permute-start | bytes 983048 | tf_op jit(solution)/shard_map/output/ppermute | solution.py:235
  309.1 14.7 %collective-permute-start.29 = (bf16[160,512]{1,0:T(8,128)(2,1)S(1)}, bf16[160,512]{1,0:T(8,128)(2,1)S(1)}, u32[]{:S(2)}, u32[]{:S(2)}) collective-permute-start(bf16[160,512]{1,0:T(8,128)(2,1)S(1)} %slice.138), channel_id=1, source_target_pairs={{0,2},{1,3},{2,4},{3,5},{4,6},{5,7},{6,0},{7,1},{8,10},{9,11},{10,... | collective-permute-start | bytes 491528 | tf_op jit(solution)/shard_map/output/ppermute | solution.py:235
  312.5 14.3 %collective-permute-start.21 = (bf16[160,512]{1,0:T(8,128)(2,1)S(1)}, bf16[160,512]{1,0:T(8,128)(2,1)S(1)}, u32[]{:S(2)}, u32[]{:S(2)}) collective-permute-start(bf16[160,512]{1,0:T(8,128)(2,1)S(1)} %slice.134), channel_id=1, source_target_pairs={{0,2},{1,3},{2,4},{3,5},{4,6},{5,7},{6,0},{7,1},{8,10},{9,11},{10,... | collective-permute-start | bytes 491528 | tf_op jit(solution)/shard_map/output/ppermute | solution.py:235
  313.3 18.3 %collective-permute-start.31 = (bf16[320,512]{1,0:T(8,128)(2,1)S(1)}, bf16[320,512]{1,0:T(8,128)(2,1)S(1)}, u32[]{:S(2)}, u32[]{:S(2)}) collective-permute-start(bf16[320,512]{1,0:T(8,128)(2,1)S(1)} %attend.7.refs_0_), channel_id=1, source_target_pairs={{0,1},{1,0},{2,3},{3,2},{4,5},{5,4},{6,7},{7,6},{8,9},{9,8},{10,11... | collective-permute-start | bytes 983048 | tf_op jit(solution)/shard_map/output/ppermute | solution.py:239
  (24 other events, 750.8 us)

commit v2 on v0

v2 whole, which is shorter than its diff:
```python
import functools
import math

import jax
import jax.numpy as jnp
from jax import lax
from jax.experimental import pallas as pl
from jax.experimental.pallas import tpu as pltpu
from jax.sharding import PartitionSpec as P

H = 32
KVH = 8
HD = 128
CAP = 2
GROUP = H // KVH
SIDE = 4
GROUPS = 16
STORED = 16
SLOTS = 16
PICK = 40
DOC = 512
TOKENS = 320
RETRIEVED = 8
TILES = 2
SUB = TOKENS // TILES
ROWS = SUB * GROUP
PADDED = 384
FAR = 2**30
EXP2 = HD ** (-0.5) * math.log2(math.e)

NEAR = [(1, 0), (3, 0), (0, 1), (0, 3)]
DIAGONAL = [(1, 1), (3, 3), (1, 3), (3, 1)]
OPPOSITE = [(2, 2)]
KNIGHT = [(1, 2), (3, 2), (2, 1), (2, 3)]
TWO = [(2, 0), (0, 2)]
CARRIED = {(2, 0): [(2, 0), (2, 1), (2, 3)], (0, 2): [(0, 2), (1, 2), (3, 2)]}
BLOCKS = [CARRIED[s] for s in TWO] + [[s] for s in DIAGONAL + NEAR + OPPOSITE]
STAGES = [[(0, 0)], TWO, DIAGONAL, NEAR, KNIGHT + OPPOSITE]
ROOM = 24 << 20

ANY = pl.BlockSpec(memory_space=pl.ANY)
HBM = pl.BlockSpec(memory_space=pltpu.HBM)
VMEM = pl.BlockSpec(memory_space=pltpu.VMEM)
SMEM = pl.BlockSpec(memory_space=pltpu.SMEM)


def shift(block, by):
    pairs = [
        (x * SIDE + y, (x + by[0]) % SIDE * SIDE + (y + by[1]) % SIDE)
        for x in range(SIDE)
        for y in range(SIDE)
    ]
    return lax.ppermute(block, "grp", pairs)


def pack_kernel(me_ref, home_ref, ids_ref, len_ref, cache_ref, *refs):
    out_refs, refs = refs[: len(BLOCKS)], refs[len(BLOCKS) :]
    table_ref, chosen, sem = refs
    me = me_ref[0]
    x, y = me // SIDE, me % SIDE

    def locate(g, i):
        return home_ref[ids_ref[g * 2 + i // RETRIEVED, i % RETRIEVED]]

    def outgoing(g, carry):
        one, two = jnp.int32(-1), jnp.int32(-1)
        for i in range(SLOTS):
            slot = locate(g, i) - me * STORED
            hit = (slot >= 0) & (slot < STORED)
            two = jnp.where(hit, one, two)
            one = jnp.where(hit, slot, one)
        chosen[g * CAP] = jnp.where(two >= 0, two, one)
        chosen[g * CAP + 1] = jnp.where(two >= 0, one, -1)
        return carry

    lax.fori_loop(0, GROUPS, outgoing, 0)

    def each(act):
        at = 0
        for block, out in zip(BLOCKS, out_refs):
            for n, (dx, dy) in enumerate(block):
                g = (x + dx) % SIDE * SIDE + (y + dy) % SIDE
                for k in range(CAP):
                    doc = chosen[g * CAP + k]

                    @pl.when(doc >= 0)
                    def _(at=at, doc=doc, out=out.at[n * CAP + k]):
                        act(at, doc, out)

                    at += 1

    def read(at, doc, out):
        return pltpu.make_async_copy(cache_ref.at[doc], out, sem.at[at])

    each(lambda at, doc, out: read(at, doc, out).start())

    for at in range(GROUPS * CAP):
        table_ref[at] = jnp.int32(-1)
    for i in range(SLOTS):
        doc = ids_ref[me * 2 + i // RETRIEVED, i % RETRIEVED]
        location = home_ref[doc]
        at = location // STORED * CAP
        table_ref[at + jnp.where(table_ref[at] >= 0, 1, 0)] = jnp.int32(i)
        table_ref[GROUPS * CAP + i] = location % STORED
        table_ref[GROUPS * CAP + SLOTS + i] = len_ref[doc]

    each(lambda at, doc, out: read(at, doc, out).wait())


def pack(me, home, ids, lengths, cache):
    shapes = [(CAP * len(b), 2, DOC, HD) for b in BLOCKS]
    total = sum(s[0] for s in shapes)
    *packed, table = pl.pallas_call(
        pack_kernel,
        out_shape=[jax.ShapeDtypeStruct(s, jnp.bfloat16) for s in shapes]
        + [jax.ShapeDtypeStruct((GROUPS * CAP + 2 * SLOTS,), jnp.int32)],
        in_specs=[SMEM] * 4 + [HBM],
        out_specs=[VMEM] * len(BLOCKS) + [SMEM],
        scratch_shapes=[
            pltpu.SMEM((GROUPS * CAP,), jnp.int32),
            pltpu.SemaphoreType.DMA((total,)),
        ],
        compiler_params=pltpu.CompilerParams(vmem_limit_bytes=ROOM),
        cost_estimate=pl.CostEstimate(flops=0, bytes_accessed=10 << 20, transcendentals=0),
        name="pack",
    )(me, home, ids, lengths, cache)
    return packed, table


def attend_kernel(shifts, base, count, first, last, *refs):
    refs = list(refs)
    me_ref, table_ref, q_ref, pos_ref = refs[:4]
    if first:
        new_idx_ref, new_k_ref, new_v_ref = refs[4:7]
    arrays, refs = refs[7 : 7 + len(shifts)], refs[7 + len(shifts) :]
    acc, top_ref, sum_ref, *refs = refs
    if last:
        out_ref, *refs = refs
    buf, items, sem = refs
    me = me_ref[0]
    x, y = me // SIDE, me % SIDE

    found = jnp.int32(0)
    for (dx, dy), array in zip(shifts, arrays):
        source = (x - dx + SIDE) % SIDE * SIDE + (y - dy + SIDE) % SIDE
        for k in range(CAP):
            i = table_ref[source * CAP + k]
            mine = (i >= base * RETRIEVED) & (i < (base + count) * RETRIEVED)

            @pl.when(mine)
            def _(i=i, array=array, k=k, at=found, own=(dx, dy) == (0, 0)):
                where = table_ref[GROUPS * CAP + i] if own else k
                items[at] = i
                pltpu.make_async_copy(array.at[where], buf.at[at], sem.at[at]).start()

            found = found + jnp.where(mine, 1, 0)

    def scores(r, tile, keys, idx):
        rows = pl.ds(pl.multiple_of(tile * SUB, SUB), SUB)
        q = jnp.concatenate(
            [q_ref[r, rows, h * HD : (h + 1) * HD] for h in range(GROUP)], axis=0
        )
        s = lax.dot_general(
            q, keys, (((1,), (1,)), ((), ())), preferred_element_type=jnp.float32
        )
        return jnp.where(idx <= pos_ref[r, tile], s, -1e30)

    def weigh(s, top):
        p = jnp.exp2((s - jnp.concatenate([top] * (s.shape[1] // HD), axis=1)) * EXP2)
        parts = [p[:, c : c + HD] for c in range(0, s.shape[1], HD)]
        return p.astype(jnp.bfloat16), functools.reduce(jnp.add, parts)

    if first:

        def start(at, carry):
            r, tile = at // TILES, at % TILES
            s = scores(r, tile, new_k_ref[r], new_idx_ref[r])
            top = jnp.broadcast_to(jnp.max(s, axis=1, keepdims=True), (ROWS, HD))
            p, sums = weigh(s, top)
            top_ref[r, tile] = top
            sum_ref[r, tile] = sums
            acc[r, tile] = jnp.dot(p, new_v_ref[r], preferred_element_type=jnp.float32)
            return carry

        lax.fori_loop(0, count * TILES, start, 0)

    def item(at, carry):
        i = items[at]
        r, j = i // RETRIEVED, i % RETRIEVED
        length = table_ref[GROUPS * CAP + SLOTS + i]
        row = lax.broadcasted_iota(jnp.int32, (1, DOC), 1)
        idx = row + j * DOC
        per = RETRIEVED // TILES
        picked = pos_ref[r, j // per, pl.ds(pl.multiple_of(j % per * PICK, PICK), PICK)]
        replaced = jnp.max(jnp.where(picked == idx, 1, 0), axis=0, keepdims=True)
        idx = jnp.where((row < length) & (replaced == 0), idx, FAR)
        pltpu.make_async_copy(arrays[0].at[0], buf.at[at], sem.at[at]).wait()

        def step(tile, carry):
            s = scores(r, tile, buf[at, 0], idx)
            before = top_ref[r, tile]
            top = jnp.maximum(before, jnp.max(s, axis=1, keepdims=True))
            fade = jnp.exp2((before - top) * EXP2)
            p, sums = weigh(s, top)
            top_ref[r, tile] = top
            sum_ref[r, tile] = sum_ref[r, tile] * fade + sums
            acc[r, tile] = acc[r, tile] * fade + jnp.dot(
                p, buf[at, 1], preferred_element_type=jnp.float32
            )
            return carry

        lax.fori_loop(j // per, TILES, step, 0)
        return carry

    lax.fori_loop(0, found, item, 0)

    if last:
        for tile in range(TILES):
            sums = jnp.sum(sum_ref[base, tile], axis=1, keepdims=True)
            done = (acc[base, tile] / sums).astype(jnp.bfloat16)
            for h in range(GROUP):
                out_ref[tile * SUB : (tile + 1) * SUB, h * HD : (h + 1) * HD] = done[
                    h * SUB : (h + 1) * SUB
                ]


def attend(me, table, query, pos, extra, arrays, shifts, base, count, first, last):
    cands = CAP * len(arrays)

    state = jax.ShapeDtypeStruct((query.shape[0], TILES, ROWS, HD), jnp.float32)
    out_shape = [state] * 3
    if last:
        out_shape.append(jax.ShapeDtypeStruct((TOKENS, GROUP * HD), jnp.bfloat16))
    return pl.pallas_call(
        functools.partial(attend_kernel, shifts, base, count, first, last),
        out_shape=out_shape,
        in_specs=[SMEM, SMEM] + [VMEM] * 5 + [ANY] * len(arrays),
        out_specs=[VMEM] * len(out_shape),
        scratch_shapes=[
            pltpu.VMEM((cands, 2, DOC, HD), jnp.bfloat16),
            pltpu.SMEM((cands,), jnp.int32),
            pltpu.SemaphoreType.DMA((cands,)),
        ],
        input_output_aliases={} if first else {4: 0, 5: 1, 6: 2},
        compiler_params=pltpu.CompilerParams(vmem_limit_bytes=ROOM),
        cost_estimate=pl.CostEstimate(
            flops=count * 2 * 1280 * 512 * 128 * len(arrays),
            bytes_accessed=count * ((4 << 20) + len(arrays) * (1 << 17)),
            transcendentals=count * 1280 * 512 * len(arrays) // 2,
        ),
        name="attend",
    )(me, table, query, pos, *extra, *arrays)


def project_kernel(spans, r, place_ref, w_ref, *refs):
    parts, (out_ref, done, sem) = refs[: len(spans)], refs[-3:]
    width, half = GROUP * HD, TOKENS // 2
    total = {}
    for part, (n, lo, hi) in zip(parts, spans):
        rows = pl.ds(pl.multiple_of(place_ref[n] * width, width), width)
        term = jnp.dot(part[...], w_ref[rows, :], preferred_element_type=jnp.float32)
        for at in range(lo, hi, half):
            piece = term[at - lo : at - lo + half]
            total[at] = total[at] + piece if at in total else piece
    for at, value in total.items():
        done[at : at + half] = value.astype(jnp.bfloat16)
    copy = pltpu.make_async_copy(done, out_ref.at[r], sem)
    copy.start()
    copy.wait()


def project(place, r, served, pieces, w_out, before):
    parts = [p for _, _, _, p in pieces]
    spans = [(n, lo, hi) for n, lo, hi, _ in pieces]
    more = [] if before is None else [before]
    return pl.pallas_call(
        functools.partial(project_kernel, spans, r),
        out_shape=jax.ShapeDtypeStruct((served, TOKENS, w_out.shape[1]), jnp.bfloat16),
        in_specs=[SMEM] + [VMEM] * (len(parts) + 1) + [HBM] * len(more),
        out_specs=HBM,
        scratch_shapes=[
            pltpu.VMEM((TOKENS, w_out.shape[1]), jnp.bfloat16),
            pltpu.SemaphoreType.DMA,
        ],
        input_output_aliases={len(parts) + 2: 0} if more else {},
        compiler_params=pltpu.CompilerParams(vmem_limit_bytes=ROOM),
        cost_estimate=pl.CostEstimate(
            flops=2 * TOKENS * 4096 * 512, bytes_accessed=7 << 20, transcendentals=0
        ),
        name="project",
    )(place, w_out, *parts, *more)


def ring(block, by):
    return lax.ppermute(block, "tp", [(i, (i + 2 * by) % KVH) for i in range(KVH)])


def other_core(block):
    return lax.ppermute(block, "tp", [(i, i ^ 1) for i in range(KVH)])


def gather(own):
    half = TOKENS // 2
    up, down = ring(own, 1), ring(own, -1)
    far_up, far_down = ring(up[:half], 1), ring(down[half:], -1)
    same = [(0, 0, TOKENS, own), (1, 0, TOKENS, up), (2, 0, TOKENS, down)]
    same += [(3, 0, half, far_up), (3, half, TOKENS, far_down)]
    return same + [(n + SIDE, lo, hi, other_core(p)) for n, lo, hi, p in same]


def body(
    sel_hidden,
    norm_gain,
    w_query,
    w_key,
    w_value,
    w_out,
    doc_cache,
    home,
    doc_ids,
    doc_len,
    positions,
):
    me = lax.axis_index("grp").astype(jnp.int32).reshape(1)
    served = sel_hidden.shape[0]

    with jax.named_scope("pack"):
        packed, table = pack(me, home, doc_ids, doc_len, doc_cache)
        packed = dict(zip([b[0] for b in BLOCKS], packed))

    with jax.named_scope("positions"):
        new_index = jnp.pad(
            positions, ((0, 0), (0, PADDED - TOKENS)), constant_values=FAR
        ).reshape(served, 1, PADDED)
        row_pos = jnp.broadcast_to(
            positions.reshape(served, TILES, 1, SUB), (served, TILES, GROUP, SUB)
        ).reshape(served, TILES, ROWS, 1)

    with jax.named_scope("projections"):
        xf = sel_hidden.astype(jnp.float32)
        normed = (
            xf * lax.rsqrt(jnp.mean(xf * xf, axis=-1, keepdims=True) + 1e-05) * norm_gain
        ).astype(jnp.bfloat16)
        normed_rows = normed.reshape(served * TOKENS, normed.shape[2])

        def dot(w):
            out = jnp.dot(normed_rows, w, preferred_element_type=jnp.float32)
            return out.astype(jnp.bfloat16).reshape(served, TOKENS, w.shape[1])

        query, key_new, value_new = dot(w_query), dot(w_key), dot(w_value)
        pad = ((0, 0), (0, PADDED - TOKENS), (0, 0))
        key_new, value_new = jnp.pad(key_new, pad), jnp.pad(value_new, pad)

    arrived = {(0, 0): doc_cache}

    def after(blocks, *done):
        return lax.optimization_barrier((blocks, done))[0]

    def send(names, blocks, hops):
        with jax.named_scope("documents"):
            for s, block, hop in zip(names, blocks, hops):
                arrived[s] = shift(block, hop)

    def attention(n, state, base, count):
        shifts, last = STAGES[n], n == len(STAGES) - 1
        with jax.named_scope("attention"):
            return attend(
                me,
                table,
                query,
                row_pos,
                state,
                [arrived[s] for s in shifts],
                shifts,
                base,
                count,
                n == 0,
                last,
            )

    send(TWO, [packed[s] for s in TWO], TWO)
    send(DIAGONAL, [packed[s] for s in DIAGONAL], DIAGONAL)
    state = attention(0, [new_index, key_new, value_new], 0, served)
    blocks = after([packed[s] for s in NEAR], [arrived[s] for s in TWO], state)
    send(NEAR, blocks, NEAR)
    state = attention(1, state, 0, served)
    blocks = []
    for s in KNIGHT:
        through = (0, 2) if s[1] == 2 else (2, 0)
        at = CAP * CARRIED[through].index(s)
        blocks.append(arrived[through][at : at + CAP])
    blocks = after(blocks, [arrived[s] for s in DIAGONAL], state)
    send(KNIGHT, blocks, NEAR)
    state = attention(2, state, 0, served)
    blocks = after([packed[s] for s in OPPOSITE], [arrived[s] for s in NEAR], state)
    send(OPPOSITE, blocks, OPPOSITE)
    state = attention(3, state, 0, served)
    outs = []
    for r in range(served):
        *state, out = attention(4, state, r, 1)
        outs.append(out)

    with jax.named_scope("output"):
        tp = lax.axis_index("tp")
        z, core = tp // 2, tp % 2
        planes = jnp.stack([z, (z + 3) % SIDE, (z + 1) % SIDE, (z + 2) % SIDE])
        place = jnp.concatenate([planes * 2 + core, planes * 2 + 1 - core]).astype(jnp.int32)
        gathered = [gather(o) for o in outs]
        mixed = None
        for r in range(served):
            mixed = project(place, r, served, gathered[r], w_out, mixed)
        return mixed


def solution(mesh):
    return jax.shard_map(
        body,
        mesh=mesh,
        in_specs=(
            P("grp", None, None),
            P(),
            P(None, "tp"),
            P(None, "tp"),
            P(None, "tp"),
            P(None, "tp"),
            P("grp", None, None, "tp"),
            P(),
            P(),
            P(),
            P("grp", None),
        ),
        out_specs=P("grp", None, "tp"),
        check_vma=False,
    )
```

time: 308 us -> 171 us (0.56)
  waiting for transfers between devices: 161 us -> 36.8 us
  matrix products: 60.4 us -> 5.9 us
  starting transfers between devices: 7.72 us -> 54.3 us
  Pallas kernels: 0 us -> 44.9 us
  other arithmetic: 38.5 us -> 8.15 us
  between operations: 13.7 us -> 0.61 us
  local copies, waits for them, and re-layouts: 25.8 us -> 18.8 us
    all_to_all x1 -> x0, waiting for transfers between devices: 118 us -> none  [body(): lax.all_to_all(outgoing, 'grp', split_axis=0, concat_axis=0, tiled=True)]
    dot_general x8 -> x3, matrix products: 60.4 us -> 5.9 us  [dot(): out = jnp.dot(normed_rows, w, preferred_element_type=jnp.float32)]
    ppermute x0 -> x33, starting transfers between devices: none -> 54.3 us  [the longest x15 30.6 us: shift(): return lax.ppermute(block, 'grp', pairs)]
    pallas_call x0 -> x9, Pallas kernels: none -> 44.9 us  [the longest x6 33.4 us: attend(): pl.pallas_call(functools.partial(attend_kernel, shifts, base, count, firs...]
    all_gather x1 -> x0, waiting for transfers between devices: 42.8 us -> none  [body(): lax.all_gather(outputs, 'tp', axis=1, tiled=True)]
    ppermute x0 -> x33, waiting for transfers between devices: none -> 36.8 us  [the longest x15 36 us: shift(): return lax.ppermute(block, 'grp', pairs)]
    reduce_sum x4 -> x0, other arithmetic: 24.8 us -> none  [the longest x1 21.2 us: body(): jnp.sum(expo_old, axis=-1, keepdims=True)]
    gather x5 -> x0, local copies, waits for them, and re-layouts: 16.5 us -> none  [the longest x1 7.14 us: body(): outgoing = doc_cache[chosen]]
  transfers between devices with their start and end apart: 2 -> 33, of which waited for: 2 -> 8; matrix products, arithmetic and copies ran while one was open for 8% -> 11% of each run, Pallas kernels for 0% -> 17%
where the time goes in v2:
time: 171 us; the launch traced here: 170 us
  starting transfers between devices  54.3 us (32%)
  Pallas kernels  44.9 us (26%)
  waiting for transfers between devices  36.8 us (22%)
  local copies, waits for them, and re-layouts  18.8 us (11%)
  other arithmetic  8.15 us (5%)
  matrix products  5.9 us (3%)
    ppermute x15, waiting for transfers between devices, shift(): return lax.ppermute(block, 'grp', pairs)  36 us
    pallas_call x6, Pallas kernels, attend(): pl.pallas_call(functools.partial(attend_kernel, shifts, base, count, firs...  33.4 us
    ppermute x15, starting transfers between devices, shift(): return lax.ppermute(block, 'grp', pairs)  30.6 us
    unnamed x53, local copies, waits for them, and re-layouts  13.6 us
    ppermute x8, starting transfers between devices, ring(): lax.ppermute(block, 'tp', [(i, (i + 2 * by) % KVH) for i in range(KVH)])  12.3 us
    ppermute x10, starting transfers between devices, other_core(): return lax.ppermute(block, 'tp', [(i, i ^ 1) for i in range(KVH)])  11.3 us
    pallas_call x2, Pallas kernels, project(): pl.pallas_call(functools.partial(project_kernel, spans, r), out_shape=jax...  6.54 us
    dot_general x3, matrix products, dot(): out = jnp.dot(normed_rows, w, preferred_element_type=jnp.float32)  5.9 us
  transfers between devices with their start and end apart: 33, of which 8 were waited for; matrix products, arithmetic and copies ran while one was open for 11% of the time, Pallas kernels for 17%

profile of v2, /device:TPU:1, one launch (start us, length us, event | category | flops | bytes accessed | tf_op | source)
XLA Modules:
  0.0 169.5 jit_solution(6130078336776973527)
XLA Ops:
  4.4 4.9 %pack.1 = (bf16[6,2,512,128]{3,2,1,0:T(8,128)(2,1)}, bf16[6,2,512,128]{3,2,1,0:T(8,128)(2,1)}, bf16[2,2,512,128]{3,2,1,0:T(8,128)(2,1)}, bf16[2,2,512,128]{3,2,1...) custom-call(s32[1]{0:T(128)} %bitcast.4.me_ref.refs_0_, ...), custom_call_target="tpu_custom_call" | custom-call | bytes 10485760 | tf_op jit(solution)/shard_map/pack/pack/pallas_call | solution.py:113
  12.6 3.6 %collective-permute-start = (bf16[6,2,512,128]{3,2,1,0:T(8,128)(2,1)}, bf16[6,2,512,128]{3,2,1,0:T(8,128)(2,1)}, u32[]{:S(2)}, u32[]{:S(2)}) collective-permute-start(bf16[6,2,512,128]{3,2,1,0:T(8,128)(2,1)} %get-tuple-element.47), channel_id=1, source_target_pairs={{0,64},{8,72},{16,80},{24,88},{32,96},{40,104},{48,112},{56,120},{... | collective-permute-start | bytes 4718600 | tf_op jit(solution)/shard_map/documents/ppermute | solution.py:53
  16.1 2.9 %collective-permute-start.1 = (bf16[6,2,512,128]{3,2,1,0:T(8,128)(2,1)}, bf16[6,2,512,128]{3,2,1,0:T(8,128)(2,1)}, u32[]{:S(2)}, u32[]{:S(2)}) collective-permute-start(bf16[6,2,512,128]{3,2,1,0:T(8,128)(2,1)} %get-tuple-element.48), channel_id=1, source_target_pairs={{0,16},{8,24},{16,0},{24,8},{32,48},{40,56},{48,32},{56,40},{64,80... | collective-permute-start | bytes 4718600 | tf_op jit(solution)/shard_map/documents/ppermute | solution.py:53
  19.4 4.4 %collective-permute-start.3 = (bf16[2,2,512,128]{3,2,1,0:T(8,128)(2,1)}, bf16[2,2,512,128]{3,2,1,0:T(8,128)(2,1)S(1)}, u32[]{:S(2)}, u32[]{:S(2)}) collective-permute-start(bf16[2,2,512,128]{3,2,1,0:T(8,128)(2,1)} %get-tuple-element.53), channel_id=1, source_target_pairs={{0,120},{8,96},{16,104},{24,112},{32,24},{40,0},{48,8},{56,16},{64... | collective-permute-start | bytes 1572872 | tf_op jit(solution)/shard_map/documents/ppermute | solution.py:53
  23.8 3.6 %fusion = f32[2,320]{1,0:T(2,128)S(1)} fusion(bf16[2,320,4096]{2,1,0:T(8,128)(2,1)} %param.11), kind=kLoop, calls=%fused_computation.2 | loop fusion | flops 7863680 | bytes 5245440 | tf_op jit(solution)/shard_map/projections/reduce_sum | solution.py:342
  28.7 4.4 %fusion.2 = bf16[2,320,4096]{2,1,0:T(8,128)(2,1)S(1)} fusion(bf16[2,320,4096]{2,1,0:T(8,128)(2,1)} %param.11, f32[4096]{0:T(1024)S(1)} %copy-done.22, f32[2,320]{1,0:T(2,128)S(1)} %add_rsqrt_fusion), kind=kLoop, calls=%fused_computation.4 | loop fusion | flops 10485760 | bytes 10504704 | tf_op jit(solution)/shard_map/projections/convert_element_type | solution.py:343
  36.9 2.9 %convolution_convert_fusion = bf16[640,512]{1,0:T(8,128)(2,1)S(1)} fusion(bf16[640,4096]{1,0:T(8,128)(2,1)S(1)} %bitcast.23, bf16[4096,512]{1,0:T(8,128)(2,1)S(1)} %copy-done.24), kind=kOutput, calls=%fused_computation.5 | convolution fusion | flops 2684682240 | bytes 10092544 | tf_op jit(solution)/shard_map/projections/dot_general | solution.py:347
  39.8 5.2 %attend.6 = (f32[2,2,640,128]{3,2,1,0:T(8,128)S(1)}, f32[2,2,640,128]{3,2,1,0:T(8,128)S(1)}, f32[2,2,640,128]{3,2,1,0:T(8,128)S(1)}) custom-call(s32[1]{0:T(128)} %bitcast.4.me_ref.refs_0_, s32[64]{0:T(128)S(1)} %get-tuple-element.43.refs_1_, bf16[2,320,512]{2,1,0:T(8,128)(2,1)S(1)} %bitcast.15, s32[2,2,640,1]{3,2,1,0:T(8,128)S(1)} %reshape.39.refs_3_, ...), custom_call_target="tpu_custom_call" | custom-call | flops 335544320 | bytes 8650752 | tf_op jit(solution)/shard_map/attention/attend/pallas_call | solution.py:234
  45.0 5.2 %collective-permute-done.refs_7_ = bf16[6,2,512,128]{3,2,1,0:T(8,128)(2,1)} collective-permute-done((bf16[6,2,512,128]{3,2,1,0:T(8,128)(2,1)}, bf16[6,2,512,128]{3,2,1,0:T(8,128)(2,1)}, u32[]{:S(2)}, u32[]{:S(2)}) %collective-permute-start) | collective-permute-done | bytes 1572896 | tf_op jit(solution)/shard_map/documents/ppermute | solution.py:53
  50.1 3.9 %collective-permute-start.5 = (bf16[2,2,512,128]{3,2,1,0:T(8,128)(2,1)S(1)}, bf16[2,2,512,128]{3,2,1,0:T(8,128)(2,1)S(1)}, u32[]{:S(2)}, u32[]{:S(2)}) collective-permute-start(bf16[2,2,512,128]{3,2,1,0:T(8,128)(2,1)S(1)} %copy-done.21), channel_id=1, source_target_pairs={{0,104},{8,112},{16,120},{24,96},{32,8},{40,16},{48,24},{56,0},{64... | collective-permute-start | bytes 1572872 | tf_op jit(solution)/shard_map/documents/ppermute | solution.py:53
  54.0 10.3 %collective-permute-done.1.refs_8_ = bf16[6,2,512,128]{3,2,1,0:T(8,128)(2,1)} collective-permute-done((bf16[6,2,512,128]{3,2,1,0:T(8,128)(2,1)}, bf16[6,2,512,128]{3,2,1,0:T(8,128)(2,1)}, u32[]{:S(2)}, u32[]{:S(2)}) %collective-permute-start.1) | collective-permute-done | bytes 1572896 | tf_op jit(solution)/shard_map/documents/ppermute | solution.py:53
  67.0 8.5 %collective-permute-done.4.refs_9_ = bf16[2,2,512,128]{3,2,1,0:T(8,128)(2,1)} collective-permute-done((bf16[2,2,512,128]{3,2,1,0:T(8,128)(2,1)}, bf16[2,2,512,128]{3,2,1,0:T(8,128)(2,1)}, u32[]{:S(2)}, u32[]{:S(2)}) %collective-permute-start.4) | collective-permute-done | bytes 524320 | tf_op jit(solution)/shard_map/documents/ppermute | solution.py:53
  79.2 4.4 %attend.7 = (f32[2,2,640,128]{3,2,1,0:T(8,128)S(1)}, f32[2,2,640,128]{3,2,1,0:T(8,128)S(1)}, f32[2,2,640,128]{3,2,1,0:T(8,128)S(1)}) custom-call(s32[1]{0:T(128)} %bitcast.4.me_ref.refs_0_, s32[64]{0:T(128)S(1)} %get-tuple-element.43.refs_1_, bf16[2,320,512]{2,1,0:T(8,128)(2,1)S(1)} %bitcast.16, ...), custom_call_target="tpu_custom_call", output_to_operand_aliasing={{0}: (4, {}), {1}: (5, {}), {2}: (6, {})} | custom-call | flops 671088640 | bytes 8912896 | tf_op jit(solution)/shard_map/attention/attend/pallas_call | solution.py:234
  85.7 4.7 %attend.8 = (f32[2,2,640,128]{3,2,1,0:T(8,128)S(1)}, f32[2,2,640,128]{3,2,1,0:T(8,128)S(1)}, f32[2,2,640,128]{3,2,1,0:T(8,128)S(1)}) custom-call(s32[1]{0:T(128)} %bitcast.4.me_ref.refs_0_, s32[64]{0:T(128)S(1)} %get-tuple-element.43.refs_1_, bf16[2,320,512]{2,1,0:T(8,128)(2,1)S(1)} %bitcast.17, ...), custom_call_target="tpu_custom_call", output_to_operand_aliasing={{0}: (4, {}), {1}: (5, {}), {2}: (6, {})} | custom-call | flops 1342177280 | bytes 9437184 | tf_op jit(solution)/shard_map/attention/attend/pallas_call | solution.py:234
  90.4 5.9 %collective-permute-start.11 = (bf16[2,2,512,128]{3,2,1,0:T(8,128)(2,1)S(1)}, bf16[2,2,512,128]{3,2,1,0:T(8,128)(2,1)S(1)}, u32[]{:S(2)}, u32[]{:S(2)}) collective-permute-start(bf16[2,2,512,128]{3,2,1,0:T(8,128)(2,1)S(1)} %get-tuple-element.71), channel_id=1, source_target_pairs={{0,96},{8,104},{16,112},{24,120},{32,0},{40,8},{48,16},{56,24},{64... | collective-permute-start | bytes 1572872 | tf_op jit(solution)/shard_map/documents/ppermute | solution.py:53
  96.3 4.7 %collective-permute-start.13 = (bf16[2,2,512,128]{3,2,1,0:T(8,128)(2,1)S(1)}, bf16[2,2,512,128]{3,2,1,0:T(8,128)(2,1)S(1)}, u32[]{:S(2)}, u32[]{:S(2)}) collective-permute-start(bf16[2,2,512,128]{3,2,1,0:T(8,128)(2,1)S(1)} %get-tuple-element.73), channel_id=1, source_target_pairs={{0,24},{8,0},{16,8},{24,16},{32,56},{40,32},{48,40},{56,48},{64,88... | collective-permute-start | bytes 1572872 | tf_op jit(solution)/shard_map/documents/ppermute | solution.py:53
  101.5 7.6 %attend.9 = (f32[2,2,640,128]{3,2,1,0:T(8,128)S(1)}, f32[2,2,640,128]{3,2,1,0:T(8,128)S(1)}, f32[2,2,640,128]{3,2,1,0:T(8,128)S(1)}) custom-call(s32[1]{0:T(128)} %bitcast.4.me_ref.refs_0_, s32[64]{0:T(128)S(1)} %get-tuple-element.43.refs_1_, bf16[2,320,512]{2,1,0:T(8,128)(2,1)S(1)} %bitcast.18, ...), custom_call_target="tpu_custom_call", output_to_operand_aliasing={{0}: (4, {}), {1}: (5, {}), {2}: (6, {})} | custom-call | flops 1342177280 | bytes 9437184 | tf_op jit(solution)/shard_map/attention/attend/pallas_call | solution.py:234
  109.1 4.1 %collective-permute-done.12.refs_9_ = bf16[2,2,512,128]{3,2,1,0:T(8,128)(2,1)S(1)} collective-permute-done((bf16[2,2,512,128]{3,2,1,0:T(8,128)(2,1)S(1)}, bf16[2,2,512,128]{3,2,1,0:T(8,128)(2,1)S(1)}, u32[]{:S(2)}, u32[]{:S(2)}) %collective-permute-start.12) | collective-permute-done | bytes 524320 | tf_op jit(solution)/shard_map/documents/ppermute | solution.py:53
  113.1 6.6 %collective-permute-done.13.refs_10_ = bf16[2,2,512,128]{3,2,1,0:T(8,128)(2,1)S(1)} collective-permute-done((bf16[2,2,512,128]{3,2,1,0:T(8,128)(2,1)S(1)}, bf16[2,2,512,128]{3,2,1,0:T(8,128)(2,1)S(1)}, u32[]{:S(2)}, u32[]{:S(2)}) %collective-permute-start.13) | collective-permute-done | bytes 524320 | tf_op jit(solution)/shard_map/documents/ppermute | solution.py:53
  119.7 7.7 %attend.10 = (f32[2,2,640,128]{3,2,1,0:T(8,128)S(1)}, f32[2,2,640,128]{3,2,1,0:T(8,128)S(1)}, f32[2,2,640,128]{3,2,1,0:T(8,128)S(1)}, bf16[320,512]{1,0:T(8,128)(2,1)}) custom-call(s32[1]{0:T(128)} %bitcast.4.me_ref.refs_0_, s32[64]{0:T(128)S(1)} %get-tuple-element.43.refs_1_, ...), custom_call_target="tpu_custom_call", output_to_operand_aliasing={{0}: (4, {}), {1}: (5, {}), {2}: (6, {})} | custom-call | flops 838860800 | bytes 4849664 | tf_op jit(solution)/shard_map/attention/attend/pallas_call | solution.py:234
  131.3 4.0 %attend.11 = (f32[2,2,640,128]{3,2,1,0:T(8,128)S(1)}, f32[2,2,640,128]{3,2,1,0:T(8,128)S(1)}, f32[2,2,640,128]{3,2,1,0:T(8,128)S(1)}, bf16[320,512]{1,0:T(8,128)(2,1)S(1)}) custom-call(s32[1]{0:T(128)} %bitcast.4.me_ref.refs_0_, s32[64]{0:T(128)S(1)} %get-tuple-element.43.refs_1_, ...), custom_call_target="tpu_custom_call", output_to_operand_aliasing={{0}: (4, {}), {1}: (5, {}), {2}: (6, {})} | custom-call | flops 838860800 | bytes 4849664 | tf_op jit(solution)/shard_map/attention/attend/pallas_call | solution.py:234
  138.0 6.2 %collective-permute-start.28 = (bf16[320,512]{1,0:T(8,128)(2,1)}, bf16[320,512]{1,0:T(8,128)(2,1)S(1)}, u32[]{:S(2)}, u32[]{:S(2)}) collective-permute-start(bf16[320,512]{1,0:T(8,128)(2,1)} %get-tuple-element.80.refs_0_), channel_id=1, source_target_pairs={{0,1},{1,0},{2,3},{3,2},{4,5},{5,4},{6,7},{7,6},{8,9},{9,8},{10,11... | collective-permute-start | bytes 983048 | tf_op jit(solution)/shard_map/output/ppermute | solution.py:299
  162.8 3.4 %project.2.refs_10_ = bf16[2,320,512]{2,1,0:T(8,128)(2,1)} custom-call(s32[8]{0:T(128)S(1)} %pad_add_fusion.place_ref, bf16[4096,512]{1,0:T(8,128)(2,1)S(1)} %copy-done.3, bf16[320,512]{1,0:T(8,128)(2,1)} %get-tuple-element.80.refs_0_, bf16[320,512]{1,0:T(8,128)(2,1)S(1)} %collective-permute-done.24.refs_1_, ...), custom_call_target="tpu_custom_call" | custom-call | flops 1342177280 | bytes 7340032 | tf_op jit(solution)/shard_map/output/project/pallas_call | solution.py:276
  166.2 3.2 %project.3 = bf16[2,320,512]{2,1,0:T(8,128)(2,1)} custom-call(s32[8]{0:T(128)S(1)} %pad_add_fusion.place_ref, bf16[4096,512]{1,0:T(8,128)(2,1)S(1)} %copy-done.3, bf16[320,512]{1,0:T(8,128)(2,1)S(1)} %get-tuple-element.79.refs_0_, bf16[320,512]{1,0:T(8,128)(2,1)S(1)} %collective-permute-done.15.refs_1_, ...), custom_call_target="tpu_custom_call", output_to_operand_aliasing={{}: (12, {})} | custom-call | flops 1342177280 | bytes 7340032 | tf_op jit(solution)/shard_map/output/project/pallas_call | solution.py:276
  (126 shorter events, 47.1 us)
Async XLA Ops:
  12.6 37.6 %collective-permute-start = (bf16[6,2,512,128]{3,2,1,0:T(8,128)(2,1)}, bf16[6,2,512,128]{3,2,1,0:T(8,128)(2,1)}, u32[]{:S(2)}, u32[]{:S(2)}) collective-permute-start(bf16[6,2,512,128]{3,2,1,0:T(8,128)(2,1)} %get-tuple-element.47), channel_id=1, source_target_pairs={{0,64},{8,72},{16,80},{24,88},{32,96},{40,104},{48,112},{56,120},{... | collective-permute-start | bytes 4718600 | tf_op jit(solution)/shard_map/documents/ppermute | solution.py:53
  16.1 48.2 %collective-permute-start.1 = (bf16[6,2,512,128]{3,2,1,0:T(8,128)(2,1)}, bf16[6,2,512,128]{3,2,1,0:T(8,128)(2,1)}, u32[]{:S(2)}, u32[]{:S(2)}) collective-permute-start(bf16[6,2,512,128]{3,2,1,0:T(8,128)(2,1)} %get-tuple-element.48), channel_id=1, source_target_pairs={{0,16},{8,24},{16,0},{24,8},{32,48},{40,56},{48,32},{56,40},{64,80... | collective-permute-start | bytes 4718600 | tf_op jit(solution)/shard_map/documents/ppermute | solution.py:53
  19.0 46.7 %collective-permute-start.2 = (bf16[2,2,512,128]{3,2,1,0:T(8,128)(2,1)}, bf16[2,2,512,128]{3,2,1,0:T(8,128)(2,1)S(1)}, u32[]{:S(2)}, u32[]{:S(2)}) collective-permute-start(bf16[2,2,512,128]{3,2,1,0:T(8,128)(2,1)} %get-tuple-element.52), channel_id=1, source_target_pairs={{0,40},{8,48},{16,56},{24,32},{32,72},{40,80},{48,88},{56,64},{64,... | collective-permute-start | bytes 1572872 | tf_op jit(solution)/shard_map/documents/ppermute | solution.py:53
  19.4 47.6 %collective-permute-start.3 = (bf16[2,2,512,128]{3,2,1,0:T(8,128)(2,1)}, bf16[2,2,512,128]{3,2,1,0:T(8,128)(2,1)S(1)}, u32[]{:S(2)}, u32[]{:S(2)}) collective-permute-start(bf16[2,2,512,128]{3,2,1,0:T(8,128)(2,1)} %get-tuple-element.53), channel_id=1, source_target_pairs={{0,120},{8,96},{16,104},{24,112},{32,24},{40,0},{48,8},{56,16},{64... | collective-permute-start | bytes 1572872 | tf_op jit(solution)/shard_map/documents/ppermute | solution.py:53
  23.8 51.7 %collective-permute-start.4 = (bf16[2,2,512,128]{3,2,1,0:T(8,128)(2,1)}, bf16[2,2,512,128]{3,2,1,0:T(8,128)(2,1)}, u32[]{:S(2)}, u32[]{:S(2)}) collective-permute-start(bf16[2,2,512,128]{3,2,1,0:T(8,128)(2,1)} %get-tuple-element.54), channel_id=1, source_target_pairs={{0,56},{8,32},{16,40},{24,48},{32,88},{40,64},{48,72},{56,80},{64,... | collective-permute-start | bytes 1572872 | tf_op jit(solution)/shard_map/documents/ppermute | solution.py:53
  50.1 34.7 %collective-permute-start.5 = (bf16[2,2,512,128]{3,2,1,0:T(8,128)(2,1)S(1)}, bf16[2,2,512,128]{3,2,1,0:T(8,128)(2,1)S(1)}, u32[]{:S(2)}, u32[]{:S(2)}) collective-permute-start(bf16[2,2,512,128]{3,2,1,0:T(8,128)(2,1)S(1)} %copy-done.21), channel_id=1, source_target_pairs={{0,104},{8,112},{16,120},{24,96},{32,8},{40,16},{48,24},{56,0},{64... | collective-permute-start | bytes 1572872 | tf_op jit(solution)/shard_map/documents/ppermute | solution.py:53
  64.3 26.1 %collective-permute-start.6 = (bf16[2,2,512,128]{3,2,1,0:T(8,128)(2,1)S(1)}, bf16[2,2,512,128]{3,2,1,0:T(8,128)(2,1)S(1)}, u32[]{:S(2)}, u32[]{:S(2)}) collective-permute-start(bf16[2,2,512,128]{3,2,1,0:T(8,128)(2,1)S(1)} %copy-done.19), channel_id=1, source_target_pairs={{0,32},{8,40},{16,48},{24,56},{32,64},{40,72},{48,80},{56,88},{64,... | collective-permute-start | bytes 1572872 | tf_op jit(solution)/shard_map/documents/ppermute | solution.py:53
  65.7 30.5 %collective-permute-start.7 = (bf16[2,2,512,128]{3,2,1,0:T(8,128)(2,1)S(1)}, bf16[2,2,512,128]{3,2,1,0:T(8,128)(2,1)S(1)}, u32[]{:S(2)}, u32[]{:S(2)}) collective-permute-start(bf16[2,2,512,128]{3,2,1,0:T(8,128)(2,1)S(1)} %copy-done.17), channel_id=1, source_target_pairs={{0,96},{8,104},{16,112},{24,120},{32,0},{40,8},{48,16},{56,24},{64... | collective-permute-start | bytes 1572872 | tf_op jit(solution)/shard_map/documents/ppermute | solution.py:53
  67.0 29.3 %collective-permute-start.8 = (bf16[2,2,512,128]{3,2,1,0:T(8,128)(2,1)S(1)}, bf16[2,2,512,128]{3,2,1,0:T(8,128)(2,1)S(1)}, u32[]{:S(2)}, u32[]{:S(2)}) collective-permute-start(bf16[2,2,512,128]{3,2,1,0:T(8,128)(2,1)S(1)} %copy-done.15), channel_id=1, source_target_pairs={{0,8},{8,16},{16,24},{24,0},{32,40},{40,48},{48,56},{56,32},{64,72... | collective-permute-start | bytes 1572872 | tf_op jit(solution)/shard_map/documents/ppermute | solution.py:53
  75.5 25.5 %collective-permute-start.9 = (bf16[2,2,512,128]{3,2,1,0:T(8,128)(2,1)S(1)}, bf16[2,2,512,128]{3,2,1,0:T(8,128)(2,1)S(1)}, u32[]{:S(2)}, u32[]{:S(2)}) collective-permute-start(bf16[2,2,512,128]{3,2,1,0:T(8,128)(2,1)S(1)} %copy-done.13), channel_id=1, source_target_pairs={{0,24},{8,0},{16,8},{24,16},{32,56},{40,32},{48,40},{56,48},{64,88... | collective-permute-start | bytes 1572872 | tf_op jit(solution)/shard_map/documents/ppermute | solution.py:53
  84.9 24.2 %collective-permute-start.10 = (bf16[2,2,512,128]{3,2,1,0:T(8,128)(2,1)S(1)}, bf16[2,2,512,128]{3,2,1,0:T(8,128)(2,1)S(1)}, u32[]{:S(2)}, u32[]{:S(2)}) collective-permute-start(bf16[2,2,512,128]{3,2,1,0:T(8,128)(2,1)S(1)} %get-tuple-element.70), channel_id=1, source_target_pairs={{0,32},{8,40},{16,48},{24,56},{32,64},{40,72},{48,80},{56,88},{64,... | collective-permute-start | bytes 1572872 | tf_op jit(solution)/shard_map/documents/ppermute | solution.py:53
  90.4 18.6 %collective-permute-start.11 = (bf16[2,2,512,128]{3,2,1,0:T(8,128)(2,1)S(1)}, bf16[2,2,512,128]{3,2,1,0:T(8,128)(2,1)S(1)}, u32[]{:S(2)}, u32[]{:S(2)}) collective-permute-start(bf16[2,2,512,128]{3,2,1,0:T(8,128)(2,1)S(1)} %get-tuple-element.71), channel_id=1, source_target_pairs={{0,96},{8,104},{16,112},{24,120},{32,0},{40,8},{48,16},{56,24},{64... | collective-permute-start | bytes 1572872 | tf_op jit(solution)/shard_map/documents/ppermute | solution.py:53
  96.3 16.8 %collective-permute-start.12 = (bf16[2,2,512,128]{3,2,1,0:T(8,128)(2,1)S(1)}, bf16[2,2,512,128]{3,2,1,0:T(8,128)(2,1)S(1)}, u32[]{:S(2)}, u32[]{:S(2)}) collective-permute-start(bf16[2,2,512,128]{3,2,1,0:T(8,128)(2,1)S(1)} %get-tuple-element.72), channel_id=1, source_target_pairs={{0,8},{8,16},{16,24},{24,0},{32,40},{40,48},{48,56},{56,32},{64,72... | collective-permute-start | bytes 1572872 | tf_op jit(solution)/shard_map/documents/ppermute | solution.py:53
  96.3 23.4 %collective-permute-start.13 = (bf16[2,2,512,128]{3,2,1,0:T(8,128)(2,1)S(1)}, bf16[2,2,512,128]{3,2,1,0:T(8,128)(2,1)S(1)}, u32[]{:S(2)}, u32[]{:S(2)}) collective-permute-start(bf16[2,2,512,128]{3,2,1,0:T(8,128)(2,1)S(1)} %get-tuple-element.73), channel_id=1, source_target_pairs={{0,24},{8,0},{16,8},{24,16},{32,56},{40,32},{48,40},{56,48},{64,88... | collective-permute-start | bytes 1572872 | tf_op jit(solution)/shard_map/documents/ppermute | solution.py:53
  101.0 18.7 %collective-permute-start.14 = (bf16[2,2,512,128]{3,2,1,0:T(8,128)(2,1)S(1)}, bf16[2,2,512,128]{3,2,1,0:T(8,128)(2,1)S(1)}, u32[]{:S(2)}, u32[]{:S(2)}) collective-permute-start(bf16[2,2,512,128]{3,2,1,0:T(8,128)(2,1)S(1)} %copy-done.11), channel_id=1, source_target_pairs={{0,80},{8,88},{16,64},{24,72},{32,112},{40,120},{48,96},{56,104},{... | collective-permute-start | bytes 1572872 | tf_op jit(solution)/shard_map/documents/ppermute | solution.py:53
  127.3 16.9 %collective-permute-start.24 = (bf16[320,512]{1,0:T(8,128)(2,1)}, bf16[320,512]{1,0:T(8,128)(2,1)S(1)}, u32[]{:S(2)}, u32[]{:S(2)}) collective-permute-start(bf16[320,512]{1,0:T(8,128)(2,1)} %get-tuple-element.80.refs_0_), channel_id=1, source_target_pairs={{0,2},{1,3},{2,4},{3,5},{4,6},{5,7},{6,0},{7,1},{8,10},{9,11},{10,... | collective-permute-start | bytes 983048 | tf_op jit(solution)/shard_map/output/ppermute | solution.py:295
  129.1 15.5 %collective-permute-start.25 = (bf16[320,512]{1,0:T(8,128)(2,1)}, bf16[320,512]{1,0:T(8,128)(2,1)S(1)}, u32[]{:S(2)}, u32[]{:S(2)}) collective-permute-start(bf16[320,512]{1,0:T(8,128)(2,1)} %get-tuple-element.80.refs_0_), channel_id=1, source_target_pairs={{0,6},{1,7},{2,0},{3,1},{4,2},{5,3},{6,4},{7,5},{8,14},{9,15},{10,... | collective-permute-start | bytes 983048 | tf_op jit(solution)/shard_map/output/ppermute | solution.py:295
  135.2 12.0 %collective-permute-start.15 = (bf16[320,512]{1,0:T(8,128)(2,1)S(1)}, bf16[320,512]{1,0:T(8,128)(2,1)S(1)}, u32[]{:S(2)}, u32[]{:S(2)}) collective-permute-start(bf16[320,512]{1,0:T(8,128)(2,1)S(1)} %get-tuple-element.79.refs_0_), channel_id=1, source_target_pairs={{0,2},{1,3},{2,4},{3,5},{4,6},{5,7},{6,0},{7,1},{8,10},{9,11},{10,... | collective-permute-start | bytes 983048 | tf_op jit(solution)/shard_map/output/ppermute | solution.py:295
  135.3 12.6 %collective-permute-start.16 = (bf16[320,512]{1,0:T(8,128)(2,1)S(1)}, bf16[320,512]{1,0:T(8,128)(2,1)S(1)}, u32[]{:S(2)}, u32[]{:S(2)}) collective-permute-start(bf16[320,512]{1,0:T(8,128)(2,1)S(1)} %get-tuple-element.79.refs_0_), channel_id=1, source_target_pairs={{0,6},{1,7},{2,0},{3,1},{4,2},{5,3},{6,4},{7,5},{8,14},{9,15},{10,... | collective-permute-start | bytes 983048 | tf_op jit(solution)/shard_map/output/ppermute | solution.py:295
  138.0 17.6 %collective-permute-start.28 = (bf16[320,512]{1,0:T(8,128)(2,1)}, bf16[320,512]{1,0:T(8,128)(2,1)S(1)}, u32[]{:S(2)}, u32[]{:S(2)}) collective-permute-start(bf16[320,512]{1,0:T(8,128)(2,1)} %get-tuple-element.80.refs_0_), channel_id=1, source_target_pairs={{0,1},{1,0},{2,3},{3,2},{4,5},{5,4},{6,7},{7,6},{8,9},{9,8},{10,11... | collective-permute-start | bytes 983048 | tf_op jit(solution)/shard_map/output/ppermute | solution.py:299
  144.6 10.3 %collective-permute-start.27 = (bf16[160,512]{1,0:T(8,128)(2,1)S(1)}, bf16[160,512]{1,0:T(8,128)(2,1)S(1)}, u32[]{:S(2)}, u32[]{:S(2)}) collective-permute-start(bf16[160,512]{1,0:T(8,128)(2,1)S(1)} %slice.39), channel_id=1, source_target_pairs={{0,6},{1,7},{2,0},{3,1},{4,2},{5,3},{6,4},{7,5},{8,14},{9,15},{10,... | collective-permute-start | bytes 491528 | tf_op jit(solution)/shard_map/output/ppermute | solution.py:295
  157.1 9.0 %collective-permute-start.19 = (bf16[320,512]{1,0:T(8,128)(2,1)S(1)}, bf16[320,512]{1,0:T(8,128)(2,1)S(1)}, u32[]{:S(2)}, u32[]{:S(2)}) collective-permute-start(bf16[320,512]{1,0:T(8,128)(2,1)S(1)} %get-tuple-element.79.refs_0_), channel_id=1, source_target_pairs={{0,1},{1,0},{2,3},{3,2},{4,5},{5,4},{6,7},{7,6},{8,9},{9,8},{10,11... | collective-permute-start | bytes 983048 | tf_op jit(solution)/shard_map/output/ppermute | solution.py:299
  157.6 8.6 %collective-permute-start.20 = (bf16[320,512]{1,0:T(8,128)(2,1)S(1)}, bf16[320,512]{1,0:T(8,128)(2,1)S(1)}, u32[]{:S(2)}, u32[]{:S(2)}) collective-permute-start(bf16[320,512]{1,0:T(8,128)(2,1)S(1)} %collective-permute-done.15.refs_1_), channel_id=1, source_target_pairs={{0,1},{1,0},{2,3},{3,2},{4,5},{5,4},{6,7},{7,6},{8,9},{9,8},{10,11... | collective-permute-start | bytes 983048 | tf_op jit(solution)/shard_map/output/ppermute | solution.py:299
  157.7 8.5 %collective-permute-start.21 = (bf16[320,512]{1,0:T(8,128)(2,1)S(1)}, bf16[320,512]{1,0:T(8,128)(2,1)S(1)}, u32[]{:S(2)}, u32[]{:S(2)}) collective-permute-start(bf16[320,512]{1,0:T(8,128)(2,1)S(1)} %collective-permute-done.16.refs_2_), channel_id=1, source_target_pairs={{0,1},{1,0},{2,3},{3,2},{4,5},{5,4},{6,7},{7,6},{8,9},{9,8},{10,11... | collective-permute-start | bytes 983048 | tf_op jit(solution)/shard_map/output/ppermute | solution.py:299
  (35 other events, 314.3 us)

commit v3 on v2

v3 whole, which is shorter than its diff:
```python
import functools
import math

import jax
import jax.numpy as jnp
from jax import lax
from jax.experimental import pallas as pl
from jax.experimental.pallas import tpu as pltpu
from jax.sharding import PartitionSpec as P

H = 32
KVH = 8
HD = 128
CAP = 2
GROUP = H // KVH
SIDE = 4
GROUPS = 16
STORED = 16
SLOTS = 16
PICK = 40
DOC = 512
TOKENS = 320
RETRIEVED = 8
TILES = 4
SUB = TOKENS // TILES
ROWS = SUB * GROUP
PADDED = 384
FAR = 2**30
EXP2 = HD ** (-0.5) * math.log2(math.e)

NEAR = [(1, 0), (3, 0), (0, 1), (0, 3)]
DIAGONAL = [(1, 1), (3, 3), (1, 3), (3, 1)]
OPPOSITE = [(2, 2)]
KNIGHT = [(1, 2), (3, 2), (2, 1), (2, 3)]
TWO = [(2, 0), (0, 2)]
CARRIED = {(2, 0): [(2, 0), (2, 1), (2, 3)], (0, 2): [(0, 2), (1, 2), (3, 2)]}
EARLY = [CARRIED[s] for s in TWO]
LATE = [[s] for s in DIAGONAL + NEAR + OPPOSITE]
CHOSEN = GROUPS * CAP + 2 * SLOTS
STAGES = [[(0, 0)], TWO, DIAGONAL, NEAR + OPPOSITE, KNIGHT]
JOINED = []
ROOM = 24 << 20
ALL_ROOM = 56 << 20
PROJECT_ROOM = 56 << 20

ANY = pl.BlockSpec(memory_space=pl.ANY)
HBM = pl.BlockSpec(memory_space=pltpu.HBM)
VMEM = pl.BlockSpec(memory_space=pltpu.VMEM)
SMEM = pl.BlockSpec(memory_space=pltpu.SMEM)


def shift(block, by):
    pairs = [
        (x * SIDE + y, (x + by[0]) % SIDE * SIDE + (y + by[1]) % SIDE)
        for x in range(SIDE)
        for y in range(SIDE)
    ]
    return lax.ppermute(block, "grp", pairs)


def copy_chosen(table_ref, cache_ref, blocks, out_refs, stage, read_sem, write_sem, between):
    me = table_ref[CHOSEN + GROUPS * CAP]
    x, y = me // SIDE, me % SIDE

    def each(act):
        at = 0
        for block, out in zip(blocks, out_refs):
            for n, (dx, dy) in enumerate(block):
                g = (x + dx) % SIDE * SIDE + (y + dy) % SIDE
                for k in range(CAP):
                    doc = table_ref[CHOSEN + g * CAP + k]

                    @pl.when(doc >= 0)
                    def _(at=at, doc=doc, out=out.at[n * CAP + k]):
                        act(at, doc, out)

                    at += 1

    def read(at, doc):
        return pltpu.make_async_copy(cache_ref.at[doc], stage.at[at], read_sem.at[at])

    def write(at, out):
        return pltpu.make_async_copy(stage.at[at], out, write_sem.at[at])

    def forward(at, doc, out):
        read(at, doc).wait()
        write(at, out).start()

    each(lambda at, doc, out: read(at, doc).start())
    between()
    each(forward)
    each(lambda at, doc, out: write(at, out).wait())


def first_pack_kernel(me_ref, home_ref, ids_ref, len_ref, cache_ref, *refs):
    out_refs, (table_ref, *scratch) = refs[: len(EARLY)], refs[len(EARLY) :]
    me = me_ref[0]

    def outgoing(g, carry):
        one, two = jnp.int32(-1), jnp.int32(-1)
        for i in range(SLOTS):
            slot = home_ref[ids_ref[g * SLOTS + i]] - me * STORED
            hit = (slot >= 0) & (slot < STORED)
            two = jnp.where(hit, one, two)
            one = jnp.where(hit, slot, one)
        table_ref[CHOSEN + g * CAP] = jnp.where(two >= 0, two, one)
        table_ref[CHOSEN + g * CAP + 1] = jnp.where(two >= 0, one, -1)
        return carry

    lax.fori_loop(0, GROUPS, outgoing, 0)
    table_ref[CHOSEN + GROUPS * CAP] = me

    def incoming():
        for at in range(GROUPS * CAP):
            table_ref[at] = jnp.int32(-1)
        for i in range(SLOTS):
            doc = ids_ref[me * SLOTS + i]
            location = home_ref[doc]
            at = location // STORED * CAP
            table_ref[at + jnp.where(table_ref[at] >= 0, 1, 0)] = jnp.int32(i)
            table_ref[GROUPS * CAP + i] = location % STORED
            table_ref[GROUPS * CAP + SLOTS + i] = len_ref[doc]

    copy_chosen(table_ref, cache_ref, EARLY, out_refs, *scratch, incoming)


def second_pack_kernel(table_ref, cache_ref, *refs):
    out_refs, scratch = refs[: len(LATE)], refs[len(LATE) :]
    copy_chosen(table_ref, cache_ref, LATE, out_refs, *scratch, lambda: None)


def pack(kernel, blocks, scalars, cache, with_table):
    shapes = [(CAP * len(b), 2, DOC, HD) for b in blocks]
    total = sum(s[0] for s in shapes)
    table = [jax.ShapeDtypeStruct((CHOSEN + GROUPS * CAP + 1,), jnp.int32)] if with_table else []
    return pl.pallas_call(
        kernel,
        out_shape=[jax.ShapeDtypeStruct(s, jnp.bfloat16) for s in shapes] + table,
        in_specs=[SMEM] * len(scalars) + [HBM],
        out_specs=[HBM] * len(blocks) + [SMEM] * len(table),
        scratch_shapes=[
            pltpu.VMEM((total, 2, DOC, HD), jnp.bfloat16),
            pltpu.SemaphoreType.DMA((total,)),
            pltpu.SemaphoreType.DMA((total,)),
        ],
        compiler_params=pltpu.CompilerParams(vmem_limit_bytes=ALL_ROOM),
        cost_estimate=pl.CostEstimate(flops=0, bytes_accessed=5 << 20, transcendentals=0),
        name="pack",
    )(*scalars, cache)


def attend_kernel(shifts, count, first, last, *refs):
    refs = list(refs)
    table_ref, q_ref, pos_ref = refs[:3]
    if first:
        new_idx_ref, new_k_ref, new_v_ref = refs[3:6]
    arrays, refs = refs[6 : 6 + len(shifts)], refs[6 + len(shifts) :]
    acc, top_ref, sum_ref, *refs = refs
    if last:
        out_ref, *refs = refs
    buf, items, sem = refs
    me = table_ref[CHOSEN + GROUPS * CAP]
    x, y = me // SIDE, me % SIDE

    found = jnp.int32(0)
    for (dx, dy), array in zip(shifts, arrays):
        skip = CAP if (dx, dy) in JOINED else 0
        source = (x - dx + SIDE) % SIDE * SIDE + (y - dy + SIDE) % SIDE
        for k in range(CAP):
            i = table_ref[source * CAP + k]
            mine = i >= 0

            @pl.when(mine)
            def _(i=i, array=array, k=k, at=found, own=(dx, dy) == (0, 0)):
                where = table_ref[GROUPS * CAP + i] if own else k + skip
                items[at] = i
                pltpu.make_async_copy(array.at[where], buf.at[at], sem.at[at]).start()

            found = found + jnp.where(mine, 1, 0)

    def scores(r, tile, wide, keys, idx):
        q = []
        for n in range(wide):
            rows = pl.ds(pl.multiple_of((tile + n) * SUB, SUB), SUB)
            q += [q_ref[r, rows, h * HD : (h + 1) * HD] for h in range(GROUP)]
        s = lax.dot_general(
            jnp.concatenate(q, axis=0),
            keys,
            (((1,), (1,)), ((), ())),
            preferred_element_type=jnp.float32,
        )
        pos = pos_ref[r, pl.ds(tile, wide)].reshape(wide * ROWS, 1)
        return jnp.where(idx <= pos, s, -1e30)

    def weigh(s, top):
        p = jnp.exp2((s - jnp.concatenate([top] * (s.shape[1] // HD), axis=1)) * EXP2)
        parts = [p[:, c : c + HD] for c in range(0, s.shape[1], HD)]
        return p.astype(jnp.bfloat16), functools.reduce(jnp.add, parts)

    def put(ref, r, tile, wide, value):
        ref[r, pl.ds(tile, wide)] = value.reshape(wide, ROWS, HD)

    if first:

        def start(at, carry):
            r, tile = at // (TILES // 2), at % (TILES // 2) * 2
            s = scores(r, tile, 2, new_k_ref[r], new_idx_ref[r])
            top = jnp.broadcast_to(jnp.max(s, axis=1, keepdims=True), (2 * ROWS, HD))
            p, sums = weigh(s, top)
            put(top_ref, r, tile, 2, top)
            put(sum_ref, r, tile, 2, sums)
            value = jnp.dot(p, new_v_ref[r], preferred_element_type=jnp.float32)
            put(acc, r, tile, 2, value)
            return carry

        lax.fori_loop(0, count * TILES // 2, start, 0)

    def item(at, carry):
        i = items[at]
        r, j = i // RETRIEVED, i % RETRIEVED
        length = table_ref[GROUPS * CAP + SLOTS + i]
        row = lax.broadcasted_iota(jnp.int32, (1, DOC), 1)
        idx = row + j * DOC
        per = RETRIEVED // TILES
        picked = pos_ref[r, j // per, pl.ds(pl.multiple_of(j % per * PICK, PICK), PICK)]
        replaced = jnp.max(jnp.where(picked == idx, 1, 0), axis=0, keepdims=True)
        idx = jnp.where((row < length) & (replaced == 0), idx, FAR)
        pltpu.make_async_copy(arrays[0].at[0], buf.at[at], sem.at[at]).wait()

        def step(tile, wide):
            def get(ref):
                return ref[r, pl.ds(tile, wide)].reshape(wide * ROWS, HD)

            s = scores(r, tile, wide, buf[at, 0], idx)
            before = get(top_ref)
            top = jnp.maximum(before, jnp.max(s, axis=1, keepdims=True))
            fade = jnp.exp2((before - top) * EXP2)
            p, sums = weigh(s, top)
            put(top_ref, r, tile, wide, top)
            put(sum_ref, r, tile, wide, get(sum_ref) * fade + sums)
            value = jnp.dot(p, buf[at, 1], preferred_element_type=jnp.float32)
            put(acc, r, tile, wide, get(acc) * fade + value)

        tile = j // per

        @pl.when(tile % 2 == 1)
        def _():
            step(tile, 1)

        def pair(n, carry):
            step(n * 2, 2)
            return carry

        lax.fori_loop((tile + 1) // 2, TILES // 2, pair, 0)
        return carry

    lax.fori_loop(0, found, item, 0)

    if last:
        for r in range(count):
            for tile in range(TILES):
                sums = jnp.sum(sum_ref[r, tile], axis=1, keepdims=True)
                done = (acc[r, tile] / sums).astype(jnp.bfloat16)
                rows = slice(r * TOKENS + tile * SUB, r * TOKENS + (tile + 1) * SUB)
                for h in range(GROUP):
                    out_ref[rows, h * HD : (h + 1) * HD] = done[h * SUB : (h + 1) * SUB]


def attend(table, query, pos, extra, arrays, shifts, first, last):
    cands, count = CAP * len(arrays), query.shape[0]

    state = jax.ShapeDtypeStruct((count, TILES, ROWS, HD), jnp.float32)
    out_shape = [state] * 3
    if last:
        out_shape.append(jax.ShapeDtypeStruct((count * TOKENS, GROUP * HD), jnp.bfloat16))
    return pl.pallas_call(
        functools.partial(attend_kernel, shifts, count, first, last),
        out_shape=out_shape,
        in_specs=[SMEM] + [VMEM] * 5 + [ANY] * len(arrays),
        out_specs=[VMEM] * len(out_shape),
        scratch_shapes=[
            pltpu.VMEM((cands, 2, DOC, HD), jnp.bfloat16),
            pltpu.SMEM((cands,), jnp.int32),
            pltpu.SemaphoreType.DMA((cands,)),
        ],
        input_output_aliases={} if first else {3: 0, 4: 1, 5: 2},
        compiler_params=pltpu.CompilerParams(vmem_limit_bytes=ROOM),
        cost_estimate=pl.CostEstimate(
            flops=count * 2 * 1280 * 512 * 128 * len(arrays),
            bytes_accessed=count * ((4 << 20) + len(arrays) * (1 << 17)),
            transcendentals=count * 1280 * 512 * len(arrays) // 2,
        ),
        name="attend",
    )(table, query, pos, *extra, *arrays)


def project_kernel(spans, last, place_ref, w_ref, *refs):
    parts, refs = refs[: len(spans)], refs[len(spans) :]
    if last:
        before_ref, *refs = refs
    out_ref, w, held, w_sem, part_sem = refs
    width = GROUP * HD
    order = list(dict.fromkeys(n for n, _, _ in spans))

    def weights(slot):
        rows = pl.ds(pl.multiple_of(place_ref[order[slot]] * width, width), width)
        return pltpu.make_async_copy(w_ref.at[rows], w.at[slot], w_sem.at[slot])

    def piece(at):
        n, lo, hi = spans[at]
        target = held.at[order.index(n), lo:hi]
        return pltpu.make_async_copy(parts[at], target, part_sem.at[at])

    for slot, n in enumerate(order):
        weights(slot).start()
        for at in range(len(spans)):
            if spans[at][0] == n:
                piece(at).start()
    total = before_ref[...] if last else None
    for slot, n in enumerate(order):
        weights(slot).wait()
        for at in range(len(spans)):
            if spans[at][0] == n:
                piece(at).wait()
        term = jnp.dot(held[slot], w[slot], preferred_element_type=jnp.float32)
        total = term if total is None else total + term
    out_ref[...] = total.astype(out_ref.dtype)


def project(place, pieces, w_out, before):
    spans, parts = [p[:3] for p in pieces], [p[3] for p in pieces]
    rows, columns = max(hi for _, _, hi in spans), w_out.shape[1]
    blocks, last = len({n for n, _, _ in spans}), before is not None
    return pl.pallas_call(
        functools.partial(project_kernel, spans, last),
        out_shape=jax.ShapeDtypeStruct((rows, columns), jnp.bfloat16 if last else jnp.float32),
        in_specs=[SMEM, HBM] + [ANY] * len(parts) + [VMEM] * last,
        out_specs=VMEM,
        scratch_shapes=[
            pltpu.VMEM((blocks, GROUP * HD, columns), jnp.bfloat16),
            pltpu.VMEM((blocks, rows, GROUP * HD), jnp.bfloat16),
            pltpu.SemaphoreType.DMA((blocks,)),
            pltpu.SemaphoreType.DMA((len(parts),)),
        ],
        compiler_params=pltpu.CompilerParams(vmem_limit_bytes=PROJECT_ROOM),
        cost_estimate=pl.CostEstimate(
            flops=2 * rows * blocks * 512 * 512, bytes_accessed=blocks << 20, transcendentals=0
        ),
        name="project",
    )(place, w_out, *parts, *([before] if last else []))


def ring(block, by):
    return lax.ppermute(block, "tp", [(i, (i + 2 * by) % KVH) for i in range(KVH)])


def other_core(block):
    return lax.ppermute(block, "tp", [(i, i ^ 1) for i in range(KVH)])


def body(
    sel_hidden,
    norm_gain,
    w_query,
    w_key,
    w_value,
    w_out,
    doc_cache,
    home,
    doc_ids,
    doc_len,
    positions,
):
    me = lax.axis_index("grp").astype(jnp.int32).reshape(1)
    served = sel_hidden.shape[0]

    with jax.named_scope("pack"):
        scalars = [me, home, doc_ids.reshape(-1), doc_len]
        *early, table = pack(first_pack_kernel, EARLY, scalars, doc_cache, True)
        late = list(pack(second_pack_kernel, LATE, [table], doc_cache, False))
        packed = {b[0]: p for b, p in zip(EARLY + LATE, early + late)}

    with jax.named_scope("positions"):
        new_index = jnp.pad(
            positions, ((0, 0), (0, PADDED - TOKENS)), constant_values=FAR
        ).reshape(served, 1, PADDED)
        row_pos = jnp.broadcast_to(
            positions.reshape(served, TILES, 1, SUB), (served, TILES, GROUP, SUB)
        ).reshape(served, TILES, ROWS, 1)

    with jax.named_scope("projections"):
        xf = sel_hidden.astype(jnp.float32)
        normed = (
            xf * lax.rsqrt(jnp.mean(xf * xf, axis=-1, keepdims=True) + 1e-05) * norm_gain
        ).astype(jnp.bfloat16)
        normed_rows = normed.reshape(served * TOKENS, normed.shape[2])

        def dot(w):
            out = jnp.dot(normed_rows, w, preferred_element_type=jnp.float32)
            return out.astype(jnp.bfloat16).reshape(served, TOKENS, w.shape[1])

        query, key_new, value_new = dot(w_query), dot(w_key), dot(w_value)
        pad = ((0, 0), (0, PADDED - TOKENS), (0, 0))
        key_new, value_new = jnp.pad(key_new, pad), jnp.pad(value_new, pad)

    arrived = {(0, 0): doc_cache}

    def after(blocks, *done):
        return lax.optimization_barrier((blocks, done))[0]

    def send(names, blocks, hops):
        with jax.named_scope("documents"):
            for s, block, hop in zip(names, blocks, hops):
                arrived[s] = shift(block, hop)

    def attention(n, state):
        shifts, last = STAGES[n], n == len(STAGES) - 1
        with jax.named_scope("attention"):
            return attend(
                table,
                query,
                row_pos,
                state,
                [arrived[s] for s in shifts],
                shifts,
                n == 0,
                last,
            )

    send(TWO, [packed[s] for s in TWO], TWO)
    send(DIAGONAL, [packed[s] for s in DIAGONAL], DIAGONAL)
    state = attention(0, [new_index, key_new, value_new])
    now = NEAR + OPPOSITE
    send(now, after([packed[s] for s in now], [arrived[s] for s in TWO], state), now)
    state = attention(1, state)
    blocks = []
    for s in KNIGHT:
        through = (0, 2) if s[1] == 2 else (2, 0)
        at = CAP * CARRIED[through].index(s)
        blocks.append(arrived[through][at : at + CAP])
    send(KNIGHT, after(blocks, [arrived[s] for s in DIAGONAL], state), NEAR)
    state = attention(2, state)
    state = attention(3, state)
    own = attention(len(STAGES) - 1, state)[-1]

    with jax.named_scope("output"):
        tp = lax.axis_index("tp")
        z, core = tp // 2, tp % 2
        planes = jnp.stack([z, (z + 3) % SIDE, (z + 1) % SIDE, (z + 2) % SIDE])
        place = jnp.concatenate([planes * 2 + core, planes * 2 + 1 - core]).astype(jnp.int32)
        rows = served * TOKENS
        half = rows // 2
        up, down, core = ring(own, 1), ring(own, -1), other_core(own)
        near = [(0, own), (4, core), (1, up), (2, down), (5, other_core(up)), (6, other_core(down))]
        near = [(n, 0, rows, p) for n, p in near]
        far = [ring(up[:half], 1), ring(down[half:], -1)]
        partial = project(place, near, w_out, None)
        far = lax.optimization_barrier((far, partial))[0]
        cross = [other_core(p) for p in far]
        pieces = [(3, 0, half, far[0]), (3, half, rows, far[1])]
        pieces += [(7, 0, half, cross[0]), (7, half, rows, cross[1])]
        mixed = project(place, pieces, w_out, partial)
        return mixed.reshape(served, TOKENS, w_out.shape[1])


def solution(mesh):
    return jax.shard_map(
        body,
        mesh=mesh,
        in_specs=(
            P("grp", None, None),
            P(),
            P(None, "tp"),
            P(None, "tp"),
            P(None, "tp"),
            P(None, "tp"),
            P("grp", None, None, "tp"),
            P(),
            P(),
            P(),
            P("grp", None),
        ),
        out_specs=P("grp", None, "tp"),
        check_vma=False,
    )
```

time: 171 us -> 159 us (0.930)
  local copies, waits for them, and re-layouts: 18.8 us -> 7.89 us
  Pallas kernels: 44.9 us -> 49.9 us
  other arithmetic: 8.15 us -> 3.71 us
  matrix products: 5.9 us -> 9.35 us
  waiting for transfers between devices: 36.8 us -> 33.8 us
    unnamed x53 -> x43, local copies, waits for them, and re-layouts: 13.6 us -> 2.99 us
    ppermute x10 -> x5, starting transfers between devices: 11.3 us -> 16.6 us  [other_core(): return lax.ppermute(block, 'tp', [(i, i ^ 1) for i in range(KVH)])]
    ppermute x8 -> x4, starting transfers between devices: 12.3 us -> 7.26 us  [ring(): lax.ppermute(block, 'tp', [(i, (i + 2 * by) % KVH) for i in range(KVH)])]
    pallas_call x9, Pallas kernels: 44.9 us -> 49.9 us  [the longest x5 30.5 us: attend(): pl.pallas_call(functools.partial(attend_kernel, shifts, count, first, las...]
    ppermute x15, waiting for transfers between devices: 36 us -> 31.1 us  [shift(): return lax.ppermute(block, 'grp', pairs)]
    dot_general x3, matrix products: 5.9 us -> 9.35 us  [dot(): out = jnp.dot(normed_rows, w, preferred_element_type=jnp.float32)]
    convert_element_type x1, other arithmetic: 4.4 us -> 1.91 us  [body(): normed = (xf * lax.rsqrt(jnp.mean(xf * xf, axis=-1, keepdims=True) + 1e-0...]
    reduce_sum x1, other arithmetic: 3.59 us -> 1.1 us  [body(): jnp.mean(xf * xf, axis=-1, keepdims=True) + 1e-05]
  transfers between devices with their start and end apart: 33 -> 24, of which waited for: 8 -> 8; matrix products, arithmetic and copies ran while one was open for 11% -> 11% of each run, Pallas kernels for 17% -> 20%
where the time goes in v3:
time: 159 us; the launch traced here: 158 us
  starting transfers between devices  52.9 us (33%)
  Pallas kernels  49.9 us (31%)
  waiting for transfers between devices  33.8 us (21%)
  matrix products  9.35 us (6%)
  local copies, waits for them, and re-layouts  7.89 us (5%)
  other arithmetic  3.71 us (2%)
    ppermute x15, waiting for transfers between devices, shift(): return lax.ppermute(block, 'grp', pairs)  31.1 us
    pallas_call x5, Pallas kernels, attend(): pl.pallas_call(functools.partial(attend_kernel, shifts, count, first, las...  30.5 us
    ppermute x15, starting transfers between devices, shift(): return lax.ppermute(block, 'grp', pairs)  29 us
    ppermute x5, starting transfers between devices, other_core(): return lax.ppermute(block, 'tp', [(i, i ^ 1) for i in range(KVH)])  16.6 us
    pallas_call x2, Pallas kernels, project(): pl.pallas_call(functools.partial(project_kernel, spans, last), out_shape=...  10.3 us
    dot_general x3, matrix products, dot(): out = jnp.dot(normed_rows, w, preferred_element_type=jnp.float32)  9.35 us
    pallas_call x2, Pallas kernels, pack(): pl.pallas_call(kernel, out_shape=[jax.ShapeDtypeStruct(s, jnp.bfloat16) f...  9.1 us
    ppermute x4, starting transfers between devices, ring(): lax.ppermute(block, 'tp', [(i, (i + 2 * by) % KVH) for i in range(KVH)])  7.26 us
  transfers between devices with their start and end apart: 24, of which 8 were waited for; matrix products, arithmetic and copies ran while one was open for 11% of the time, Pallas kernels for 20%

profile of v3, /device:TPU:1, one launch (start us, length us, event | category | flops | bytes accessed | tf_op | source)
XLA Modules:
  0.0 158.1 jit_solution(15900745861025680706)
XLA Ops:
  1.5 5.1 %pack.2 = (bf16[6,2,512,128]{3,2,1,0:T(8,128)(2,1)}, bf16[6,2,512,128]{3,2,1,0:T(8,128)(2,1)}, s32[97]{0:T(128)}) custom-call(s32[1]{0:T(128)} %bitcast.4.me_ref, s32[256]{0:T(256)} %home_ref.1, s32[256]{0:T(256)} %reshape.39.ids_ref, s32[256]{0:T(256)} %len_ref.1, bf16[16,2,512,128]{3,2,1,0:T(8,128)(2,1)} %cache_ref.3), custom_call_target="tpu_custom_call" | custom-call | bytes 5242880 | tf_op jit(solution)/shard_map/pack/pack/pallas_call | solution.py:136
  6.7 3.0 %collective-permute-start = (bf16[6,2,512,128]{3,2,1,0:T(8,128)(2,1)}, bf16[6,2,512,128]{3,2,1,0:T(8,128)(2,1)}, u32[]{:S(2)}, u32[]{:S(2)}) collective-permute-start(bf16[6,2,512,128]{3,2,1,0:T(8,128)(2,1)} %get-tuple-element.45), channel_id=1, source_target_pairs={{0,64},{8,72},{16,80},{24,88},{32,96},{40,104},{48,112},{56,120},{... | collective-permute-start | bytes 4718600 | tf_op jit(solution)/shard_map/documents/ppermute | solution.py:58
  9.6 3.4 %collective-permute-start.1 = (bf16[6,2,512,128]{3,2,1,0:T(8,128)(2,1)}, bf16[6,2,512,128]{3,2,1,0:T(8,128)(2,1)}, u32[]{:S(2)}, u32[]{:S(2)}) collective-permute-start(bf16[6,2,512,128]{3,2,1,0:T(8,128)(2,1)} %get-tuple-element.46), channel_id=1, source_target_pairs={{0,16},{8,24},{16,0},{24,8},{32,48},{40,56},{48,32},{56,40},{64,80... | collective-permute-start | bytes 4718600 | tf_op jit(solution)/shard_map/documents/ppermute | solution.py:58
  13.0 4.0 %pack.3 = (bf16[2,2,512,128]{3,2,1,0:T(8,128)(2,1)}, bf16[2,2,512,128]{3,2,1,0:T(8,128)(2,1)}, bf16[2,2,512,128]{3,2,1,0:T(8,128)(2,1)}, bf16[2,2,512,128]{3,2,1...) custom-call(s32[97]{0:T(128)} %get-tuple-element.41.refs_0_.table_re, ...), custom_call_target="tpu_custom_call" | custom-call | bytes 5242880 | tf_op jit(solution)/shard_map/pack/pack/pallas_call | solution.py:136
  17.4 4.4 %collective-permute-start.3 = (bf16[2,2,512,128]{3,2,1,0:T(8,128)(2,1)}, bf16[2,2,512,128]{3,2,1,0:T(8,128)(2,1)}, u32[]{:S(2)}, u32[]{:S(2)}) collective-permute-start(bf16[2,2,512,128]{3,2,1,0:T(8,128)(2,1)} %get-tuple-element.51), channel_id=1, source_target_pairs={{0,120},{8,96},{16,104},{24,112},{32,24},{40,0},{48,8},{56,16},{64... | collective-permute-start | bytes 1572872 | tf_op jit(solution)/shard_map/documents/ppermute | solution.py:58
  25.1 2.9 %convolution_convert_fusion = bf16[640,512]{1,0:T(8,128)(2,1)S(1)} fusion(bf16[640,4096]{1,0:T(8,128)(2,1)S(1)} %bitcast.21, bf16[4096,512]{1,0:T(8,128)(2,1)S(1)} %copy-done.15), kind=kOutput, calls=%fused_computation.5 | convolution fusion | flops 2684682240 | bytes 10092544 | tf_op jit(solution)/shard_map/projections/dot_general | solution.py:399
  28.0 2.2 %convolution_convert_fusion.2 = bf16[640,128]{1,0:T(8,128)(2,1)} fusion(bf16[640,4096]{1,0:T(8,128)(2,1)S(1)} %bitcast.22, bf16[4096,128]{1,0:T(8,128)(2,1)S(1)} %copy-done), kind=kOutput, calls=%fused_computation.7 | convolution fusion | flops 671170560 | bytes 6455296 | tf_op jit(solution)/shard_map/projections/dot_general | solution.py:399
  31.9 11.2 %collective-permute-done.refs_6_ = bf16[6,2,512,128]{3,2,1,0:T(8,128)(2,1)} collective-permute-done((bf16[6,2,512,128]{3,2,1,0:T(8,128)(2,1)}, bf16[6,2,512,128]{3,2,1,0:T(8,128)(2,1)}, u32[]{:S(2)}, u32[]{:S(2)}) %collective-permute-start) | collective-permute-done | bytes 1572896 | tf_op jit(solution)/shard_map/documents/ppermute | solution.py:58
  43.1 4.6 %collective-permute-start.5 = (bf16[2,2,512,128]{3,2,1,0:T(8,128)(2,1)}, bf16[2,2,512,128]{3,2,1,0:T(8,128)(2,1)S(1)}, u32[]{:S(2)}, u32[]{:S(2)}) collective-permute-start(bf16[2,2,512,128]{3,2,1,0:T(8,128)(2,1)} %get-tuple-element.53), channel_id=1, source_target_pairs={{0,104},{8,112},{16,120},{24,96},{32,8},{40,16},{48,24},{56,0},{64... | collective-permute-start | bytes 1572872 | tf_op jit(solution)/shard_map/documents/ppermute | solution.py:58
  47.7 4.3 %convolution_convert_fusion.1 = bf16[640,128]{1,0:T(8,128)(2,1)S(1)} fusion(bf16[640,4096]{1,0:T(8,128)(2,1)} %bitcast.23, bf16[4096,128]{1,0:T(8,128)(2,1)} %param.15), kind=kOutput, calls=%fused_computation.6 | convolution fusion | flops 671170560 | bytes 6455296 | tf_op jit(solution)/shard_map/projections/dot_general | solution.py:399
  52.1 5.8 %attend.5 = (f32[2,4,320,128]{3,2,1,0:T(8,128)S(1)}, f32[2,4,320,128]{3,2,1,0:T(8,128)S(1)}, f32[2,4,320,128]{3,2,1,0:T(8,128)S(1)}) custom-call(s32[97]{0:T(128)S(1)} %copy-done.2, bf16[2,320,512]{2,1,0:T(8,128)(2,1)S(1)} %bitcast.16, s32[2,4,320,1]{3,2,1,0:T(8,128)S(1)} %reshape.47.refs_2_, s32[2,1,384]{2,1,0:T(1,128)S(1)} %reshape.43.refs_3_, ...), custom_call_target="tpu_custom_call" | custom-call | flops 335544320 | bytes 8650752 | tf_op jit(solution)/shard_map/attention/attend/pallas_call | solution.py:276
  57.9 9.6 %collective-permute-done.1.refs_7_ = bf16[6,2,512,128]{3,2,1,0:T(8,128)(2,1)} collective-permute-done((bf16[6,2,512,128]{3,2,1,0:T(8,128)(2,1)}, bf16[6,2,512,128]{3,2,1,0:T(8,128)(2,1)}, u32[]{:S(2)}, u32[]{:S(2)}) %collective-permute-start.1) | collective-permute-done | bytes 1572896 | tf_op jit(solution)/shard_map/documents/ppermute | solution.py:58
  67.6 2.6 %collective-permute-start.7 = (bf16[2,2,512,128]{3,2,1,0:T(8,128)(2,1)S(1)}, bf16[2,2,512,128]{3,2,1,0:T(8,128)(2,1)S(1)}, u32[]{:S(2)}, u32[]{:S(2)}) collective-permute-start(bf16[2,2,512,128]{3,2,1,0:T(8,128)(2,1)S(1)} %copy-done.18), channel_id=1, source_target_pairs={{0,96},{8,104},{16,112},{24,120},{32,0},{40,8},{48,16},{56,24},{64... | collective-permute-start | bytes 1572872 | tf_op jit(solution)/shard_map/documents/ppermute | solution.py:58
  72.7 8.9 %collective-permute-done.5.refs_9_ = bf16[2,2,512,128]{3,2,1,0:T(8,128)(2,1)S(1)} collective-permute-done((bf16[2,2,512,128]{3,2,1,0:T(8,128)(2,1)}, bf16[2,2,512,128]{3,2,1,0:T(8,128)(2,1)S(1)}, u32[]{:S(2)}, u32[]{:S(2)}) %collective-permute-start.5) | collective-permute-done | bytes 524320 | tf_op jit(solution)/shard_map/documents/ppermute | solution.py:58
  82.9 4.1 %attend.6 = (f32[2,4,320,128]{3,2,1,0:T(8,128)S(1)}, f32[2,4,320,128]{3,2,1,0:T(8,128)S(1)}, f32[2,4,320,128]{3,2,1,0:T(8,128)S(1)}) custom-call(s32[97]{0:T(128)S(1)} %copy-done.2, bf16[2,320,512]{2,1,0:T(8,128)(2,1)S(1)} %bitcast.17, s32[2,4,320,1]{3,2,1,0:T(8,128)S(1)} %reshape.47.refs_2_, ...), custom_call_target="tpu_custom_call", output_to_operand_aliasing={{0}: (3, {}), {1}: (4, {}), {2}: (5, {})} | custom-call | flops 671088640 | bytes 8912896 | tf_op jit(solution)/shard_map/attention/attend/pallas_call | solution.py:276
  88.9 6.1 %collective-permute-start.12 = (bf16[2,2,512,128]{3,2,1,0:T(8,128)(2,1)S(1)}, bf16[2,2,512,128]{3,2,1,0:T(8,128)(2,1)S(1)}, u32[]{:S(2)}, u32[]{:S(2)}) collective-permute-start(bf16[2,2,512,128]{3,2,1,0:T(8,128)(2,1)S(1)} %get-tuple-element.71), channel_id=1, source_target_pairs={{0,96},{8,104},{16,112},{24,120},{32,0},{40,8},{48,16},{56,24},{64... | collective-permute-start | bytes 1572872 | tf_op jit(solution)/shard_map/documents/ppermute | solution.py:58
  97.7 5.1 %attend.7 = (f32[2,4,320,128]{3,2,1,0:T(8,128)S(1)}, f32[2,4,320,128]{3,2,1,0:T(8,128)S(1)}, f32[2,4,320,128]{3,2,1,0:T(8,128)S(1)}) custom-call(s32[97]{0:T(128)S(1)} %copy-done.2, bf16[2,320,512]{2,1,0:T(8,128)(2,1)S(1)} %bitcast.18, s32[2,4,320,1]{3,2,1,0:T(8,128)S(1)} %reshape.47.refs_2_, ...), custom_call_target="tpu_custom_call", output_to_operand_aliasing={{0}: (3, {}), {1}: (4, {}), {2}: (5, {})} | custom-call | flops 1342177280 | bytes 9437184 | tf_op jit(solution)/shard_map/attention/attend/pallas_call | solution.py:276
  102.8 6.1 %attend.8 = (f32[2,4,320,128]{3,2,1,0:T(8,128)S(1)}, f32[2,4,320,128]{3,2,1,0:T(8,128)S(1)}, f32[2,4,320,128]{3,2,1,0:T(8,128)S(1)}) custom-call(s32[97]{0:T(128)S(1)} %copy-done.2, bf16[2,320,512]{2,1,0:T(8,128)(2,1)S(1)} %bitcast.19, s32[2,4,320,1]{3,2,1,0:T(8,128)S(1)} %reshape.47.refs_2_, ...), custom_call_target="tpu_custom_call", output_to_operand_aliasing={{0}: (3, {}), {1}: (4, {}), {2}: (5, {})} | custom-call | flops 1677721600 | bytes 9699328 | tf_op jit(solution)/shard_map/attention/attend/pallas_call | solution.py:276
  109.0 9.4 %attend.9 = (f32[2,4,320,128]{3,2,1,0:T(8,128)S(1)}, f32[2,4,320,128]{3,2,1,0:T(8,128)S(1)}, f32[2,4,320,128]{3,2,1,0:T(8,128)S(1)}, bf16[640,512]{1,0:T(8,128)(2,1)}) custom-call(s32[97]{0:T(128)S(1)} %copy-done.2, bf16[2,320,512]{2,1,0:T(8,128)(2,1)S(1)} %bitcast.20, ...), custom_call_target="tpu_custom_call", output_to_operand_aliasing={{0}: (3, {}), {1}: (4, {}), {2}: (5, {})} | custom-call | flops 1342177280 | bytes 9437184 | tf_op jit(solution)/shard_map/attention/attend/pallas_call | solution.py:276
  120.6 2.2 %collective-permute-start.17 = (bf16[640,512]{1,0:T(8,128)(2,1)}, bf16[640,512]{1,0:T(8,128)(2,1)S(1)}, u32[]{:S(2)}, u32[]{:S(2)}) collective-permute-start(bf16[640,512]{1,0:T(8,128)(2,1)} %get-tuple-element.74.refs_0_), channel_id=1, source_target_pairs={{0,6},{1,7},{2,0},{3,1},{4,2},{5,3},{6,4},{7,5},{8,14},{9,15},{10,... | collective-permute-start | bytes 1966088 | tf_op jit(solution)/shard_map/output/ppermute | solution.py:354
  122.8 7.3 %collective-permute-start.19 = (bf16[640,512]{1,0:T(8,128)(2,1)}, bf16[640,512]{1,0:T(8,128)(2,1)S(1)}, u32[]{:S(2)}, u32[]{:S(2)}) collective-permute-start(bf16[640,512]{1,0:T(8,128)(2,1)} %get-tuple-element.74.refs_0_), channel_id=1, source_target_pairs={{0,1},{1,0},{2,3},{3,2},{4,5},{5,4},{6,7},{7,6},{8,9},{9,8},{10,11... | collective-permute-start | bytes 1966088 | tf_op jit(solution)/shard_map/output/ppermute | solution.py:358
  130.9 7.9 %collective-permute-start.20 = (bf16[640,512]{1,0:T(8,128)(2,1)S(1)}, bf16[640,512]{1,0:T(8,128)(2,1)}, u32[]{:S(2)}, u32[]{:S(2)}) collective-permute-start(bf16[640,512]{1,0:T(8,128)(2,1)S(1)} %collective-permute-done.15.refs_2_), channel_id=1, source_target_pairs={{0,1},{1,0},{2,3},{3,2},{4,5},{5,4},{6,7},{7,6},{8,9},{9,8},{10,11... | collective-permute-start | bytes 1966088 | tf_op jit(solution)/shard_map/output/ppermute | solution.py:358
  143.6 5.9 %project.2.refs_4_ = f32[640,512]{1,0:T(8,128)} custom-call(s32[8]{0:T(128)} %pad_add_fusion.place_ref, bf16[4096,512]{1,0:T(8,128)(2,1)} %w_ref.3, bf16[640,512]{1,0:T(8,128)(2,1)} %get-tuple-element.74.refs_0_, bf16[640,512]{1,0:T(8,128)(2,1)} %copy-done.7, bf16[640,512]{1,0:T(8,128)(2,1)} %copy-done.5, bf16[640,512]{1,0:T(8,128)(2,1)} %copy-done.6, ...), custom_call_target="tpu_custom_call" | custom-call | flops 2013265920 | bytes 6291456 | tf_op jit(solution)/shard_map/output/project/pallas_call | solution.py:334
  153.5 4.4 %project.3 = bf16[640,512]{1,0:T(8,128)(2,1)} custom-call(s32[8]{0:T(128)} %pad_add_fusion.place_ref, bf16[4096,512]{1,0:T(8,128)(2,1)} %w_ref.3, bf16[320,512]{1,0:T(8,128)(2,1)} %copy-done.8, bf16[320,512]{1,0:T(8,128)(2,1)} %copy-done.9, bf16[320,512]{1,0:T(8,128)(2,1)} %copy-done.10, bf16[320,512]{1,0:T(8,128)(2,1)} %copy-done.11, f32[640,512]{1,0:T(8,128)} %project.2.refs_4_), custom_call_target="tpu_custom_call" | custom-call | flops 671088640 | bytes 2097152 | tf_op jit(solution)/shard_map/output/project/pallas_call | solution.py:334
  (97 shorter events, 27.1 us)
Async XLA Ops:
  6.7 36.4 %collective-permute-start = (bf16[6,2,512,128]{3,2,1,0:T(8,128)(2,1)}, bf16[6,2,512,128]{3,2,1,0:T(8,128)(2,1)}, u32[]{:S(2)}, u32[]{:S(2)}) collective-permute-start(bf16[6,2,512,128]{3,2,1,0:T(8,128)(2,1)} %get-tuple-element.45), channel_id=1, source_target_pairs={{0,64},{8,72},{16,80},{24,88},{32,96},{40,104},{48,112},{56,120},{... | collective-permute-start | bytes 4718600 | tf_op jit(solution)/shard_map/documents/ppermute | solution.py:58
  9.6 57.9 %collective-permute-start.1 = (bf16[6,2,512,128]{3,2,1,0:T(8,128)(2,1)}, bf16[6,2,512,128]{3,2,1,0:T(8,128)(2,1)}, u32[]{:S(2)}, u32[]{:S(2)}) collective-permute-start(bf16[6,2,512,128]{3,2,1,0:T(8,128)(2,1)} %get-tuple-element.46), channel_id=1, source_target_pairs={{0,16},{8,24},{16,0},{24,8},{32,48},{40,56},{48,32},{56,40},{64,80... | collective-permute-start | bytes 4718600 | tf_op jit(solution)/shard_map/documents/ppermute | solution.py:58
  17.0 50.6 %collective-permute-start.2 = (bf16[2,2,512,128]{3,2,1,0:T(8,128)(2,1)}, bf16[2,2,512,128]{3,2,1,0:T(8,128)(2,1)S(1)}, u32[]{:S(2)}, u32[]{:S(2)}) collective-permute-start(bf16[2,2,512,128]{3,2,1,0:T(8,128)(2,1)} %get-tuple-element.50), channel_id=1, source_target_pairs={{0,40},{8,48},{16,56},{24,32},{32,72},{40,80},{48,88},{56,64},{64,... | collective-permute-start | bytes 1572872 | tf_op jit(solution)/shard_map/documents/ppermute | solution.py:58
  17.4 50.2 %collective-permute-start.3 = (bf16[2,2,512,128]{3,2,1,0:T(8,128)(2,1)}, bf16[2,2,512,128]{3,2,1,0:T(8,128)(2,1)}, u32[]{:S(2)}, u32[]{:S(2)}) collective-permute-start(bf16[2,2,512,128]{3,2,1,0:T(8,128)(2,1)} %get-tuple-element.51), channel_id=1, source_target_pairs={{0,120},{8,96},{16,104},{24,112},{32,24},{40,0},{48,8},{56,16},{64... | collective-permute-start | bytes 1572872 | tf_op jit(solution)/shard_map/documents/ppermute | solution.py:58
  21.8 48.5 %collective-permute-start.4 = (bf16[2,2,512,128]{3,2,1,0:T(8,128)(2,1)}, bf16[2,2,512,128]{3,2,1,0:T(8,128)(2,1)}, u32[]{:S(2)}, u32[]{:S(2)}) collective-permute-start(bf16[2,2,512,128]{3,2,1,0:T(8,128)(2,1)} %get-tuple-element.52), channel_id=1, source_target_pairs={{0,56},{8,32},{16,40},{24,48},{32,88},{40,64},{48,72},{56,80},{64,... | collective-permute-start | bytes 1572872 | tf_op jit(solution)/shard_map/documents/ppermute | solution.py:58
  43.1 38.5 %collective-permute-start.5 = (bf16[2,2,512,128]{3,2,1,0:T(8,128)(2,1)}, bf16[2,2,512,128]{3,2,1,0:T(8,128)(2,1)S(1)}, u32[]{:S(2)}, u32[]{:S(2)}) collective-permute-start(bf16[2,2,512,128]{3,2,1,0:T(8,128)(2,1)} %get-tuple-element.53), channel_id=1, source_target_pairs={{0,104},{8,112},{16,120},{24,96},{32,8},{40,16},{48,24},{56,0},{64... | collective-permute-start | bytes 1572872 | tf_op jit(solution)/shard_map/documents/ppermute | solution.py:58
  67.5 19.5 %collective-permute-start.10 = (bf16[2,2,512,128]{3,2,1,0:T(8,128)(2,1)S(1)}, bf16[2,2,512,128]{3,2,1,0:T(8,128)(2,1)S(1)}, u32[]{:S(2)}, u32[]{:S(2)}) collective-permute-start(bf16[2,2,512,128]{3,2,1,0:T(8,128)(2,1)S(1)} %copy-done.20), channel_id=1, source_target_pairs={{0,80},{8,88},{16,64},{24,72},{32,112},{40,120},{48,96},{56,104},{... | collective-permute-start | bytes 1572872 | tf_op jit(solution)/shard_map/documents/ppermute | solution.py:58
  67.5 21.4 %collective-permute-start.6 = (bf16[2,2,512,128]{3,2,1,0:T(8,128)(2,1)S(1)}, bf16[2,2,512,128]{3,2,1,0:T(8,128)(2,1)S(1)}, u32[]{:S(2)}, u32[]{:S(2)}) collective-permute-start(bf16[2,2,512,128]{3,2,1,0:T(8,128)(2,1)S(1)} %copy-done.19), channel_id=1, source_target_pairs={{0,32},{8,40},{16,48},{24,56},{32,64},{40,72},{48,80},{56,88},{64,... | collective-permute-start | bytes 1572872 | tf_op jit(solution)/shard_map/documents/ppermute | solution.py:58
  67.6 27.4 %collective-permute-start.7 = (bf16[2,2,512,128]{3,2,1,0:T(8,128)(2,1)S(1)}, bf16[2,2,512,128]{3,2,1,0:T(8,128)(2,1)S(1)}, u32[]{:S(2)}, u32[]{:S(2)}) collective-permute-start(bf16[2,2,512,128]{3,2,1,0:T(8,128)(2,1)S(1)} %copy-done.18), channel_id=1, source_target_pairs={{0,96},{8,104},{16,112},{24,120},{32,0},{40,8},{48,16},{56,24},{64... | collective-permute-start | bytes 1572872 | tf_op jit(solution)/shard_map/documents/ppermute | solution.py:58
  70.3 26.8 %collective-permute-start.8 = (bf16[2,2,512,128]{3,2,1,0:T(8,128)(2,1)S(1)}, bf16[2,2,512,128]{3,2,1,0:T(8,128)(2,1)S(1)}, u32[]{:S(2)}, u32[]{:S(2)}) collective-permute-start(bf16[2,2,512,128]{3,2,1,0:T(8,128)(2,1)S(1)} %copy-done.17), channel_id=1, source_target_pairs={{0,8},{8,16},{16,24},{24,0},{32,40},{40,48},{48,56},{56,32},{64,72... | collective-permute-start | bytes 1572872 | tf_op jit(solution)/shard_map/documents/ppermute | solution.py:58
  81.6 21.2 %collective-permute-start.9 = (bf16[2,2,512,128]{3,2,1,0:T(8,128)(2,1)S(1)}, bf16[2,2,512,128]{3,2,1,0:T(8,128)(2,1)S(1)}, u32[]{:S(2)}, u32[]{:S(2)}) collective-permute-start(bf16[2,2,512,128]{3,2,1,0:T(8,128)(2,1)S(1)} %copy-done.16), channel_id=1, source_target_pairs={{0,24},{8,0},{16,8},{24,16},{32,56},{40,32},{48,40},{56,48},{64,88... | collective-permute-start | bytes 1572872 | tf_op jit(solution)/shard_map/documents/ppermute | solution.py:58
  87.0 21.9 %collective-permute-start.11 = (bf16[2,2,512,128]{3,2,1,0:T(8,128)(2,1)S(1)}, bf16[2,2,512,128]{3,2,1,0:T(8,128)(2,1)S(1)}, u32[]{:S(2)}, u32[]{:S(2)}) collective-permute-start(bf16[2,2,512,128]{3,2,1,0:T(8,128)(2,1)S(1)} %get-tuple-element.70), channel_id=1, source_target_pairs={{0,32},{8,40},{16,48},{24,56},{32,64},{40,72},{48,80},{56,88},{64,... | collective-permute-start | bytes 1572872 | tf_op jit(solution)/shard_map/documents/ppermute | solution.py:58
  88.9 20.0 %collective-permute-start.12 = (bf16[2,2,512,128]{3,2,1,0:T(8,128)(2,1)S(1)}, bf16[2,2,512,128]{3,2,1,0:T(8,128)(2,1)S(1)}, u32[]{:S(2)}, u32[]{:S(2)}) collective-permute-start(bf16[2,2,512,128]{3,2,1,0:T(8,128)(2,1)S(1)} %get-tuple-element.71), channel_id=1, source_target_pairs={{0,96},{8,104},{16,112},{24,120},{32,0},{40,8},{48,16},{56,24},{64... | collective-permute-start | bytes 1572872 | tf_op jit(solution)/shard_map/documents/ppermute | solution.py:58
  95.0 13.9 %collective-permute-start.13 = (bf16[2,2,512,128]{3,2,1,0:T(8,128)(2,1)S(1)}, bf16[2,2,512,128]{3,2,1,0:T(8,128)(2,1)S(1)}, u32[]{:S(2)}, u32[]{:S(2)}) collective-permute-start(bf16[2,2,512,128]{3,2,1,0:T(8,128)(2,1)S(1)} %get-tuple-element.72), channel_id=1, source_target_pairs={{0,8},{8,16},{16,24},{24,0},{32,40},{40,48},{48,56},{56,32},{64,72... | collective-permute-start | bytes 1572872 | tf_op jit(solution)/shard_map/documents/ppermute | solution.py:58
  97.1 11.9 %collective-permute-start.14 = (bf16[2,2,512,128]{3,2,1,0:T(8,128)(2,1)S(1)}, bf16[2,2,512,128]{3,2,1,0:T(8,128)(2,1)S(1)}, u32[]{:S(2)}, u32[]{:S(2)}) collective-permute-start(bf16[2,2,512,128]{3,2,1,0:T(8,128)(2,1)S(1)} %get-tuple-element.73), channel_id=1, source_target_pairs={{0,24},{8,0},{16,8},{24,16},{32,56},{40,32},{48,40},{56,48},{64,88... | collective-permute-start | bytes 1572872 | tf_op jit(solution)/shard_map/documents/ppermute | solution.py:58
  118.4 12.5 %collective-permute-start.15 = (bf16[640,512]{1,0:T(8,128)(2,1)}, bf16[640,512]{1,0:T(8,128)(2,1)S(1)}, u32[]{:S(2)}, u32[]{:S(2)}) collective-permute-start(bf16[640,512]{1,0:T(8,128)(2,1)} %get-tuple-element.74.refs_0_), channel_id=1, source_target_pairs={{0,2},{1,3},{2,4},{3,5},{4,6},{5,7},{6,0},{7,1},{8,10},{9,11},{10,... | collective-permute-start | bytes 1966088 | tf_op jit(solution)/shard_map/output/ppermute | solution.py:354
  120.6 18.2 %collective-permute-start.17 = (bf16[640,512]{1,0:T(8,128)(2,1)}, bf16[640,512]{1,0:T(8,128)(2,1)S(1)}, u32[]{:S(2)}, u32[]{:S(2)}) collective-permute-start(bf16[640,512]{1,0:T(8,128)(2,1)} %get-tuple-element.74.refs_0_), channel_id=1, source_target_pairs={{0,6},{1,7},{2,0},{3,1},{4,2},{5,3},{6,4},{7,5},{8,14},{9,15},{10,... | collective-permute-start | bytes 1966088 | tf_op jit(solution)/shard_map/output/ppermute | solution.py:354
  122.8 19.9 %collective-permute-start.19 = (bf16[640,512]{1,0:T(8,128)(2,1)}, bf16[640,512]{1,0:T(8,128)(2,1)S(1)}, u32[]{:S(2)}, u32[]{:S(2)}) collective-permute-start(bf16[640,512]{1,0:T(8,128)(2,1)} %get-tuple-element.74.refs_0_), channel_id=1, source_target_pairs={{0,1},{1,0},{2,3},{3,2},{4,5},{5,4},{6,7},{7,6},{8,9},{9,8},{10,11... | collective-permute-start | bytes 1966088 | tf_op jit(solution)/shard_map/output/ppermute | solution.py:358
  130.9 11.8 %collective-permute-start.20 = (bf16[640,512]{1,0:T(8,128)(2,1)S(1)}, bf16[640,512]{1,0:T(8,128)(2,1)}, u32[]{:S(2)}, u32[]{:S(2)}) collective-permute-start(bf16[640,512]{1,0:T(8,128)(2,1)S(1)} %collective-permute-done.15.refs_2_), channel_id=1, source_target_pairs={{0,1},{1,0},{2,3},{3,2},{4,5},{5,4},{6,7},{7,6},{8,9},{9,8},{10,11... | collective-permute-start | bytes 1966088 | tf_op jit(solution)/shard_map/output/ppermute | solution.py:358
  138.8 3.9 %collective-permute-start.21 = (bf16[640,512]{1,0:T(8,128)(2,1)S(1)}, bf16[640,512]{1,0:T(8,128)(2,1)}, u32[]{:S(2)}, u32[]{:S(2)}) collective-permute-start(bf16[640,512]{1,0:T(8,128)(2,1)S(1)} %collective-permute-done.17.refs_3_), channel_id=1, source_target_pairs={{0,1},{1,0},{2,3},{3,2},{4,5},{5,4},{6,7},{7,6},{8,9},{9,8},{10,11... | collective-permute-start | bytes 1966088 | tf_op jit(solution)/shard_map/output/ppermute | solution.py:358
  139.2 10.5 %collective-permute-start.16 = (bf16[320,512]{1,0:T(8,128)(2,1)S(1)}, bf16[320,512]{1,0:T(8,128)(2,1)S(1)}, u32[]{:S(2)}, u32[]{:S(2)}) collective-permute-start(bf16[320,512]{1,0:T(8,128)(2,1)S(1)} %slice.28), channel_id=1, source_target_pairs={{0,2},{1,3},{2,4},{3,5},{4,6},{5,7},{6,0},{7,1},{8,10},{9,11},{10,... | collective-permute-start | bytes 983048 | tf_op jit(solution)/shard_map/output/ppermute | solution.py:354
  140.5 9.2 %collective-permute-start.18 = (bf16[320,512]{1,0:T(8,128)(2,1)S(1)}, bf16[320,512]{1,0:T(8,128)(2,1)S(1)}, u32[]{:S(2)}, u32[]{:S(2)}) collective-permute-start(bf16[320,512]{1,0:T(8,128)(2,1)S(1)} %slice.29), channel_id=1, source_target_pairs={{0,6},{1,7},{2,0},{3,1},{4,2},{5,3},{6,4},{7,5},{8,14},{9,15},{10,... | collective-permute-start | bytes 983048 | tf_op jit(solution)/shard_map/output/ppermute | solution.py:354
  149.7 2.3 %collective-permute-start.22 = (bf16[320,512]{1,0:T(8,128)(2,1)S(1)}, bf16[320,512]{1,0:T(8,128)(2,1)S(1)}, u32[]{:S(2)}, u32[]{:S(2)}) collective-permute-start(bf16[320,512]{1,0:T(8,128)(2,1)S(1)} %collective-permute-done.16.refs_0_), channel_id=1, source_target_pairs={{0,1},{1,0},{2,3},{3,2},{4,5},{5,4},{6,7},{7,6},{8,9},{9,8},{10,11... | collective-permute-start | bytes 983048 | tf_op jit(solution)/shard_map/output/ppermute | solution.py:358
  150.7 1.7 %collective-permute-start.23 = (bf16[320,512]{1,0:T(8,128)(2,1)S(1)}, bf16[320,512]{1,0:T(8,128)(2,1)S(1)}, u32[]{:S(2)}, u32[]{:S(2)}) collective-permute-start(bf16[320,512]{1,0:T(8,128)(2,1)S(1)} %collective-permute-done.18.refs_1_), channel_id=1, source_target_pairs={{0,1},{1,0},{2,3},{3,2},{4,5},{5,4},{6,7},{7,6},{8,9},{9,8},{10,11... | collective-permute-start | bytes 983048 | tf_op jit(solution)/shard_map/output/ppermute | solution.py:358
  (21 other events, 244.6 us)

commit v4 on v3

--- a/solution.py
+++ b/solution.py
@@ -41,7 +41,7 @@
 JOINED = []
 ROOM = 24 << 20
 ALL_ROOM = 56 << 20
-PROJECT_ROOM = 56 << 20
+PROJECT_ROOM = 24 << 20
 
 ANY = pl.BlockSpec(memory_space=pl.ANY)
 HBM = pl.BlockSpec(memory_space=pltpu.HBM)
@@ -95,6 +95,8 @@
 def first_pack_kernel(me_ref, home_ref, ids_ref, len_ref, cache_ref, *refs):
     out_refs, (table_ref, *scratch) = refs[: len(EARLY)], refs[len(EARLY) :]
     me = me_ref[0]
+
+    x, y = me // SIDE, me % SIDE
 
     def outgoing(g, carry):
         one, two = jnp.int32(-1), jnp.int32(-1)
@@ -107,10 +109,13 @@
         table_ref[CHOSEN + g * CAP + 1] = jnp.where(two >= 0, one, -1)
         return carry
 
-    lax.fori_loop(0, GROUPS, outgoing, 0)
+    for block in EARLY:
+        for dx, dy in block:
+            outgoing((x + dx) % SIDE * SIDE + (y + dy) % SIDE, 0)
     table_ref[CHOSEN + GROUPS * CAP] = me
 
-    def incoming():
+    def rest():
+        lax.fori_loop(0, GROUPS, outgoing, 0)
         for at in range(GROUPS * CAP):
             table_ref[at] = jnp.int32(-1)
         for i in range(SLOTS):
@@ -121,7 +126,7 @@
             table_ref[GROUPS * CAP + i] = location % STORED
             table_ref[GROUPS * CAP + SLOTS + i] = len_ref[doc]
 
-    copy_chosen(table_ref, cache_ref, EARLY, out_refs, *scratch, incoming)
+    copy_chosen(table_ref, cache_ref, EARLY, out_refs, *scratch, rest)
 
 
 def second_pack_kernel(table_ref, cache_ref, *refs):
@@ -298,33 +303,22 @@
     parts, refs = refs[: len(spans)], refs[len(spans) :]
     if last:
         before_ref, *refs = refs
-    out_ref, w, held, w_sem, part_sem = refs
+    out_ref = refs[0]
     width = GROUP * HD
-    order = list(dict.fromkeys(n for n, _, _ in spans))
-
-    def weights(slot):
-        rows = pl.ds(pl.multiple_of(place_ref[order[slot]] * width, width), width)
-        return pltpu.make_async_copy(w_ref.at[rows], w.at[slot], w_sem.at[slot])
-
-    def piece(at):
-        n, lo, hi = spans[at]
-        target = held.at[order.index(n), lo:hi]
-        return pltpu.make_async_copy(parts[at], target, part_sem.at[at])
-
-    for slot, n in enumerate(order):
-        weights(slot).start()
-        for at in range(len(spans)):
-            if spans[at][0] == n:
-                piece(at).start()
-    total = before_ref[...] if last else None
-    for slot, n in enumerate(order):
-        weights(slot).wait()
-        for at in range(len(spans)):
-            if spans[at][0] == n:
-                piece(at).wait()
-        term = jnp.dot(held[slot], w[slot], preferred_element_type=jnp.float32)
-        total = term if total is None else total + term
-    out_ref[...] = total.astype(out_ref.dtype)
+    rows = out_ref.shape[0]
+    half = rows // 2
+    for at in range(0, rows, half):
+        total = before_ref[at : at + half] if last else None
+        for part, (n, lo, hi) in zip(parts, spans):
+            if lo <= at < hi:
+                block = pl.ds(pl.multiple_of(place_ref[n] * width, width), width)
+                term = jnp.dot(
+                    part[at - lo : at - lo + half],
+                    w_ref[block, :],
+                    preferred_element_type=jnp.float32,
+                )
+                total = term if total is None else total + term
+        out_ref[at : at + half] = total.astype(out_ref.dtype)
 
 
 def project(place, pieces, w_out, before):
@@ -334,14 +328,8 @@
     return pl.pallas_call(
         functools.partial(project_kernel, spans, last),
         out_shape=jax.ShapeDtypeStruct((rows, columns), jnp.bfloat16 if last else jnp.float32),
-        in_specs=[SMEM, HBM] + [ANY] * len(parts) + [VMEM] * last,
+        in_specs=[SMEM] + [VMEM] * (len(parts) + 1 + last),
         out_specs=VMEM,
-        scratch_shapes=[
-            pltpu.VMEM((blocks, GROUP * HD, columns), jnp.bfloat16),
-            pltpu.VMEM((blocks, rows, GROUP * HD), jnp.bfloat16),
-            pltpu.SemaphoreType.DMA((blocks,)),
-            pltpu.SemaphoreType.DMA((len(parts),)),
-        ],
         compiler_params=pltpu.CompilerParams(vmem_limit_bytes=PROJECT_ROOM),
         cost_estimate=pl.CostEstimate(
             flops=2 * rows * blocks * 512 * 512, bytes_accessed=blocks << 20, transcendentals=0

time: 159 us -> 155 us (0.975)
  starting transfers between devices: 52.9 us -> 65.5 us
  waiting for transfers between devices: 33.8 us -> 24.5 us
  Pallas kernels: 49.9 us -> 43.9 us
    ppermute x15, starting transfers between devices: 29 us -> 40.3 us  [shift(): return lax.ppermute(block, 'grp', pairs)]
    ppermute x15, waiting for transfers between devices: 31.1 us -> 21.3 us  [shift(): return lax.ppermute(block, 'grp', pairs)]
    pallas_call x2, Pallas kernels: 10.3 us -> 6.06 us  [project(): pl.pallas_call(functools.partial(project_kernel, spans, last), out_shape=...]
    pallas_call x2, Pallas kernels: 9.1 us -> 7.46 us  [pack(): pl.pallas_call(kernel, out_shape=[jax.ShapeDtypeStruct(s, jnp.bfloat16) f...]
    unnamed x43 -> x33, local copies, waits for them, and re-layouts: 2.99 us -> 3.35 us
  transfers between devices with their start and end apart: 24 -> 24, of which waited for: 8 -> 8; matrix products, arithmetic and copies ran while one was open for 11% -> 11% of each run, Pallas kernels for 20% -> 19%
where the time goes in v4:
time: 155 us
  starting transfers between devices  65.5 us (42%)
  Pallas kernels  43.9 us (28%)
  waiting for transfers between devices  24.5 us (16%)
  matrix products  9.35 us (6%)
  local copies, waits for them, and re-layouts  8.26 us (5%)
  other arithmetic  3.18 us (2%)
    ppermute x15, starting transfers between devices, shift(): return lax.ppermute(block, 'grp', pairs)  40.3 us
    pallas_call x5, Pallas kernels, attend(): pl.pallas_call(functools.partial(attend_kernel, shifts, count, first, las...  30.3 us
    ppermute x15, waiting for transfers between devices, shift(): return lax.ppermute(block, 'grp', pairs)  21.3 us
    ppermute x5, starting transfers between devices, other_core(): return lax.ppermute(block, 'tp', [(i, i ^ 1) for i in range(KVH)])  18.2 us
    dot_general x3, matrix products, dot(): out = jnp.dot(normed_rows, w, preferred_element_type=jnp.float32)  9.35 us
    pallas_call x2, Pallas kernels, pack(): pl.pallas_call(kernel, out_shape=[jax.ShapeDtypeStruct(s, jnp.bfloat16) f...  7.46 us
    ppermute x4, starting transfers between devices, ring(): lax.ppermute(block, 'tp', [(i, (i + 2 * by) % KVH) for i in range(KVH)])  7.09 us
    pallas_call x2, Pallas kernels, project(): pl.pallas_call(functools.partial(project_kernel, spans, last), out_shape=...  6.06 us
  transfers between devices with their start and end apart: 24, of which 8 were waited for; matrix products, arithmetic and copies ran while one was open for 11% of the time, Pallas kernels for 19%

profile of v4, /device:TPU:1, one launch (start us, length us, event | category | flops | bytes accessed | tf_op | source)
XLA Modules:
  0.0 155.1 jit_solution(16578499594136493287)
XLA Ops:
  1.5 4.3 %pack.2 = (bf16[6,2,512,128]{3,2,1,0:T(8,128)(2,1)}, bf16[6,2,512,128]{3,2,1,0:T(8,128)(2,1)}, s32[97]{0:T(128)}) custom-call(s32[1]{0:T(128)} %bitcast.4.me_ref, s32[256]{0:T(256)} %home_ref.1, s32[256]{0:T(256)} %reshape.39.ids_ref, s32[256]{0:T(256)} %len_ref.1, bf16[16,2,512,128]{3,2,1,0:T(8,128)(2,1)} %cache_ref.3), custom_call_target="tpu_custom_call" | custom-call | bytes 5242880 | tf_op jit(solution)/shard_map/pack/pack/pallas_call | solution.py:141
  5.8 3.8 %collective-permute-start = (bf16[6,2,512,128]{3,2,1,0:T(8,128)(2,1)}, bf16[6,2,512,128]{3,2,1,0:T(8,128)(2,1)}, u32[]{:S(2)}, u32[]{:S(2)}) collective-permute-start(bf16[6,2,512,128]{3,2,1,0:T(8,128)(2,1)} %get-tuple-element.45), channel_id=1, source_target_pairs={{0,64},{8,72},{16,80},{24,88},{32,96},{40,104},{48,112},{56,120},{... | collective-permute-start | bytes 4718600 | tf_op jit(solution)/shard_map/documents/ppermute | solution.py:58
  9.6 2.8 %collective-permute-start.1 = (bf16[6,2,512,128]{3,2,1,0:T(8,128)(2,1)}, bf16[6,2,512,128]{3,2,1,0:T(8,128)(2,1)}, u32[]{:S(2)}, u32[]{:S(2)}) collective-permute-start(bf16[6,2,512,128]{3,2,1,0:T(8,128)(2,1)} %get-tuple-element.46), channel_id=1, source_target_pairs={{0,16},{8,24},{16,0},{24,8},{32,48},{40,56},{48,32},{56,40},{64,80... | collective-permute-start | bytes 4718600 | tf_op jit(solution)/shard_map/documents/ppermute | solution.py:58
  12.4 3.2 %pack.3 = (bf16[2,2,512,128]{3,2,1,0:T(8,128)(2,1)}, bf16[2,2,512,128]{3,2,1,0:T(8,128)(2,1)}, bf16[2,2,512,128]{3,2,1,0:T(8,128)(2,1)}, bf16[2,2,512,128]{3,2,1...) custom-call(s32[97]{0:T(128)} %get-tuple-element.41.refs_0_.table_re, ...), custom_call_target="tpu_custom_call" | custom-call | bytes 5242880 | tf_op jit(solution)/shard_map/pack/pack/pallas_call | solution.py:141
  17.4 3.0 %collective-permute-start.3 = (bf16[2,2,512,128]{3,2,1,0:T(8,128)(2,1)}, bf16[2,2,512,128]{3,2,1,0:T(8,128)(2,1)}, u32[]{:S(2)}, u32[]{:S(2)}) collective-permute-start(bf16[2,2,512,128]{3,2,1,0:T(8,128)(2,1)} %get-tuple-element.51), channel_id=1, source_target_pairs={{0,120},{8,96},{16,104},{24,112},{32,24},{40,0},{48,8},{56,16},{64... | collective-permute-start | bytes 1572872 | tf_op jit(solution)/shard_map/documents/ppermute | solution.py:58
  23.7 2.9 %convolution_convert_fusion = bf16[640,512]{1,0:T(8,128)(2,1)S(1)} fusion(bf16[640,4096]{1,0:T(8,128)(2,1)S(1)} %bitcast.21, bf16[4096,512]{1,0:T(8,128)(2,1)S(1)} %copy-done.10), kind=kOutput, calls=%fused_computation.5 | convolution fusion | flops 2684682240 | bytes 10092544 | tf_op jit(solution)/shard_map/projections/dot_general | solution.py:387
  30.5 13.2 %collective-permute-done.refs_6_ = bf16[6,2,512,128]{3,2,1,0:T(8,128)(2,1)} collective-permute-done((bf16[6,2,512,128]{3,2,1,0:T(8,128)(2,1)}, bf16[6,2,512,128]{3,2,1,0:T(8,128)(2,1)}, u32[]{:S(2)}, u32[]{:S(2)}) %collective-permute-start) | collective-permute-done | bytes 1572896 | tf_op jit(solution)/shard_map/documents/ppermute | solution.py:58
  43.7 3.8 %collective-permute-start.5 = (bf16[2,2,512,128]{3,2,1,0:T(8,128)(2,1)}, bf16[2,2,512,128]{3,2,1,0:T(8,128)(2,1)S(1)}, u32[]{:S(2)}, u32[]{:S(2)}) collective-permute-start(bf16[2,2,512,128]{3,2,1,0:T(8,128)(2,1)} %get-tuple-element.53), channel_id=1, source_target_pairs={{0,104},{8,112},{16,120},{24,96},{32,8},{40,16},{48,24},{56,0},{64... | collective-permute-start | bytes 1572872 | tf_op jit(solution)/shard_map/documents/ppermute | solution.py:58
  47.5 4.3 %convolution_convert_fusion.1 = bf16[640,128]{1,0:T(8,128)(2,1)S(1)} fusion(bf16[640,4096]{1,0:T(8,128)(2,1)} %bitcast.23, bf16[4096,128]{1,0:T(8,128)(2,1)} %param.15), kind=kOutput, calls=%fused_computation.6 | convolution fusion | flops 671170560 | bytes 6455296 | tf_op jit(solution)/shard_map/projections/dot_general | solution.py:387
  52.0 5.2 %attend.5 = (f32[2,4,320,128]{3,2,1,0:T(8,128)S(1)}, f32[2,4,320,128]{3,2,1,0:T(8,128)S(1)}, f32[2,4,320,128]{3,2,1,0:T(8,128)S(1)}) custom-call(s32[97]{0:T(128)S(1)} %copy-done.4, bf16[2,320,512]{2,1,0:T(8,128)(2,1)S(1)} %bitcast.16, s32[2,4,320,1]{3,2,1,0:T(8,128)S(1)} %reshape.47.refs_2_, s32[2,1,384]{2,1,0:T(1,128)S(1)} %reshape.43.refs_3_, ...), custom_call_target="tpu_custom_call" | custom-call | flops 335544320 | bytes 8650752 | tf_op jit(solution)/shard_map/attention/attend/pallas_call | solution.py:281
  57.6 3.5 %collective-permute-start.10 = (bf16[2,2,512,128]{3,2,1,0:T(8,128)(2,1)S(1)}, bf16[2,2,512,128]{3,2,1,0:T(8,128)(2,1)S(1)}, u32[]{:S(2)}, u32[]{:S(2)}) collective-permute-start(bf16[2,2,512,128]{3,2,1,0:T(8,128)(2,1)S(1)} %copy-done.15), channel_id=1, source_target_pairs={{0,80},{8,88},{16,64},{24,72},{32,112},{40,120},{48,96},{56,104},{... | collective-permute-start | bytes 1572872 | tf_op jit(solution)/shard_map/documents/ppermute | solution.py:58
  63.8 5.3 %collective-permute-done.4.refs_8_ = bf16[2,2,512,128]{3,2,1,0:T(8,128)(2,1)} collective-permute-done((bf16[2,2,512,128]{3,2,1,0:T(8,128)(2,1)}, bf16[2,2,512,128]{3,2,1,0:T(8,128)(2,1)}, u32[]{:S(2)}, u32[]{:S(2)}) %collective-permute-start.4) | collective-permute-done | bytes 524320 | tf_op jit(solution)/shard_map/documents/ppermute | solution.py:58
  69.1 2.7 %collective-permute-start.8 = (bf16[2,2,512,128]{3,2,1,0:T(8,128)(2,1)S(1)}, bf16[2,2,512,128]{3,2,1,0:T(8,128)(2,1)S(1)}, u32[]{:S(2)}, u32[]{:S(2)}) collective-permute-start(bf16[2,2,512,128]{3,2,1,0:T(8,128)(2,1)S(1)} %copy-done.12), channel_id=1, source_target_pairs={{0,8},{8,16},{16,24},{24,0},{32,40},{40,48},{48,56},{56,32},{64,72... | collective-permute-start | bytes 1572872 | tf_op jit(solution)/shard_map/documents/ppermute | solution.py:58
  77.2 3.8 %attend.6 = (f32[2,4,320,128]{3,2,1,0:T(8,128)S(1)}, f32[2,4,320,128]{3,2,1,0:T(8,128)S(1)}, f32[2,4,320,128]{3,2,1,0:T(8,128)S(1)}) custom-call(s32[97]{0:T(128)S(1)} %copy-done.4, bf16[2,320,512]{2,1,0:T(8,128)(2,1)S(1)} %bitcast.17, s32[2,4,320,1]{3,2,1,0:T(8,128)S(1)} %reshape.47.refs_2_, ...), custom_call_target="tpu_custom_call", output_to_operand_aliasing={{0}: (3, {}), {1}: (4, {}), {2}: (5, {})} | custom-call | flops 671088640 | bytes 8912896 | tf_op jit(solution)/shard_map/attention/attend/pallas_call | solution.py:281
  81.0 2.2 %collective-permute-start.11 = (bf16[2,2,512,128]{3,2,1,0:T(8,128)(2,1)S(1)}, bf16[2,2,512,128]{3,2,1,0:T(8,128)(2,1)S(1)}, u32[]{:S(2)}, u32[]{:S(2)}) collective-permute-start(bf16[2,2,512,128]{3,2,1,0:T(8,128)(2,1)S(1)} %get-tuple-element.70), channel_id=1, source_target_pairs={{0,32},{8,40},{16,48},{24,56},{32,64},{40,72},{48,80},{56,88},{64,... | collective-permute-start | bytes 1572872 | tf_op jit(solution)/shard_map/documents/ppermute | solution.py:58
  84.1 9.6 %collective-permute-start.12 = (bf16[2,2,512,128]{3,2,1,0:T(8,128)(2,1)S(1)}, bf16[2,2,512,128]{3,2,1,0:T(8,128)(2,1)S(1)}, u32[]{:S(2)}, u32[]{:S(2)}) collective-permute-start(bf16[2,2,512,128]{3,2,1,0:T(8,128)(2,1)S(1)} %get-tuple-element.71), channel_id=1, source_target_pairs={{0,96},{8,104},{16,112},{24,120},{32,0},{40,8},{48,16},{56,24},{64... | collective-permute-start | bytes 1572872 | tf_op jit(solution)/shard_map/documents/ppermute | solution.py:58
  93.8 2.9 %collective-permute-start.13 = (bf16[2,2,512,128]{3,2,1,0:T(8,128)(2,1)S(1)}, bf16[2,2,512,128]{3,2,1,0:T(8,128)(2,1)S(1)}, u32[]{:S(2)}, u32[]{:S(2)}) collective-permute-start(bf16[2,2,512,128]{3,2,1,0:T(8,128)(2,1)S(1)} %get-tuple-element.72), channel_id=1, source_target_pairs={{0,8},{8,16},{16,24},{24,0},{32,40},{40,48},{48,56},{56,32},{64,72... | collective-permute-start | bytes 1572872 | tf_op jit(solution)/shard_map/documents/ppermute | solution.py:58
  96.7 6.6 %attend.7 = (f32[2,4,320,128]{3,2,1,0:T(8,128)S(1)}, f32[2,4,320,128]{3,2,1,0:T(8,128)S(1)}, f32[2,4,320,128]{3,2,1,0:T(8,128)S(1)}) custom-call(s32[97]{0:T(128)S(1)} %copy-done.4, bf16[2,320,512]{2,1,0:T(8,128)(2,1)S(1)} %bitcast.18, s32[2,4,320,1]{3,2,1,0:T(8,128)S(1)} %reshape.47.refs_2_, ...), custom_call_target="tpu_custom_call", output_to_operand_aliasing={{0}: (3, {}), {1}: (4, {}), {2}: (5, {})} | custom-call | flops 1342177280 | bytes 9437184 | tf_op jit(solution)/shard_map/attention/attend/pallas_call | solution.py:281
  103.3 7.4 %attend.8 = (f32[2,4,320,128]{3,2,1,0:T(8,128)S(1)}, f32[2,4,320,128]{3,2,1,0:T(8,128)S(1)}, f32[2,4,320,128]{3,2,1,0:T(8,128)S(1)}) custom-call(s32[97]{0:T(128)S(1)} %copy-done.4, bf16[2,320,512]{2,1,0:T(8,128)(2,1)S(1)} %bitcast.19, s32[2,4,320,1]{3,2,1,0:T(8,128)S(1)} %reshape.47.refs_2_, ...), custom_call_target="tpu_custom_call", output_to_operand_aliasing={{0}: (3, {}), {1}: (4, {}), {2}: (5, {})} | custom-call | flops 1677721600 | bytes 9699328 | tf_op jit(solution)/shard_map/attention/attend/pallas_call | solution.py:281
  110.8 7.3 %attend.9 = (f32[2,4,320,128]{3,2,1,0:T(8,128)S(1)}, f32[2,4,320,128]{3,2,1,0:T(8,128)S(1)}, f32[2,4,320,128]{3,2,1,0:T(8,128)S(1)}, bf16[640,512]{1,0:T(8,128)(2,1)}) custom-call(s32[97]{0:T(128)S(1)} %copy-done.4, bf16[2,320,512]{2,1,0:T(8,128)(2,1)S(1)} %bitcast.20, ...), custom_call_target="tpu_custom_call", output_to_operand_aliasing={{0}: (3, {}), {1}: (4, {}), {2}: (5, {})} | custom-call | flops 1342177280 | bytes 9437184 | tf_op jit(solution)/shard_map/attention/attend/pallas_call | solution.py:281
  122.0 8.5 %collective-permute-start.19 = (bf16[640,512]{1,0:T(8,128)(2,1)}, bf16[640,512]{1,0:T(8,128)(2,1)S(1)}, u32[]{:S(2)}, u32[]{:S(2)}) collective-permute-start(bf16[640,512]{1,0:T(8,128)(2,1)} %get-tuple-element.74.refs_0_), channel_id=1, source_target_pairs={{0,1},{1,0},{2,3},{3,2},{4,5},{5,4},{6,7},{7,6},{8,9},{9,8},{10,11... | collective-permute-start | bytes 1966088 | tf_op jit(solution)/shard_map/output/ppermute | solution.py:346
  130.5 8.7 %collective-permute-start.20 = (bf16[640,512]{1,0:T(8,128)(2,1)S(1)}, bf16[640,512]{1,0:T(8,128)(2,1)}, u32[]{:S(2)}, u32[]{:S(2)}) collective-permute-start(bf16[640,512]{1,0:T(8,128)(2,1)S(1)} %collective-permute-done.15.refs_2_), channel_id=1, source_target_pairs={{0,1},{1,0},{2,3},{3,2},{4,5},{5,4},{6,7},{7,6},{8,9},{9,8},{10,11... | collective-permute-start | bytes 1966088 | tf_op jit(solution)/shard_map/output/ppermute | solution.py:346
  144.8 3.8 %project.2.refs_4_ = f32[640,512]{1,0:T(8,128)S(1)} custom-call(s32[8]{0:T(128)S(1)} %pad_add_fusion.place_ref, bf16[4096,512]{1,0:T(8,128)(2,1)S(1)} %copy-done.2, bf16[640,512]{1,0:T(8,128)(2,1)} %get-tuple-element.74.refs_0_, bf16[640,512]{1,0:T(8,128)(2,1)S(1)} %collective-permute-done.19.refs_1_, bf16[640,512]{1,0:T(8,128)(2,1)S(1)} %collective-permute-done.15.refs_2_, ...), custom_call_target="tpu_custom_call" | custom-call | flops 2013265920 | bytes 6291456 | tf_op jit(solution)/shard_map/output/project/pallas_call | solution.py:328
  152.8 2.2 %project.3 = bf16[640,512]{1,0:T(8,128)(2,1)} custom-call(s32[8]{0:T(128)S(1)} %pad_add_fusion.place_ref, bf16[4096,512]{1,0:T(8,128)(2,1)S(1)} %copy-done.3, bf16[320,512]{1,0:T(8,128)(2,1)S(1)} %collective-permute-done.16.refs_0_, bf16[320,512]{1,0:T(8,128)(2,1)S(1)} %collective-permute-done.18.refs_1_, ...), custom_call_target="tpu_custom_call" | custom-call | flops 671088640 | bytes 2097152 | tf_op jit(solution)/shard_map/output/project/pallas_call | solution.py:328
  (87 shorter events, 33.7 us)
Async XLA Ops:
  5.8 37.9 %collective-permute-start = (bf16[6,2,512,128]{3,2,1,0:T(8,128)(2,1)}, bf16[6,2,512,128]{3,2,1,0:T(8,128)(2,1)}, u32[]{:S(2)}, u32[]{:S(2)}) collective-permute-start(bf16[6,2,512,128]{3,2,1,0:T(8,128)(2,1)} %get-tuple-element.45), channel_id=1, source_target_pairs={{0,64},{8,72},{16,80},{24,88},{32,96},{40,104},{48,112},{56,120},{... | collective-permute-start | bytes 4718600 | tf_op jit(solution)/shard_map/documents/ppermute | solution.py:58
  9.6 48.0 %collective-permute-start.1 = (bf16[6,2,512,128]{3,2,1,0:T(8,128)(2,1)}, bf16[6,2,512,128]{3,2,1,0:T(8,128)(2,1)}, u32[]{:S(2)}, u32[]{:S(2)}) collective-permute-start(bf16[6,2,512,128]{3,2,1,0:T(8,128)(2,1)} %get-tuple-element.46), channel_id=1, source_target_pairs={{0,16},{8,24},{16,0},{24,8},{32,48},{40,56},{48,32},{56,40},{64,80... | collective-permute-start | bytes 4718600 | tf_op jit(solution)/shard_map/documents/ppermute | solution.py:58
  15.6 45.5 %collective-permute-start.2 = (bf16[2,2,512,128]{3,2,1,0:T(8,128)(2,1)}, bf16[2,2,512,128]{3,2,1,0:T(8,128)(2,1)S(1)}, u32[]{:S(2)}, u32[]{:S(2)}) collective-permute-start(bf16[2,2,512,128]{3,2,1,0:T(8,128)(2,1)} %get-tuple-element.50), channel_id=1, source_target_pairs={{0,40},{8,48},{16,56},{24,32},{32,72},{40,80},{48,88},{56,64},{64,... | collective-permute-start | bytes 1572872 | tf_op jit(solution)/shard_map/documents/ppermute | solution.py:58
  17.4 44.4 %collective-permute-start.3 = (bf16[2,2,512,128]{3,2,1,0:T(8,128)(2,1)}, bf16[2,2,512,128]{3,2,1,0:T(8,128)(2,1)}, u32[]{:S(2)}, u32[]{:S(2)}) collective-permute-start(bf16[2,2,512,128]{3,2,1,0:T(8,128)(2,1)} %get-tuple-element.51), channel_id=1, source_target_pairs={{0,120},{8,96},{16,104},{24,112},{32,24},{40,0},{48,8},{56,16},{64... | collective-permute-start | bytes 1572872 | tf_op jit(solution)/shard_map/documents/ppermute | solution.py:58
  20.4 48.7 %collective-permute-start.4 = (bf16[2,2,512,128]{3,2,1,0:T(8,128)(2,1)}, bf16[2,2,512,128]{3,2,1,0:T(8,128)(2,1)}, u32[]{:S(2)}, u32[]{:S(2)}) collective-permute-start(bf16[2,2,512,128]{3,2,1,0:T(8,128)(2,1)} %get-tuple-element.52), channel_id=1, source_target_pairs={{0,56},{8,32},{16,40},{24,48},{32,88},{40,64},{48,72},{56,80},{64,... | collective-permute-start | bytes 1572872 | tf_op jit(solution)/shard_map/documents/ppermute | solution.py:58
  43.7 30.8 %collective-permute-start.5 = (bf16[2,2,512,128]{3,2,1,0:T(8,128)(2,1)}, bf16[2,2,512,128]{3,2,1,0:T(8,128)(2,1)S(1)}, u32[]{:S(2)}, u32[]{:S(2)}) collective-permute-start(bf16[2,2,512,128]{3,2,1,0:T(8,128)(2,1)} %get-tuple-element.53), channel_id=1, source_target_pairs={{0,104},{8,112},{16,120},{24,96},{32,8},{40,16},{48,24},{56,0},{64... | collective-permute-start | bytes 1572872 | tf_op jit(solution)/shard_map/documents/ppermute | solution.py:58
  57.6 23.4 %collective-permute-start.10 = (bf16[2,2,512,128]{3,2,1,0:T(8,128)(2,1)S(1)}, bf16[2,2,512,128]{3,2,1,0:T(8,128)(2,1)S(1)}, u32[]{:S(2)}, u32[]{:S(2)}) collective-permute-start(bf16[2,2,512,128]{3,2,1,0:T(8,128)(2,1)S(1)} %copy-done.15), channel_id=1, source_target_pairs={{0,80},{8,88},{16,64},{24,72},{32,112},{40,120},{48,96},{56,104},{... | collective-permute-start | bytes 1572872 | tf_op jit(solution)/shard_map/documents/ppermute | solution.py:58
  61.1 23.1 %collective-permute-start.6 = (bf16[2,2,512,128]{3,2,1,0:T(8,128)(2,1)S(1)}, bf16[2,2,512,128]{3,2,1,0:T(8,128)(2,1)S(1)}, u32[]{:S(2)}, u32[]{:S(2)}) collective-permute-start(bf16[2,2,512,128]{3,2,1,0:T(8,128)(2,1)S(1)} %copy-done.14), channel_id=1, source_target_pairs={{0,32},{8,40},{16,48},{24,56},{32,64},{40,72},{48,80},{56,88},{64,... | collective-permute-start | bytes 1572872 | tf_op jit(solution)/shard_map/documents/ppermute | solution.py:58
  61.8 32.0 %collective-permute-start.7 = (bf16[2,2,512,128]{3,2,1,0:T(8,128)(2,1)S(1)}, bf16[2,2,512,128]{3,2,1,0:T(8,128)(2,1)S(1)}, u32[]{:S(2)}, u32[]{:S(2)}) collective-permute-start(bf16[2,2,512,128]{3,2,1,0:T(8,128)(2,1)S(1)} %copy-done.13), channel_id=1, source_target_pairs={{0,96},{8,104},{16,112},{24,120},{32,0},{40,8},{48,16},{56,24},{64... | collective-permute-start | bytes 1572872 | tf_op jit(solution)/shard_map/documents/ppermute | solution.py:58
  69.1 27.6 %collective-permute-start.8 = (bf16[2,2,512,128]{3,2,1,0:T(8,128)(2,1)S(1)}, bf16[2,2,512,128]{3,2,1,0:T(8,128)(2,1)S(1)}, u32[]{:S(2)}, u32[]{:S(2)}) collective-permute-start(bf16[2,2,512,128]{3,2,1,0:T(8,128)(2,1)S(1)} %copy-done.12), channel_id=1, source_target_pairs={{0,8},{8,16},{16,24},{24,0},{32,40},{40,48},{48,56},{56,32},{64,72... | collective-permute-start | bytes 1572872 | tf_op jit(solution)/shard_map/documents/ppermute | solution.py:58
  74.5 28.8 %collective-permute-start.9 = (bf16[2,2,512,128]{3,2,1,0:T(8,128)(2,1)S(1)}, bf16[2,2,512,128]{3,2,1,0:T(8,128)(2,1)S(1)}, u32[]{:S(2)}, u32[]{:S(2)}) collective-permute-start(bf16[2,2,512,128]{3,2,1,0:T(8,128)(2,1)S(1)} %copy-done.11), channel_id=1, source_target_pairs={{0,24},{8,0},{16,8},{24,16},{32,56},{40,32},{48,40},{56,48},{64,88... | collective-permute-start | bytes 1572872 | tf_op jit(solution)/shard_map/documents/ppermute | solution.py:58
  81.0 29.7 %collective-permute-start.11 = (bf16[2,2,512,128]{3,2,1,0:T(8,128)(2,1)S(1)}, bf16[2,2,512,128]{3,2,1,0:T(8,128)(2,1)S(1)}, u32[]{:S(2)}, u32[]{:S(2)}) collective-permute-start(bf16[2,2,512,128]{3,2,1,0:T(8,128)(2,1)S(1)} %get-tuple-element.70), channel_id=1, source_target_pairs={{0,32},{8,40},{16,48},{24,56},{32,64},{40,72},{48,80},{56,88},{64,... | collective-permute-start | bytes 1572872 | tf_op jit(solution)/shard_map/documents/ppermute | solution.py:58
  84.1 26.6 %collective-permute-start.12 = (bf16[2,2,512,128]{3,2,1,0:T(8,128)(2,1)S(1)}, bf16[2,2,512,128]{3,2,1,0:T(8,128)(2,1)S(1)}, u32[]{:S(2)}, u32[]{:S(2)}) collective-permute-start(bf16[2,2,512,128]{3,2,1,0:T(8,128)(2,1)S(1)} %get-tuple-element.71), channel_id=1, source_target_pairs={{0,96},{8,104},{16,112},{24,120},{32,0},{40,8},{48,16},{56,24},{64... | collective-permute-start | bytes 1572872 | tf_op jit(solution)/shard_map/documents/ppermute | solution.py:58
  93.8 17.0 %collective-permute-start.13 = (bf16[2,2,512,128]{3,2,1,0:T(8,128)(2,1)S(1)}, bf16[2,2,512,128]{3,2,1,0:T(8,128)(2,1)S(1)}, u32[]{:S(2)}, u32[]{:S(2)}) collective-permute-start(bf16[2,2,512,128]{3,2,1,0:T(8,128)(2,1)S(1)} %get-tuple-element.72), channel_id=1, source_target_pairs={{0,8},{8,16},{16,24},{24,0},{32,40},{40,48},{48,56},{56,32},{64,72... | collective-permute-start | bytes 1572872 | tf_op jit(solution)/shard_map/documents/ppermute | solution.py:58
  96.7 14.1 %collective-permute-start.14 = (bf16[2,2,512,128]{3,2,1,0:T(8,128)(2,1)S(1)}, bf16[2,2,512,128]{3,2,1,0:T(8,128)(2,1)S(1)}, u32[]{:S(2)}, u32[]{:S(2)}) collective-permute-start(bf16[2,2,512,128]{3,2,1,0:T(8,128)(2,1)S(1)} %get-tuple-element.73), channel_id=1, source_target_pairs={{0,24},{8,0},{16,8},{24,16},{32,56},{40,32},{48,40},{56,48},{64,88... | collective-permute-start | bytes 1572872 | tf_op jit(solution)/shard_map/documents/ppermute | solution.py:58
  118.1 12.4 %collective-permute-start.15 = (bf16[640,512]{1,0:T(8,128)(2,1)}, bf16[640,512]{1,0:T(8,128)(2,1)S(1)}, u32[]{:S(2)}, u32[]{:S(2)}) collective-permute-start(bf16[640,512]{1,0:T(8,128)(2,1)} %get-tuple-element.74.refs_0_), channel_id=1, source_target_pairs={{0,2},{1,3},{2,4},{3,5},{4,6},{5,7},{6,0},{7,1},{8,10},{9,11},{10,... | collective-permute-start | bytes 1966088 | tf_op jit(solution)/shard_map/output/ppermute | solution.py:342
  119.8 19.4 %collective-permute-start.17 = (bf16[640,512]{1,0:T(8,128)(2,1)}, bf16[640,512]{1,0:T(8,128)(2,1)S(1)}, u32[]{:S(2)}, u32[]{:S(2)}) collective-permute-start(bf16[640,512]{1,0:T(8,128)(2,1)} %get-tuple-element.74.refs_0_), channel_id=1, source_target_pairs={{0,6},{1,7},{2,0},{3,1},{4,2},{5,3},{6,4},{7,5},{8,14},{9,15},{10,... | collective-permute-start | bytes 1966088 | tf_op jit(solution)/shard_map/output/ppermute | solution.py:342
  122.0 20.6 %collective-permute-start.19 = (bf16[640,512]{1,0:T(8,128)(2,1)}, bf16[640,512]{1,0:T(8,128)(2,1)S(1)}, u32[]{:S(2)}, u32[]{:S(2)}) collective-permute-start(bf16[640,512]{1,0:T(8,128)(2,1)} %get-tuple-element.74.refs_0_), channel_id=1, source_target_pairs={{0,1},{1,0},{2,3},{3,2},{4,5},{5,4},{6,7},{7,6},{8,9},{9,8},{10,11... | collective-permute-start | bytes 1966088 | tf_op jit(solution)/shard_map/output/ppermute | solution.py:346
  130.5 12.1 %collective-permute-start.20 = (bf16[640,512]{1,0:T(8,128)(2,1)S(1)}, bf16[640,512]{1,0:T(8,128)(2,1)}, u32[]{:S(2)}, u32[]{:S(2)}) collective-permute-start(bf16[640,512]{1,0:T(8,128)(2,1)S(1)} %collective-permute-done.15.refs_2_), channel_id=1, source_target_pairs={{0,1},{1,0},{2,3},{3,2},{4,5},{5,4},{6,7},{7,6},{8,9},{9,8},{10,11... | collective-permute-start | bytes 1966088 | tf_op jit(solution)/shard_map/output/ppermute | solution.py:346
  139.2 3.4 %collective-permute-start.21 = (bf16[640,512]{1,0:T(8,128)(2,1)S(1)}, bf16[640,512]{1,0:T(8,128)(2,1)}, u32[]{:S(2)}, u32[]{:S(2)}) collective-permute-start(bf16[640,512]{1,0:T(8,128)(2,1)S(1)} %collective-permute-done.17.refs_3_), channel_id=1, source_target_pairs={{0,1},{1,0},{2,3},{3,2},{4,5},{5,4},{6,7},{7,6},{8,9},{9,8},{10,11... | collective-permute-start | bytes 1966088 | tf_op jit(solution)/shard_map/output/ppermute | solution.py:346
  139.3 10.8 %collective-permute-start.16 = (bf16[320,512]{1,0:T(8,128)(2,1)S(1)}, bf16[320,512]{1,0:T(8,128)(2,1)S(1)}, u32[]{:S(2)}, u32[]{:S(2)}) collective-permute-start(bf16[320,512]{1,0:T(8,128)(2,1)S(1)} %slice.28), channel_id=1, source_target_pairs={{0,2},{1,3},{2,4},{3,5},{4,6},{5,7},{6,0},{7,1},{8,10},{9,11},{10,... | collective-permute-start | bytes 983048 | tf_op jit(solution)/shard_map/output/ppermute | solution.py:342
  140.9 9.2 %collective-permute-start.18 = (bf16[320,512]{1,0:T(8,128)(2,1)S(1)}, bf16[320,512]{1,0:T(8,128)(2,1)S(1)}, u32[]{:S(2)}, u32[]{:S(2)}) collective-permute-start(bf16[320,512]{1,0:T(8,128)(2,1)S(1)} %slice.29), channel_id=1, source_target_pairs={{0,6},{1,7},{2,0},{3,1},{4,2},{5,3},{6,4},{7,5},{8,14},{9,15},{10,... | collective-permute-start | bytes 983048 | tf_op jit(solution)/shard_map/output/ppermute | solution.py:342
  150.1 2.3 %collective-permute-start.22 = (bf16[320,512]{1,0:T(8,128)(2,1)S(1)}, bf16[320,512]{1,0:T(8,128)(2,1)S(1)}, u32[]{:S(2)}, u32[]{:S(2)}) collective-permute-start(bf16[320,512]{1,0:T(8,128)(2,1)S(1)} %collective-permute-done.16.refs_0_), channel_id=1, source_target_pairs={{0,1},{1,0},{2,3},{3,2},{4,5},{5,4},{6,7},{7,6},{8,9},{9,8},{10,11... | collective-permute-start | bytes 983048 | tf_op jit(solution)/shard_map/output/ppermute | solution.py:346
  151.1 1.7 %collective-permute-start.23 = (bf16[320,512]{1,0:T(8,128)(2,1)S(1)}, bf16[320,512]{1,0:T(8,128)(2,1)S(1)}, u32[]{:S(2)}, u32[]{:S(2)}) collective-permute-start(bf16[320,512]{1,0:T(8,128)(2,1)S(1)} %collective-permute-done.18.refs_1_), channel_id=1, source_target_pairs={{0,1},{1,0},{2,3},{3,2},{4,5},{5,4},{6,7},{7,6},{8,9},{9,8},{10,11... | collective-permute-start | bytes 983048 | tf_op jit(solution)/shard_map/output/ppermute | solution.py:346
  (16 other events, 201.4 us)

commit v5 on v4

--- a/solution.py
+++ b/solution.py
@@ -232,31 +232,38 @@
         idx = jnp.where((row < length) & (replaced == 0), idx, FAR)
         pltpu.make_async_copy(arrays[0].at[0], buf.at[at], sem.at[at]).wait()
 
-        def step(tile, wide):
+        bias = jnp.where(idx < FAR, 0.0, -1e30)
+
+        def step(tile):
+            wide = TILES - tile
+
             def get(ref):
-                return ref[r, pl.ds(tile, wide)].reshape(wide * ROWS, HD)
-
-            s = scores(r, tile, wide, buf[at, 0], idx)
+                return ref[r, tile:].reshape(wide * ROWS, HD)
+
+            q = []
+            for n in range(tile, TILES):
+                rows = slice(n * SUB, (n + 1) * SUB)
+                q += [q_ref[r, rows, h * HD : (h + 1) * HD] for h in range(GROUP)]
+            s = lax.dot_general(
+                jnp.concatenate(q, axis=0),
+                buf[at, 0],
+                (((1,), (1,)), ((), ())),
+                preferred_element_type=jnp.float32,
+            )
+            within = jnp.where(idx <= pos_ref[r, tile], s[:ROWS], -1e30)
+            s = jnp.concatenate([within, s[ROWS:] + bias], axis=0) if wide > 1 else within
             before = get(top_ref)
             top = jnp.maximum(before, jnp.max(s, axis=1, keepdims=True))
             fade = jnp.exp2((before - top) * EXP2)
             p, sums = weigh(s, top)
-            put(top_ref, r, tile, wide, top)
-            put(sum_ref, r, tile, wide, get(sum_ref) * fade + sums)
             value = jnp.dot(p, buf[at, 1], preferred_element_type=jnp.float32)
-            put(acc, r, tile, wide, get(acc) * fade + value)
-
-        tile = j // per
-
-        @pl.when(tile % 2 == 1)
-        def _():
-            step(tile, 1)
-
-        def pair(n, carry):
-            step(n * 2, 2)
-            return carry
-
-        lax.fori_loop((tile + 1) // 2, TILES // 2, pair, 0)
+            shape = (wide, ROWS, HD)
+            top_ref[r, tile:] = top.reshape(shape)
+            sum_ref[r, tile:] = (get(sum_ref) * fade + sums).reshape(shape)
+            acc[r, tile:] = (get(acc) * fade + value).reshape(shape)
+
+        for tile in range(TILES):
+            pl.when(j // per == tile)(functools.partial(step, tile))
         return carry
 
     lax.fori_loop(0, found, item, 0)

time: 155 us -> 151 us (0.974)
  starting transfers between devices: 65.5 us -> 59.3 us
  waiting for transfers between devices: 24.5 us -> 29.1 us
  Pallas kernels: 43.9 us -> 41.2 us
    ppermute x15, starting transfers between devices: 40.3 us -> 34.2 us  [shift(): return lax.ppermute(block, 'grp', pairs)]
    ppermute x15, waiting for transfers between devices: 21.3 us -> 25.9 us  [shift(): return lax.ppermute(block, 'grp', pairs)]
    pallas_call x5, Pallas kernels: 30.3 us -> 26.3 us  [attend(): pl.pallas_call(functools.partial(attend_kernel, shifts, count, first, las...]
  transfers between devices with their start and end apart: 24 -> 24, of which waited for: 8 -> 8; matrix products, arithmetic and copies ran while one was open for 11% -> 11% of each run, Pallas kernels for 19% -> 20%
where the time goes in v5:
time: 151 us
  starting transfers between devices  59.3 us (39%)
  Pallas kernels  41.2 us (27%)
  waiting for transfers between devices  29.1 us (19%)
  matrix products  9.35 us (6%)
  local copies, waits for them, and re-layouts  8.26 us (5%)
  other arithmetic  3.18 us (2%)
    ppermute x15, starting transfers between devices, shift(): return lax.ppermute(block, 'grp', pairs)  34.2 us
    pallas_call x5, Pallas kernels, attend(): pl.pallas_call(functools.partial(attend_kernel, shifts, count, first, las...  26.3 us
    ppermute x15, waiting for transfers between devices, shift(): return lax.ppermute(block, 'grp', pairs)  25.9 us
    ppermute x5, starting transfers between devices, other_core(): return lax.ppermute(block, 'tp', [(i, i ^ 1) for i in range(KVH)])  17.7 us
    dot_general x3, matrix products, dot(): out = jnp.dot(normed_rows, w, preferred_element_type=jnp.float32)  9.35 us
    pallas_call x2, Pallas kernels, pack(): pl.pallas_call(kernel, out_shape=[jax.ShapeDtypeStruct(s, jnp.bfloat16) f...  8.84 us
    ppermute x4, starting transfers between devices, ring(): lax.ppermute(block, 'tp', [(i, (i + 2 * by) % KVH) for i in range(KVH)])  7.45 us
    pallas_call x2, Pallas kernels, project(): pl.pallas_call(functools.partial(project_kernel, spans, last), out_shape=...  6.06 us
  transfers between devices with their start and end apart: 24, of which 8 were waited for; matrix products, arithmetic and copies ran while one was open for 11% of the time, Pallas kernels for 20%

profile of v5, /device:TPU:1, one launch (start us, length us, event | category | flops | bytes accessed | tf_op | source)
XLA Modules:
  0.0 150.8 jit_solution(11323746848022991390)
XLA Ops:
  1.5 4.4 %pack.2 = (bf16[6,2,512,128]{3,2,1,0:T(8,128)(2,1)}, bf16[6,2,512,128]{3,2,1,0:T(8,128)(2,1)}, s32[97]{0:T(128)}) custom-call(s32[1]{0:T(128)} %bitcast.4.me_ref, s32[256]{0:T(256)} %home_ref.1, s32[256]{0:T(256)} %reshape.39.ids_ref, s32[256]{0:T(256)} %len_ref.1, bf16[16,2,512,128]{3,2,1,0:T(8,128)(2,1)} %cache_ref.3), custom_call_target="tpu_custom_call" | custom-call | bytes 5242880 | tf_op jit(solution)/shard_map/pack/pack/pallas_call | solution.py:141
  5.9 3.7 %collective-permute-start = (bf16[6,2,512,128]{3,2,1,0:T(8,128)(2,1)}, bf16[6,2,512,128]{3,2,1,0:T(8,128)(2,1)}, u32[]{:S(2)}, u32[]{:S(2)}) collective-permute-start(bf16[6,2,512,128]{3,2,1,0:T(8,128)(2,1)} %get-tuple-element.45), channel_id=1, source_target_pairs={{0,64},{8,72},{16,80},{24,88},{32,96},{40,104},{48,112},{56,120},{... | collective-permute-start | bytes 4718600 | tf_op jit(solution)/shard_map/documents/ppermute | solution.py:58
  9.6 2.9 %collective-permute-start.1 = (bf16[6,2,512,128]{3,2,1,0:T(8,128)(2,1)}, bf16[6,2,512,128]{3,2,1,0:T(8,128)(2,1)}, u32[]{:S(2)}, u32[]{:S(2)}) collective-permute-start(bf16[6,2,512,128]{3,2,1,0:T(8,128)(2,1)} %get-tuple-element.46), channel_id=1, source_target_pairs={{0,16},{8,24},{16,0},{24,8},{32,48},{40,56},{48,32},{56,40},{64,80... | collective-permute-start | bytes 4718600 | tf_op jit(solution)/shard_map/documents/ppermute | solution.py:58
  12.6 4.4 %pack.3 = (bf16[2,2,512,128]{3,2,1,0:T(8,128)(2,1)}, bf16[2,2,512,128]{3,2,1,0:T(8,128)(2,1)}, bf16[2,2,512,128]{3,2,1,0:T(8,128)(2,1)}, bf16[2,2,512,128]{3,2,1...) custom-call(s32[97]{0:T(128)} %get-tuple-element.41.refs_0_.table_re, ...), custom_call_target="tpu_custom_call" | custom-call | bytes 5242880 | tf_op jit(solution)/shard_map/pack/pack/pallas_call | solution.py:141
  17.3 4.6 %collective-permute-start.3 = (bf16[2,2,512,128]{3,2,1,0:T(8,128)(2,1)}, bf16[2,2,512,128]{3,2,1,0:T(8,128)(2,1)}, u32[]{:S(2)}, u32[]{:S(2)}) collective-permute-start(bf16[2,2,512,128]{3,2,1,0:T(8,128)(2,1)} %get-tuple-element.51), channel_id=1, source_target_pairs={{0,120},{8,96},{16,104},{24,112},{32,24},{40,0},{48,8},{56,16},{64... | collective-permute-start | bytes 1572872 | tf_op jit(solution)/shard_map/documents/ppermute | solution.py:58
  25.2 2.9 %convolution_convert_fusion = bf16[640,512]{1,0:T(8,128)(2,1)S(1)} fusion(bf16[640,4096]{1,0:T(8,128)(2,1)S(1)} %bitcast.21, bf16[4096,512]{1,0:T(8,128)(2,1)S(1)} %copy-done.10), kind=kOutput, calls=%fused_computation.5 | convolution fusion | flops 2684682240 | bytes 10092544 | tf_op jit(solution)/shard_map/projections/dot_general | solution.py:394
  28.1 2.2 %convolution_convert_fusion.2 = bf16[640,128]{1,0:T(8,128)(2,1)} fusion(bf16[640,4096]{1,0:T(8,128)(2,1)S(1)} %bitcast.22, bf16[4096,128]{1,0:T(8,128)(2,1)S(1)} %copy-done), kind=kOutput, calls=%fused_computation.7 | convolution fusion | flops 671170560 | bytes 6455296 | tf_op jit(solution)/shard_map/projections/dot_general | solution.py:394
  32.0 11.8 %collective-permute-done.refs_6_ = bf16[6,2,512,128]{3,2,1,0:T(8,128)(2,1)} collective-permute-done((bf16[6,2,512,128]{3,2,1,0:T(8,128)(2,1)}, bf16[6,2,512,128]{3,2,1,0:T(8,128)(2,1)}, u32[]{:S(2)}, u32[]{:S(2)}) %collective-permute-start) | collective-permute-done | bytes 1572896 | tf_op jit(solution)/shard_map/documents/ppermute | solution.py:58
  43.8 3.9 %collective-permute-start.5 = (bf16[2,2,512,128]{3,2,1,0:T(8,128)(2,1)}, bf16[2,2,512,128]{3,2,1,0:T(8,128)(2,1)S(1)}, u32[]{:S(2)}, u32[]{:S(2)}) collective-permute-start(bf16[2,2,512,128]{3,2,1,0:T(8,128)(2,1)} %get-tuple-element.53), channel_id=1, source_target_pairs={{0,104},{8,112},{16,120},{24,96},{32,8},{40,16},{48,24},{56,0},{64... | collective-permute-start | bytes 1572872 | tf_op jit(solution)/shard_map/documents/ppermute | solution.py:58
  47.6 4.3 %convolution_convert_fusion.1 = bf16[640,128]{1,0:T(8,128)(2,1)S(1)} fusion(bf16[640,4096]{1,0:T(8,128)(2,1)} %bitcast.23, bf16[4096,128]{1,0:T(8,128)(2,1)} %param.15), kind=kOutput, calls=%fused_computation.6 | convolution fusion | flops 671170560 | bytes 6455296 | tf_op jit(solution)/shard_map/projections/dot_general | solution.py:394
  52.1 6.2 %attend.5 = (f32[2,4,320,128]{3,2,1,0:T(8,128)S(1)}, f32[2,4,320,128]{3,2,1,0:T(8,128)S(1)}, f32[2,4,320,128]{3,2,1,0:T(8,128)S(1)}) custom-call(s32[97]{0:T(128)S(1)} %copy-done.4, bf16[2,320,512]{2,1,0:T(8,128)(2,1)S(1)} %bitcast.16, s32[2,4,320,1]{3,2,1,0:T(8,128)S(1)} %reshape.47.refs_2_, s32[2,1,384]{2,1,0:T(1,128)S(1)} %reshape.43.refs_3_, ...), custom_call_target="tpu_custom_call" | custom-call | flops 335544320 | bytes 8650752 | tf_op jit(solution)/shard_map/attention/attend/pallas_call | solution.py:288
  62.2 6.8 %collective-permute-done.4.refs_8_ = bf16[2,2,512,128]{3,2,1,0:T(8,128)(2,1)} collective-permute-done((bf16[2,2,512,128]{3,2,1,0:T(8,128)(2,1)}, bf16[2,2,512,128]{3,2,1,0:T(8,128)(2,1)}, u32[]{:S(2)}, u32[]{:S(2)}) %collective-permute-start.4) | collective-permute-done | bytes 524320 | tf_op jit(solution)/shard_map/documents/ppermute | solution.py:58
  72.5 7.2 %collective-permute-done.5.refs_9_ = bf16[2,2,512,128]{3,2,1,0:T(8,128)(2,1)S(1)} collective-permute-done((bf16[2,2,512,128]{3,2,1,0:T(8,128)(2,1)}, bf16[2,2,512,128]{3,2,1,0:T(8,128)(2,1)S(1)}, u32[]{:S(2)}, u32[]{:S(2)}) %collective-permute-start.5) | collective-permute-done | bytes 524320 | tf_op jit(solution)/shard_map/documents/ppermute | solution.py:58
  81.0 3.3 %attend.6 = (f32[2,4,320,128]{3,2,1,0:T(8,128)S(1)}, f32[2,4,320,128]{3,2,1,0:T(8,128)S(1)}, f32[2,4,320,128]{3,2,1,0:T(8,128)S(1)}) custom-call(s32[97]{0:T(128)S(1)} %copy-done.4, bf16[2,320,512]{2,1,0:T(8,128)(2,1)S(1)} %bitcast.17, s32[2,4,320,1]{3,2,1,0:T(8,128)S(1)} %reshape.47.refs_2_, ...), custom_call_target="tpu_custom_call", output_to_operand_aliasing={{0}: (3, {}), {1}: (4, {}), {2}: (5, {})} | custom-call | flops 671088640 | bytes 8912896 | tf_op jit(solution)/shard_map/attention/attend/pallas_call | solution.py:288
  84.3 4.0 %collective-permute-start.11 = (bf16[2,2,512,128]{3,2,1,0:T(8,128)(2,1)S(1)}, bf16[2,2,512,128]{3,2,1,0:T(8,128)(2,1)S(1)}, u32[]{:S(2)}, u32[]{:S(2)}) collective-permute-start(bf16[2,2,512,128]{3,2,1,0:T(8,128)(2,1)S(1)} %get-tuple-element.70), channel_id=1, source_target_pairs={{0,32},{8,40},{16,48},{24,56},{32,64},{40,72},{48,80},{56,88},{64,... | collective-permute-start | bytes 1572872 | tf_op jit(solution)/shard_map/documents/ppermute | solution.py:58
  88.3 6.0 %collective-permute-start.12 = (bf16[2,2,512,128]{3,2,1,0:T(8,128)(2,1)S(1)}, bf16[2,2,512,128]{3,2,1,0:T(8,128)(2,1)S(1)}, u32[]{:S(2)}, u32[]{:S(2)}) collective-permute-start(bf16[2,2,512,128]{3,2,1,0:T(8,128)(2,1)S(1)} %get-tuple-element.71), channel_id=1, source_target_pairs={{0,96},{8,104},{16,112},{24,120},{32,0},{40,8},{48,16},{56,24},{64... | collective-permute-start | bytes 1572872 | tf_op jit(solution)/shard_map/documents/ppermute | solution.py:58
  94.4 2.3 %collective-permute-start.13 = (bf16[2,2,512,128]{3,2,1,0:T(8,128)(2,1)S(1)}, bf16[2,2,512,128]{3,2,1,0:T(8,128)(2,1)S(1)}, u32[]{:S(2)}, u32[]{:S(2)}) collective-permute-start(bf16[2,2,512,128]{3,2,1,0:T(8,128)(2,1)S(1)} %get-tuple-element.72), channel_id=1, source_target_pairs={{0,8},{8,16},{16,24},{24,0},{32,40},{40,48},{48,56},{56,32},{64,72... | collective-permute-start | bytes 1572872 | tf_op jit(solution)/shard_map/documents/ppermute | solution.py:58
  97.0 5.6 %attend.7 = (f32[2,4,320,128]{3,2,1,0:T(8,128)S(1)}, f32[2,4,320,128]{3,2,1,0:T(8,128)S(1)}, f32[2,4,320,128]{3,2,1,0:T(8,128)S(1)}) custom-call(s32[97]{0:T(128)S(1)} %copy-done.4, bf16[2,320,512]{2,1,0:T(8,128)(2,1)S(1)} %bitcast.18, s32[2,4,320,1]{3,2,1,0:T(8,128)S(1)} %reshape.47.refs_2_, ...), custom_call_target="tpu_custom_call", output_to_operand_aliasing={{0}: (3, {}), {1}: (4, {}), {2}: (5, {})} | custom-call | flops 1342177280 | bytes 9437184 | tf_op jit(solution)/shard_map/attention/attend/pallas_call | solution.py:288
  102.6 7.0 %attend.8 = (f32[2,4,320,128]{3,2,1,0:T(8,128)S(1)}, f32[2,4,320,128]{3,2,1,0:T(8,128)S(1)}, f32[2,4,320,128]{3,2,1,0:T(8,128)S(1)}) custom-call(s32[97]{0:T(128)S(1)} %copy-done.4, bf16[2,320,512]{2,1,0:T(8,128)(2,1)S(1)} %bitcast.19, s32[2,4,320,1]{3,2,1,0:T(8,128)S(1)} %reshape.47.refs_2_, ...), custom_call_target="tpu_custom_call", output_to_operand_aliasing={{0}: (3, {}), {1}: (4, {}), {2}: (5, {})} | custom-call | flops 1677721600 | bytes 9699328 | tf_op jit(solution)/shard_map/attention/attend/pallas_call | solution.py:288
  109.7 4.2 %attend.9 = (f32[2,4,320,128]{3,2,1,0:T(8,128)S(1)}, f32[2,4,320,128]{3,2,1,0:T(8,128)S(1)}, f32[2,4,320,128]{3,2,1,0:T(8,128)S(1)}, bf16[640,512]{1,0:T(8,128)(2,1)}) custom-call(s32[97]{0:T(128)S(1)} %copy-done.4, bf16[2,320,512]{2,1,0:T(8,128)(2,1)S(1)} %bitcast.20, ...), custom_call_target="tpu_custom_call", output_to_operand_aliasing={{0}: (3, {}), {1}: (4, {}), {2}: (5, {})} | custom-call | flops 1342177280 | bytes 9437184 | tf_op jit(solution)/shard_map/attention/attend/pallas_call | solution.py:288
  117.9 8.0 %collective-permute-start.19 = (bf16[640,512]{1,0:T(8,128)(2,1)}, bf16[640,512]{1,0:T(8,128)(2,1)S(1)}, u32[]{:S(2)}, u32[]{:S(2)}) collective-permute-start(bf16[640,512]{1,0:T(8,128)(2,1)} %get-tuple-element.74.refs_0_), channel_id=1, source_target_pairs={{0,1},{1,0},{2,3},{3,2},{4,5},{5,4},{6,7},{7,6},{8,9},{9,8},{10,11... | collective-permute-start | bytes 1966088 | tf_op jit(solution)/shard_map/output/ppermute | solution.py:353
  126.0 8.6 %collective-permute-start.20 = (bf16[640,512]{1,0:T(8,128)(2,1)S(1)}, bf16[640,512]{1,0:T(8,128)(2,1)}, u32[]{:S(2)}, u32[]{:S(2)}) collective-permute-start(bf16[640,512]{1,0:T(8,128)(2,1)S(1)} %collective-permute-done.15.refs_2_), channel_id=1, source_target_pairs={{0,1},{1,0},{2,3},{3,2},{4,5},{5,4},{6,7},{7,6},{8,9},{9,8},{10,11... | collective-permute-start | bytes 1966088 | tf_op jit(solution)/shard_map/output/ppermute | solution.py:353
  140.5 3.8 %project.2.refs_4_ = f32[640,512]{1,0:T(8,128)S(1)} custom-call(s32[8]{0:T(128)S(1)} %pad_add_fusion.place_ref, bf16[4096,512]{1,0:T(8,128)(2,1)S(1)} %copy-done.2, bf16[640,512]{1,0:T(8,128)(2,1)} %get-tuple-element.74.refs_0_, bf16[640,512]{1,0:T(8,128)(2,1)S(1)} %collective-permute-done.19.refs_1_, bf16[640,512]{1,0:T(8,128)(2,1)S(1)} %collective-permute-done.15.refs_2_, ...), custom_call_target="tpu_custom_call" | custom-call | flops 2013265920 | bytes 6291456 | tf_op jit(solution)/shard_map/output/project/pallas_call | solution.py:335
  148.6 2.2 %project.3 = bf16[640,512]{1,0:T(8,128)(2,1)} custom-call(s32[8]{0:T(128)S(1)} %pad_add_fusion.place_ref, bf16[4096,512]{1,0:T(8,128)(2,1)S(1)} %copy-done.3, bf16[320,512]{1,0:T(8,128)(2,1)S(1)} %collective-permute-done.16.refs_0_, bf16[320,512]{1,0:T(8,128)(2,1)S(1)} %collective-permute-done.18.refs_1_, ...), custom_call_target="tpu_custom_call" | custom-call | flops 671088640 | bytes 2097152 | tf_op jit(solution)/shard_map/output/project/pallas_call | solution.py:335
  (87 shorter events, 30.0 us)
Async XLA Ops:
  5.9 37.8 %collective-permute-start = (bf16[6,2,512,128]{3,2,1,0:T(8,128)(2,1)}, bf16[6,2,512,128]{3,2,1,0:T(8,128)(2,1)}, u32[]{:S(2)}, u32[]{:S(2)}) collective-permute-start(bf16[6,2,512,128]{3,2,1,0:T(8,128)(2,1)} %get-tuple-element.45), channel_id=1, source_target_pairs={{0,64},{8,72},{16,80},{24,88},{32,96},{40,104},{48,112},{56,120},{... | collective-permute-start | bytes 4718600 | tf_op jit(solution)/shard_map/documents/ppermute | solution.py:58
  9.6 48.6 %collective-permute-start.1 = (bf16[6,2,512,128]{3,2,1,0:T(8,128)(2,1)}, bf16[6,2,512,128]{3,2,1,0:T(8,128)(2,1)}, u32[]{:S(2)}, u32[]{:S(2)}) collective-permute-start(bf16[6,2,512,128]{3,2,1,0:T(8,128)(2,1)} %get-tuple-element.46), channel_id=1, source_target_pairs={{0,16},{8,24},{16,0},{24,8},{32,48},{40,56},{48,32},{56,40},{64,80... | collective-permute-start | bytes 4718600 | tf_op jit(solution)/shard_map/documents/ppermute | solution.py:58
  17.0 42.3 %collective-permute-start.2 = (bf16[2,2,512,128]{3,2,1,0:T(8,128)(2,1)}, bf16[2,2,512,128]{3,2,1,0:T(8,128)(2,1)S(1)}, u32[]{:S(2)}, u32[]{:S(2)}) collective-permute-start(bf16[2,2,512,128]{3,2,1,0:T(8,128)(2,1)} %get-tuple-element.50), channel_id=1, source_target_pairs={{0,40},{8,48},{16,56},{24,32},{32,72},{40,80},{48,88},{56,64},{64,... | collective-permute-start | bytes 1572872 | tf_op jit(solution)/shard_map/documents/ppermute | solution.py:58
  17.3 44.2 %collective-permute-start.3 = (bf16[2,2,512,128]{3,2,1,0:T(8,128)(2,1)}, bf16[2,2,512,128]{3,2,1,0:T(8,128)(2,1)}, u32[]{:S(2)}, u32[]{:S(2)}) collective-permute-start(bf16[2,2,512,128]{3,2,1,0:T(8,128)(2,1)} %get-tuple-element.51), channel_id=1, source_target_pairs={{0,120},{8,96},{16,104},{24,112},{32,24},{40,0},{48,8},{56,16},{64... | collective-permute-start | bytes 1572872 | tf_op jit(solution)/shard_map/documents/ppermute | solution.py:58
  21.9 47.2 %collective-permute-start.4 = (bf16[2,2,512,128]{3,2,1,0:T(8,128)(2,1)}, bf16[2,2,512,128]{3,2,1,0:T(8,128)(2,1)}, u32[]{:S(2)}, u32[]{:S(2)}) collective-permute-start(bf16[2,2,512,128]{3,2,1,0:T(8,128)(2,1)} %get-tuple-element.52), channel_id=1, source_target_pairs={{0,56},{8,32},{16,40},{24,48},{32,88},{40,64},{48,72},{56,80},{64,... | collective-permute-start | bytes 1572872 | tf_op jit(solution)/shard_map/documents/ppermute | solution.py:58
  43.8 35.9 %collective-permute-start.5 = (bf16[2,2,512,128]{3,2,1,0:T(8,128)(2,1)}, bf16[2,2,512,128]{3,2,1,0:T(8,128)(2,1)S(1)}, u32[]{:S(2)}, u32[]{:S(2)}) collective-permute-start(bf16[2,2,512,128]{3,2,1,0:T(8,128)(2,1)} %get-tuple-element.53), channel_id=1, source_target_pairs={{0,104},{8,112},{16,120},{24,96},{32,8},{40,16},{48,24},{56,0},{64... | collective-permute-start | bytes 1572872 | tf_op jit(solution)/shard_map/documents/ppermute | solution.py:58
  58.3 26.0 %collective-permute-start.10 = (bf16[2,2,512,128]{3,2,1,0:T(8,128)(2,1)S(1)}, bf16[2,2,512,128]{3,2,1,0:T(8,128)(2,1)S(1)}, u32[]{:S(2)}, u32[]{:S(2)}) collective-permute-start(bf16[2,2,512,128]{3,2,1,0:T(8,128)(2,1)S(1)} %copy-done.15), channel_id=1, source_target_pairs={{0,80},{8,88},{16,64},{24,72},{32,112},{40,120},{48,96},{56,104},{... | collective-permute-start | bytes 1572872 | tf_op jit(solution)/shard_map/documents/ppermute | solution.py:58
  59.3 29.0 %collective-permute-start.6 = (bf16[2,2,512,128]{3,2,1,0:T(8,128)(2,1)S(1)}, bf16[2,2,512,128]{3,2,1,0:T(8,128)(2,1)S(1)}, u32[]{:S(2)}, u32[]{:S(2)}) collective-permute-start(bf16[2,2,512,128]{3,2,1,0:T(8,128)(2,1)S(1)} %copy-done.14), channel_id=1, source_target_pairs={{0,32},{8,40},{16,48},{24,56},{32,64},{40,72},{48,80},{56,88},{64,... | collective-permute-start | bytes 1572872 | tf_op jit(solution)/shard_map/documents/ppermute | solution.py:58
  61.5 32.9 %collective-permute-start.7 = (bf16[2,2,512,128]{3,2,1,0:T(8,128)(2,1)S(1)}, bf16[2,2,512,128]{3,2,1,0:T(8,128)(2,1)S(1)}, u32[]{:S(2)}, u32[]{:S(2)}) collective-permute-start(bf16[2,2,512,128]{3,2,1,0:T(8,128)(2,1)S(1)} %copy-done.13), channel_id=1, source_target_pairs={{0,96},{8,104},{16,112},{24,120},{32,0},{40,8},{48,16},{56,24},{64... | collective-permute-start | bytes 1572872 | tf_op jit(solution)/shard_map/documents/ppermute | solution.py:58
  69.1 27.6 %collective-permute-start.8 = (bf16[2,2,512,128]{3,2,1,0:T(8,128)(2,1)S(1)}, bf16[2,2,512,128]{3,2,1,0:T(8,128)(2,1)S(1)}, u32[]{:S(2)}, u32[]{:S(2)}) collective-permute-start(bf16[2,2,512,128]{3,2,1,0:T(8,128)(2,1)S(1)} %copy-done.12), channel_id=1, source_target_pairs={{0,8},{8,16},{16,24},{24,0},{32,40},{40,48},{48,56},{56,32},{64,72... | collective-permute-start | bytes 1572872 | tf_op jit(solution)/shard_map/documents/ppermute | solution.py:58
  79.7 22.9 %collective-permute-start.9 = (bf16[2,2,512,128]{3,2,1,0:T(8,128)(2,1)S(1)}, bf16[2,2,512,128]{3,2,1,0:T(8,128)(2,1)S(1)}, u32[]{:S(2)}, u32[]{:S(2)}) collective-permute-start(bf16[2,2,512,128]{3,2,1,0:T(8,128)(2,1)S(1)} %copy-done.11), channel_id=1, source_target_pairs={{0,24},{8,0},{16,8},{24,16},{32,56},{40,32},{48,40},{56,48},{64,88... | collective-permute-start | bytes 1572872 | tf_op jit(solution)/shard_map/documents/ppermute | solution.py:58
  84.3 25.3 %collective-permute-start.11 = (bf16[2,2,512,128]{3,2,1,0:T(8,128)(2,1)S(1)}, bf16[2,2,512,128]{3,2,1,0:T(8,128)(2,1)S(1)}, u32[]{:S(2)}, u32[]{:S(2)}) collective-permute-start(bf16[2,2,512,128]{3,2,1,0:T(8,128)(2,1)S(1)} %get-tuple-element.70), channel_id=1, source_target_pairs={{0,32},{8,40},{16,48},{24,56},{32,64},{40,72},{48,80},{56,88},{64,... | collective-permute-start | bytes 1572872 | tf_op jit(solution)/shard_map/documents/ppermute | solution.py:58
  88.3 21.3 %collective-permute-start.12 = (bf16[2,2,512,128]{3,2,1,0:T(8,128)(2,1)S(1)}, bf16[2,2,512,128]{3,2,1,0:T(8,128)(2,1)S(1)}, u32[]{:S(2)}, u32[]{:S(2)}) collective-permute-start(bf16[2,2,512,128]{3,2,1,0:T(8,128)(2,1)S(1)} %get-tuple-element.71), channel_id=1, source_target_pairs={{0,96},{8,104},{16,112},{24,120},{32,0},{40,8},{48,16},{56,24},{64... | collective-permute-start | bytes 1572872 | tf_op jit(solution)/shard_map/documents/ppermute | solution.py:58
  94.4 15.3 %collective-permute-start.13 = (bf16[2,2,512,128]{3,2,1,0:T(8,128)(2,1)S(1)}, bf16[2,2,512,128]{3,2,1,0:T(8,128)(2,1)S(1)}, u32[]{:S(2)}, u32[]{:S(2)}) collective-permute-start(bf16[2,2,512,128]{3,2,1,0:T(8,128)(2,1)S(1)} %get-tuple-element.72), channel_id=1, source_target_pairs={{0,8},{8,16},{16,24},{24,0},{32,40},{40,48},{48,56},{56,32},{64,72... | collective-permute-start | bytes 1572872 | tf_op jit(solution)/shard_map/documents/ppermute | solution.py:58
  96.6 13.0 %collective-permute-start.14 = (bf16[2,2,512,128]{3,2,1,0:T(8,128)(2,1)S(1)}, bf16[2,2,512,128]{3,2,1,0:T(8,128)(2,1)S(1)}, u32[]{:S(2)}, u32[]{:S(2)}) collective-permute-start(bf16[2,2,512,128]{3,2,1,0:T(8,128)(2,1)S(1)} %get-tuple-element.73), channel_id=1, source_target_pairs={{0,24},{8,0},{16,8},{24,16},{32,56},{40,32},{48,40},{56,48},{64,88... | collective-permute-start | bytes 1572872 | tf_op jit(solution)/shard_map/documents/ppermute | solution.py:58
  113.9 12.1 %collective-permute-start.15 = (bf16[640,512]{1,0:T(8,128)(2,1)}, bf16[640,512]{1,0:T(8,128)(2,1)S(1)}, u32[]{:S(2)}, u32[]{:S(2)}) collective-permute-start(bf16[640,512]{1,0:T(8,128)(2,1)} %get-tuple-element.74.refs_0_), channel_id=1, source_target_pairs={{0,2},{1,3},{2,4},{3,5},{4,6},{5,7},{6,0},{7,1},{8,10},{9,11},{10,... | collective-permute-start | bytes 1966088 | tf_op jit(solution)/shard_map/output/ppermute | solution.py:349
  115.7 18.9 %collective-permute-start.17 = (bf16[640,512]{1,0:T(8,128)(2,1)}, bf16[640,512]{1,0:T(8,128)(2,1)S(1)}, u32[]{:S(2)}, u32[]{:S(2)}) collective-permute-start(bf16[640,512]{1,0:T(8,128)(2,1)} %get-tuple-element.74.refs_0_), channel_id=1, source_target_pairs={{0,6},{1,7},{2,0},{3,1},{4,2},{5,3},{6,4},{7,5},{8,14},{9,15},{10,... | collective-permute-start | bytes 1966088 | tf_op jit(solution)/shard_map/output/ppermute | solution.py:349
  117.9 20.4 %collective-permute-start.19 = (bf16[640,512]{1,0:T(8,128)(2,1)}, bf16[640,512]{1,0:T(8,128)(2,1)S(1)}, u32[]{:S(2)}, u32[]{:S(2)}) collective-permute-start(bf16[640,512]{1,0:T(8,128)(2,1)} %get-tuple-element.74.refs_0_), channel_id=1, source_target_pairs={{0,1},{1,0},{2,3},{3,2},{4,5},{5,4},{6,7},{7,6},{8,9},{9,8},{10,11... | collective-permute-start | bytes 1966088 | tf_op jit(solution)/shard_map/output/ppermute | solution.py:353
  126.0 12.3 %collective-permute-start.20 = (bf16[640,512]{1,0:T(8,128)(2,1)S(1)}, bf16[640,512]{1,0:T(8,128)(2,1)}, u32[]{:S(2)}, u32[]{:S(2)}) collective-permute-start(bf16[640,512]{1,0:T(8,128)(2,1)S(1)} %collective-permute-done.15.refs_2_), channel_id=1, source_target_pairs={{0,1},{1,0},{2,3},{3,2},{4,5},{5,4},{6,7},{7,6},{8,9},{9,8},{10,11... | collective-permute-start | bytes 1966088 | tf_op jit(solution)/shard_map/output/ppermute | solution.py:353
  134.7 3.7 %collective-permute-start.21 = (bf16[640,512]{1,0:T(8,128)(2,1)S(1)}, bf16[640,512]{1,0:T(8,128)(2,1)}, u32[]{:S(2)}, u32[]{:S(2)}) collective-permute-start(bf16[640,512]{1,0:T(8,128)(2,1)S(1)} %collective-permute-done.17.refs_3_), channel_id=1, source_target_pairs={{0,1},{1,0},{2,3},{3,2},{4,5},{5,4},{6,7},{7,6},{8,9},{9,8},{10,11... | collective-permute-start | bytes 1966088 | tf_op jit(solution)/shard_map/output/ppermute | solution.py:353
  134.8 11.1 %collective-permute-start.16 = (bf16[320,512]{1,0:T(8,128)(2,1)S(1)}, bf16[320,512]{1,0:T(8,128)(2,1)S(1)}, u32[]{:S(2)}, u32[]{:S(2)}) collective-permute-start(bf16[320,512]{1,0:T(8,128)(2,1)S(1)} %slice.28), channel_id=1, source_target_pairs={{0,2},{1,3},{2,4},{3,5},{4,6},{5,7},{6,0},{7,1},{8,10},{9,11},{10,... | collective-permute-start | bytes 983048 | tf_op jit(solution)/shard_map/output/ppermute | solution.py:349
  136.7 9.2 %collective-permute-start.18 = (bf16[320,512]{1,0:T(8,128)(2,1)S(1)}, bf16[320,512]{1,0:T(8,128)(2,1)S(1)}, u32[]{:S(2)}, u32[]{:S(2)}) collective-permute-start(bf16[320,512]{1,0:T(8,128)(2,1)S(1)} %slice.29), channel_id=1, source_target_pairs={{0,6},{1,7},{2,0},{3,1},{4,2},{5,3},{6,4},{7,5},{8,14},{9,15},{10,... | collective-permute-start | bytes 983048 | tf_op jit(solution)/shard_map/output/ppermute | solution.py:349
  145.8 2.3 %collective-permute-start.22 = (bf16[320,512]{1,0:T(8,128)(2,1)S(1)}, bf16[320,512]{1,0:T(8,128)(2,1)S(1)}, u32[]{:S(2)}, u32[]{:S(2)}) collective-permute-start(bf16[320,512]{1,0:T(8,128)(2,1)S(1)} %collective-permute-done.16.refs_0_), channel_id=1, source_target_pairs={{0,1},{1,0},{2,3},{3,2},{4,5},{5,4},{6,7},{7,6},{8,9},{9,8},{10,11... | collective-permute-start | bytes 983048 | tf_op jit(solution)/shard_map/output/ppermute | solution.py:353
  146.9 1.7 %collective-permute-start.23 = (bf16[320,512]{1,0:T(8,128)(2,1)S(1)}, bf16[320,512]{1,0:T(8,128)(2,1)S(1)}, u32[]{:S(2)}, u32[]{:S(2)}) collective-permute-start(bf16[320,512]{1,0:T(8,128)(2,1)S(1)} %collective-permute-done.18.refs_1_), channel_id=1, source_target_pairs={{0,1},{1,0},{2,3},{3,2},{4,5},{5,4},{6,7},{7,6},{8,9},{9,8},{10,11... | collective-permute-start | bytes 983048 | tf_op jit(solution)/shard_map/output/ppermute | solution.py:353
  (16 other events, 204.9 us)

commit v6 on v5

--- a/solution.py
+++ b/solution.py
@@ -17,6 +17,7 @@
 GROUPS = 16
 STORED = 16
 SLOTS = 16
+SERVED = 2
 PICK = 40
 DOC = 512
 TOKENS = 320
@@ -101,7 +102,7 @@
     def outgoing(g, carry):
         one, two = jnp.int32(-1), jnp.int32(-1)
         for i in range(SLOTS):
-            slot = home_ref[ids_ref[g * SLOTS + i]] - me * STORED
+            slot = home_ref[ids_ref[i % RETRIEVED, g * SERVED + i // RETRIEVED]] - me * STORED
             hit = (slot >= 0) & (slot < STORED)
             two = jnp.where(hit, one, two)
             one = jnp.where(hit, slot, one)
@@ -119,7 +120,7 @@
         for at in range(GROUPS * CAP):
             table_ref[at] = jnp.int32(-1)
         for i in range(SLOTS):
-            doc = ids_ref[me * SLOTS + i]
+            doc = ids_ref[i % RETRIEVED, me * SERVED + i // RETRIEVED]
             location = home_ref[doc]
             at = location // STORED * CAP
             table_ref[at + jnp.where(table_ref[at] >= 0, 1, 0)] = jnp.int32(i)
@@ -370,7 +371,7 @@
     served = sel_hidden.shape[0]
 
     with jax.named_scope("pack"):
-        scalars = [me, home, doc_ids.reshape(-1), doc_len]
+        scalars = [me, home, doc_ids.T, doc_len]
         *early, table = pack(first_pack_kernel, EARLY, scalars, doc_cache, True)
         late = list(pack(second_pack_kernel, LATE, [table], doc_cache, False))
         packed = {b[0]: p for b, p in zip(EARLY + LATE, early + late)}
@@ -433,8 +434,9 @@
         through = (0, 2) if s[1] == 2 else (2, 0)
         at = CAP * CARRIED[through].index(s)
         blocks.append(arrived[through][at : at + CAP])
-    send(KNIGHT, after(blocks, [arrived[s] for s in DIAGONAL], state), NEAR)
+    send(KNIGHT[:1], after(blocks[:1], [arrived[s] for s in DIAGONAL], state), NEAR[:1])
     state = attention(2, state)
+    send(KNIGHT[1:], after(blocks[1:], state), NEAR[1:])
     state = attention(3, state)
     own = attention(len(STAGES) - 1, state)[-1]
 

time: 151 us -> 148 us (0.980)
  the two profiles are of different devices: /device:TPU:1 before, /device:TPU:17 now
where the time goes in v6:
time: 148 us; the launch traced here: 146 us
  starting transfers between devices  43.8 us (30%)
  waiting for transfers between devices  41.9 us (28%)
  Pallas kernels  39.4 us (27%)
  other arithmetic  8.15 us (6%)
  local copies, waits for them, and re-layouts  6.18 us (4%)
  matrix products  5.91 us (4%)
    ppermute x15, waiting for transfers between devices, shift(): return lax.ppermute(block, 'grp', pairs)  35.8 us
    pallas_call x5, Pallas kernels, attend(): pl.pallas_call(functools.partial(attend_kernel, shifts, count, first, las...  25.5 us
    ppermute x15, starting transfers between devices, shift(): return lax.ppermute(block, 'grp', pairs)  23.5 us
    ppermute x5, starting transfers between devices, other_core(): return lax.ppermute(block, 'tp', [(i, i ^ 1) for i in range(KVH)])  13.7 us
    pallas_call x2, Pallas kernels, pack(): pl.pallas_call(kernel, out_shape=[jax.ShapeDtypeStruct(s, jnp.bfloat16) f...  7.83 us
    ppermute x4, starting transfers between devices, ring(): lax.ppermute(block, 'tp', [(i, (i + 2 * by) % KVH) for i in range(KVH)])  6.64 us
    pallas_call x2, Pallas kernels, project(): pl.pallas_call(functools.partial(project_kernel, spans, last), out_shape=...  6.06 us
    dot_general x3, matrix products, dot(): out = jnp.dot(normed_rows, w, preferred_element_type=jnp.float32)  5.91 us
  transfers between devices with their start and end apart: 24, of which 9 were waited for; matrix products, arithmetic and copies ran while one was open for 12% of the time, Pallas kernels for 17%

profile of v6, /device:TPU:17, one launch (start us, length us, event | category | flops | bytes accessed | tf_op | source)
XLA Modules:
  0.0 145.7 jit_solution(8766767616923168694)
XLA Ops:
  0.0 4.2 %pack.2 = (bf16[6,2,512,128]{3,2,1,0:T(8,128)(2,1)}, bf16[6,2,512,128]{3,2,1,0:T(8,128)(2,1)}, s32[97]{0:T(128)}) custom-call(s32[1]{0:T(128)} %bitcast.4.me_ref, s32[256]{0:T(256)} %home_ref.1, s32[8,32]{1,0:T(8,128)} %bitcast.27, s32[256]{0:T(256)} %len_ref.1, bf16[16,2,512,128]{3,2,1,0:T(8,128)(2,1)} %cache_ref.3), custom_call_target="tpu_custom_call" | custom-call | bytes 5242880 | tf_op jit(solution)/shard_map/pack/pack/pallas_call | solution.py:142
  4.3 2.8 %collective-permute-start = (bf16[6,2,512,128]{3,2,1,0:T(8,128)(2,1)}, bf16[6,2,512,128]{3,2,1,0:T(8,128)(2,1)}, u32[]{:S(2)}, u32[]{:S(2)}) collective-permute-start(bf16[6,2,512,128]{3,2,1,0:T(8,128)(2,1)} %get-tuple-element.45), channel_id=1, source_target_pairs={{0,64},{8,72},{16,80},{24,88},{32,96},{40,104},{48,112},{56,120},{... | collective-permute-start | bytes 4718600 | tf_op jit(solution)/shard_map/documents/ppermute | solution.py:59
  7.1 3.6 %pack.3 = (bf16[2,2,512,128]{3,2,1,0:T(8,128)(2,1)}, bf16[2,2,512,128]{3,2,1,0:T(8,128)(2,1)}, bf16[2,2,512,128]{3,2,1,0:T(8,128)(2,1)}, bf16[2,2,512,128]{3,2,1...) custom-call(s32[97]{0:T(128)} %get-tuple-element.41.refs_0_.table_re, ...), custom_call_target="tpu_custom_call" | custom-call | bytes 5242880 | tf_op jit(solution)/shard_map/pack/pack/pallas_call | solution.py:142
  10.7 2.6 %collective-permute-start.2 = (bf16[2,2,512,128]{3,2,1,0:T(8,128)(2,1)}, bf16[2,2,512,128]{3,2,1,0:T(8,128)(2,1)S(1)}, u32[]{:S(2)}, u32[]{:S(2)}) collective-permute-start(bf16[2,2,512,128]{3,2,1,0:T(8,128)(2,1)} %get-tuple-element.50), channel_id=1, source_target_pairs={{0,40},{8,48},{16,56},{24,32},{32,72},{40,80},{48,88},{56,64},{64,... | collective-permute-start | bytes 1572872 | tf_op jit(solution)/shard_map/documents/ppermute | solution.py:59
  16.0 3.6 %fusion = f32[2,320]{1,0:T(2,128)S(1)} fusion(bf16[2,320,4096]{2,1,0:T(8,128)(2,1)} %param.11), kind=kLoop, calls=%fused_computation.2 | loop fusion | flops 7863680 | bytes 5245440 | tf_op jit(solution)/shard_map/projections/reduce_sum | solution.py:390
  20.4 4.4 %fusion.2 = bf16[2,320,4096]{2,1,0:T(8,128)(2,1)S(1)} fusion(bf16[2,320,4096]{2,1,0:T(8,128)(2,1)} %param.11, f32[4096]{0:T(1024)S(1)} %copy-done.5, f32[2,320]{1,0:T(2,128)S(1)} %add_rsqrt_fusion), kind=kLoop, calls=%fused_computation.4 | loop fusion | flops 10485760 | bytes 10504704 | tf_op jit(solution)/shard_map/projections/convert_element_type | solution.py:391
  28.6 2.9 %convolution_convert_fusion = bf16[640,512]{1,0:T(8,128)(2,1)S(1)} fusion(bf16[640,4096]{1,0:T(8,128)(2,1)S(1)} %bitcast.24, bf16[4096,512]{1,0:T(8,128)(2,1)S(1)} %copy-done.7), kind=kOutput, calls=%fused_computation.5 | convolution fusion | flops 2684682240 | bytes 10092544 | tf_op jit(solution)/shard_map/projections/dot_general | solution.py:395
  31.5 4.1 %attend.5 = (f32[2,4,320,128]{3,2,1,0:T(8,128)S(1)}, f32[2,4,320,128]{3,2,1,0:T(8,128)S(1)}, f32[2,4,320,128]{3,2,1,0:T(8,128)S(1)}) custom-call(s32[97]{0:T(128)S(1)} %copy-done.4, bf16[2,320,512]{2,1,0:T(8,128)(2,1)S(1)} %bitcast.17, s32[2,4,320,1]{3,2,1,0:T(8,128)S(1)} %reshape.43.refs_2_, s32[2,1,384]{2,1,0:T(1,128)S(1)} %reshape.39.refs_3_, ...), custom_call_target="tpu_custom_call" | custom-call | flops 335544320 | bytes 8650752 | tf_op jit(solution)/shard_map/attention/attend/pallas_call | solution.py:289
  35.6 5.8 %collective-permute-done.refs_6_ = bf16[6,2,512,128]{3,2,1,0:T(8,128)(2,1)} collective-permute-done((bf16[6,2,512,128]{3,2,1,0:T(8,128)(2,1)}, bf16[6,2,512,128]{3,2,1,0:T(8,128)(2,1)}, u32[]{:S(2)}, u32[]{:S(2)}) %collective-permute-start) | collective-permute-done | bytes 1572896 | tf_op jit(solution)/shard_map/documents/ppermute | solution.py:59
  41.5 3.3 %collective-permute-start.5 = (bf16[2,2,512,128]{3,2,1,0:T(8,128)(2,1)S(1)}, bf16[2,2,512,128]{3,2,1,0:T(8,128)(2,1)S(1)}, u32[]{:S(2)}, u32[]{:S(2)}) collective-permute-start(bf16[2,2,512,128]{3,2,1,0:T(8,128)(2,1)S(1)} %copy-done.14), channel_id=1, source_target_pairs={{0,104},{8,112},{16,120},{24,96},{32,8},{40,16},{48,24},{56,0},{64... | collective-permute-start | bytes 1572872 | tf_op jit(solution)/shard_map/documents/ppermute | solution.py:59
  44.7 20.9 %collective-permute-done.1.refs_7_ = bf16[6,2,512,128]{3,2,1,0:T(8,128)(2,1)} collective-permute-done((bf16[6,2,512,128]{3,2,1,0:T(8,128)(2,1)}, bf16[6,2,512,128]{3,2,1,0:T(8,128)(2,1)}, u32[]{:S(2)}, u32[]{:S(2)}) %collective-permute-start.1) | collective-permute-done | bytes 1572896 | tf_op jit(solution)/shard_map/documents/ppermute | solution.py:59
  65.7 2.6 %collective-permute-start.7 = (bf16[2,2,512,128]{3,2,1,0:T(8,128)(2,1)S(1)}, bf16[2,2,512,128]{3,2,1,0:T(8,128)(2,1)S(1)}, u32[]{:S(2)}, u32[]{:S(2)}) collective-permute-start(bf16[2,2,512,128]{3,2,1,0:T(8,128)(2,1)S(1)} %copy-done.11), channel_id=1, source_target_pairs={{0,96},{8,104},{16,112},{24,120},{32,0},{40,8},{48,16},{56,24},{64... | collective-permute-start | bytes 1572872 | tf_op jit(solution)/shard_map/documents/ppermute | solution.py:59
  73.0 5.2 %attend.6 = (f32[2,4,320,128]{3,2,1,0:T(8,128)S(1)}, f32[2,4,320,128]{3,2,1,0:T(8,128)S(1)}, f32[2,4,320,128]{3,2,1,0:T(8,128)S(1)}) custom-call(s32[97]{0:T(128)S(1)} %copy-done.4, bf16[2,320,512]{2,1,0:T(8,128)(2,1)S(1)} %bitcast.18, s32[2,4,320,1]{3,2,1,0:T(8,128)S(1)} %reshape.43.refs_2_, ...), custom_call_target="tpu_custom_call", output_to_operand_aliasing={{0}: (3, {}), {1}: (4, {}), {2}: (5, {})} | custom-call | flops 671088640 | bytes 8912896 | tf_op jit(solution)/shard_map/attention/attend/pallas_call | solution.py:289
  78.2 3.9 %attend.7 = (f32[2,4,320,128]{3,2,1,0:T(8,128)S(1)}, f32[2,4,320,128]{3,2,1,0:T(8,128)S(1)}, f32[2,4,320,128]{3,2,1,0:T(8,128)S(1)}) custom-call(s32[97]{0:T(128)S(1)} %copy-done.4, bf16[2,320,512]{2,1,0:T(8,128)(2,1)S(1)} %bitcast.19, s32[2,4,320,1]{3,2,1,0:T(8,128)S(1)} %reshape.43.refs_2_, ...), custom_call_target="tpu_custom_call", output_to_operand_aliasing={{0}: (3, {}), {1}: (4, {}), {2}: (5, {})} | custom-call | flops 1342177280 | bytes 9437184 | tf_op jit(solution)/shard_map/attention/attend/pallas_call | solution.py:289
  82.1 5.8 %collective-permute-start.12 = (bf16[2,2,512,128]{3,2,1,0:T(8,128)(2,1)S(1)}, bf16[2,2,512,128]{3,2,1,0:T(8,128)(2,1)S(1)}, u32[]{:S(2)}, u32[]{:S(2)}) collective-permute-start(bf16[2,2,512,128]{3,2,1,0:T(8,128)(2,1)S(1)} %get-tuple-element.71), channel_id=1, source_target_pairs={{0,96},{8,104},{16,112},{24,120},{32,0},{40,8},{48,16},{56,24},{64... | collective-permute-start | bytes 1572872 | tf_op jit(solution)/shard_map/documents/ppermute | solution.py:59
  91.9 4.7 %attend.8 = (f32[2,4,320,128]{3,2,1,0:T(8,128)S(1)}, f32[2,4,320,128]{3,2,1,0:T(8,128)S(1)}, f32[2,4,320,128]{3,2,1,0:T(8,128)S(1)}) custom-call(s32[97]{0:T(128)S(1)} %copy-done.4, bf16[2,320,512]{2,1,0:T(8,128)(2,1)S(1)} %bitcast.20, s32[2,4,320,1]{3,2,1,0:T(8,128)S(1)} %reshape.43.refs_2_, ...), custom_call_target="tpu_custom_call", output_to_operand_aliasing={{0}: (3, {}), {1}: (4, {}), {2}: (5, {})} | custom-call | flops 1677721600 | bytes 9699328 | tf_op jit(solution)/shard_map/attention/attend/pallas_call | solution.py:289
  96.6 6.6 %collective-permute-done.13.refs_8_ = bf16[2,2,512,128]{3,2,1,0:T(8,128)(2,1)S(1)} collective-permute-done((bf16[2,2,512,128]{3,2,1,0:T(8,128)(2,1)S(1)}, bf16[2,2,512,128]{3,2,1,0:T(8,128)(2,1)S(1)}, u32[]{:S(2)}, u32[]{:S(2)}) %collective-permute-start.13) | collective-permute-done | bytes 524320 | tf_op jit(solution)/shard_map/documents/ppermute | solution.py:59
  103.3 7.5 %attend.9 = (f32[2,4,320,128]{3,2,1,0:T(8,128)S(1)}, f32[2,4,320,128]{3,2,1,0:T(8,128)S(1)}, f32[2,4,320,128]{3,2,1,0:T(8,128)S(1)}, bf16[640,512]{1,0:T(8,128)(2,1)S(1)}) custom-call(s32[97]{0:T(128)S(1)} %copy-done.4, bf16[2,320,512]{2,1,0:T(8,128)(2,1)S(1)} %bitcast.21, ...), custom_call_target="tpu_custom_call", output_to_operand_aliasing={{0}: (3, {}), {1}: (4, {}), {2}: (5, {})} | custom-call | flops 1342177280 | bytes 9437184 | tf_op jit(solution)/shard_map/attention/attend/pallas_call | solution.py:289
  112.4 2.2 %collective-permute-start.17 = (bf16[640,512]{1,0:T(8,128)(2,1)S(1)}, bf16[640,512]{1,0:T(8,128)(2,1)S(1)}, u32[]{:S(2)}, u32[]{:S(2)}) collective-permute-start(bf16[640,512]{1,0:T(8,128)(2,1)S(1)} %get-tuple-element.74.refs_0_), channel_id=1, source_target_pairs={{0,6},{1,7},{2,0},{3,1},{4,2},{5,3},{6,4},{7,5},{8,14},{9,15},{10,... | collective-permute-start | bytes 1966088 | tf_op jit(solution)/shard_map/output/ppermute | solution.py:350
  114.6 6.0 %collective-permute-start.19 = (bf16[640,512]{1,0:T(8,128)(2,1)S(1)}, bf16[640,512]{1,0:T(8,128)(2,1)}, u32[]{:S(2)}, u32[]{:S(2)}) collective-permute-start(bf16[640,512]{1,0:T(8,128)(2,1)S(1)} %get-tuple-element.74.refs_0_), channel_id=1, source_target_pairs={{0,1},{1,0},{2,3},{3,2},{4,5},{5,4},{6,7},{7,6},{8,9},{9,8},{10,11... | collective-permute-start | bytes 1966088 | tf_op jit(solution)/shard_map/output/ppermute | solution.py:354
  120.6 3.2 %collective-permute-done.15.refs_2_ = bf16[640,512]{1,0:T(8,128)(2,1)S(1)} collective-permute-done((bf16[640,512]{1,0:T(8,128)(2,1)S(1)}, bf16[640,512]{1,0:T(8,128)(2,1)S(1)}, u32[]{:S(2)}, u32[]{:S(2)}) %collective-permute-start.15) | collective-permute-done | bytes 655392 | tf_op jit(solution)/shard_map/output/ppermute | solution.py:350
  123.8 6.4 %collective-permute-start.20 = (bf16[640,512]{1,0:T(8,128)(2,1)S(1)}, bf16[640,512]{1,0:T(8,128)(2,1)}, u32[]{:S(2)}, u32[]{:S(2)}) collective-permute-start(bf16[640,512]{1,0:T(8,128)(2,1)S(1)} %collective-permute-done.15.refs_2_), channel_id=1, source_target_pairs={{0,1},{1,0},{2,3},{3,2},{4,5},{5,4},{6,7},{7,6},{8,9},{9,8},{10,11... | collective-permute-start | bytes 1966088 | tf_op jit(solution)/shard_map/output/ppermute | solution.py:354
  135.5 3.8 %project.2.refs_4_ = f32[640,512]{1,0:T(8,128)S(1)} custom-call(s32[8]{0:T(128)S(1)} %pad_add_fusion.place_ref, bf16[4096,512]{1,0:T(8,128)(2,1)S(1)} %copy-done.2, bf16[640,512]{1,0:T(8,128)(2,1)S(1)} %get-tuple-element.74.refs_0_, bf16[640,512]{1,0:T(8,128)(2,1)} %collective-permute-done.19.refs_1_, bf16[640,512]{1,0:T(8,128)(2,1)S(1)} %collective-permute-done.15.refs_2_, ...), custom_call_target="tpu_custom_call" | custom-call | flops 2013265920 | bytes 6291456 | tf_op jit(solution)/shard_map/output/project/pallas_call | solution.py:336
  143.5 2.2 %project.3 = bf16[640,512]{1,0:T(8,128)(2,1)} custom-call(s32[8]{0:T(128)S(1)} %pad_add_fusion.place_ref, bf16[4096,512]{1,0:T(8,128)(2,1)S(1)} %copy-done.3, bf16[320,512]{1,0:T(8,128)(2,1)S(1)} %collective-permute-done.16.refs_0_, bf16[320,512]{1,0:T(8,128)(2,1)S(1)} %collective-permute-done.18.refs_1_, ...), custom_call_target="tpu_custom_call" | custom-call | flops 671088640 | bytes 2097152 | tf_op jit(solution)/shard_map/output/project/pallas_call | solution.py:336
  (83 shorter events, 26.9 us)
Async XLA Ops:
  4.3 37.2 %collective-permute-start = (bf16[6,2,512,128]{3,2,1,0:T(8,128)(2,1)}, bf16[6,2,512,128]{3,2,1,0:T(8,128)(2,1)}, u32[]{:S(2)}, u32[]{:S(2)}) collective-permute-start(bf16[6,2,512,128]{3,2,1,0:T(8,128)(2,1)} %get-tuple-element.45), channel_id=1, source_target_pairs={{0,64},{8,72},{16,80},{24,88},{32,96},{40,104},{48,112},{56,120},{... | collective-permute-start | bytes 4718600 | tf_op jit(solution)/shard_map/documents/ppermute | solution.py:59
  7.1 58.5 %collective-permute-start.1 = (bf16[6,2,512,128]{3,2,1,0:T(8,128)(2,1)}, bf16[6,2,512,128]{3,2,1,0:T(8,128)(2,1)}, u32[]{:S(2)}, u32[]{:S(2)}) collective-permute-start(bf16[6,2,512,128]{3,2,1,0:T(8,128)(2,1)} %get-tuple-element.46), channel_id=1, source_target_pairs={{0,16},{8,24},{16,0},{24,8},{32,48},{40,56},{48,32},{56,40},{64,80... | collective-permute-start | bytes 4718600 | tf_op jit(solution)/shard_map/documents/ppermute | solution.py:59
  10.7 55.0 %collective-permute-start.2 = (bf16[2,2,512,128]{3,2,1,0:T(8,128)(2,1)}, bf16[2,2,512,128]{3,2,1,0:T(8,128)(2,1)S(1)}, u32[]{:S(2)}, u32[]{:S(2)}) collective-permute-start(bf16[2,2,512,128]{3,2,1,0:T(8,128)(2,1)} %get-tuple-element.50), channel_id=1, source_target_pairs={{0,40},{8,48},{16,56},{24,32},{32,72},{40,80},{48,88},{56,64},{64,... | collective-permute-start | bytes 1572872 | tf_op jit(solution)/shard_map/documents/ppermute | solution.py:59
  13.2 52.5 %collective-permute-start.3 = (bf16[2,2,512,128]{3,2,1,0:T(8,128)(2,1)}, bf16[2,2,512,128]{3,2,1,0:T(8,128)(2,1)S(1)}, u32[]{:S(2)}, u32[]{:S(2)}) collective-permute-start(bf16[2,2,512,128]{3,2,1,0:T(8,128)(2,1)} %get-tuple-element.51), channel_id=1, source_target_pairs={{0,120},{8,96},{16,104},{24,112},{32,24},{40,0},{48,8},{56,16},{64... | collective-permute-start | bytes 1572872 | tf_op jit(solution)/shard_map/documents/ppermute | solution.py:59
  14.3 54.1 %collective-permute-start.4 = (bf16[2,2,512,128]{3,2,1,0:T(8,128)(2,1)}, bf16[2,2,512,128]{3,2,1,0:T(8,128)(2,1)}, u32[]{:S(2)}, u32[]{:S(2)}) collective-permute-start(bf16[2,2,512,128]{3,2,1,0:T(8,128)(2,1)} %get-tuple-element.52), channel_id=1, source_target_pairs={{0,56},{8,32},{16,40},{24,48},{32,88},{40,64},{48,72},{56,80},{64,... | collective-permute-start | bytes 1572872 | tf_op jit(solution)/shard_map/documents/ppermute | solution.py:59
  41.5 31.5 %collective-permute-start.5 = (bf16[2,2,512,128]{3,2,1,0:T(8,128)(2,1)S(1)}, bf16[2,2,512,128]{3,2,1,0:T(8,128)(2,1)S(1)}, u32[]{:S(2)}, u32[]{:S(2)}) collective-permute-start(bf16[2,2,512,128]{3,2,1,0:T(8,128)(2,1)S(1)} %copy-done.14), channel_id=1, source_target_pairs={{0,104},{8,112},{16,120},{24,96},{32,8},{40,16},{48,24},{56,0},{64... | collective-permute-start | bytes 1572872 | tf_op jit(solution)/shard_map/documents/ppermute | solution.py:59
  65.6 16.5 %collective-permute-start.10 = (bf16[2,2,512,128]{3,2,1,0:T(8,128)(2,1)S(1)}, bf16[2,2,512,128]{3,2,1,0:T(8,128)(2,1)S(1)}, u32[]{:S(2)}, u32[]{:S(2)}) collective-permute-start(bf16[2,2,512,128]{3,2,1,0:T(8,128)(2,1)S(1)} %copy-done.13), channel_id=1, source_target_pairs={{0,80},{8,88},{16,64},{24,72},{32,112},{40,120},{48,96},{56,104},{... | collective-permute-start | bytes 1572872 | tf_op jit(solution)/shard_map/documents/ppermute | solution.py:59
  65.6 23.9 %collective-permute-start.6 = (bf16[2,2,512,128]{3,2,1,0:T(8,128)(2,1)S(1)}, bf16[2,2,512,128]{3,2,1,0:T(8,128)(2,1)S(1)}, u32[]{:S(2)}, u32[]{:S(2)}) collective-permute-start(bf16[2,2,512,128]{3,2,1,0:T(8,128)(2,1)S(1)} %copy-done.12), channel_id=1, source_target_pairs={{0,32},{8,40},{16,48},{24,56},{32,64},{40,72},{48,80},{56,88},{64,... | collective-permute-start | bytes 1572872 | tf_op jit(solution)/shard_map/documents/ppermute | solution.py:59
  65.7 23.8 %collective-permute-start.7 = (bf16[2,2,512,128]{3,2,1,0:T(8,128)(2,1)S(1)}, bf16[2,2,512,128]{3,2,1,0:T(8,128)(2,1)S(1)}, u32[]{:S(2)}, u32[]{:S(2)}) collective-permute-start(bf16[2,2,512,128]{3,2,1,0:T(8,128)(2,1)S(1)} %copy-done.11), channel_id=1, source_target_pairs={{0,96},{8,104},{16,112},{24,120},{32,0},{40,8},{48,16},{56,24},{64... | collective-permute-start | bytes 1572872 | tf_op jit(solution)/shard_map/documents/ppermute | solution.py:59
  68.4 23.5 %collective-permute-start.8 = (bf16[2,2,512,128]{3,2,1,0:T(8,128)(2,1)S(1)}, bf16[2,2,512,128]{3,2,1,0:T(8,128)(2,1)S(1)}, u32[]{:S(2)}, u32[]{:S(2)}) collective-permute-start(bf16[2,2,512,128]{3,2,1,0:T(8,128)(2,1)S(1)} %copy-done.10), channel_id=1, source_target_pairs={{0,8},{8,16},{16,24},{24,0},{32,40},{40,48},{48,56},{56,32},{64,72... | collective-permute-start | bytes 1572872 | tf_op jit(solution)/shard_map/documents/ppermute | solution.py:59
  72.9 18.9 %collective-permute-start.9 = (bf16[2,2,512,128]{3,2,1,0:T(8,128)(2,1)S(1)}, bf16[2,2,512,128]{3,2,1,0:T(8,128)(2,1)S(1)}, u32[]{:S(2)}, u32[]{:S(2)}) collective-permute-start(bf16[2,2,512,128]{3,2,1,0:T(8,128)(2,1)S(1)} %copy-done.9), channel_id=1, source_target_pairs={{0,24},{8,0},{16,8},{24,16},{32,56},{40,32},{48,40},{56,48},{64,88... | collective-permute-start | bytes 1572872 | tf_op jit(solution)/shard_map/documents/ppermute | solution.py:59
  82.1 14.5 %collective-permute-start.12 = (bf16[2,2,512,128]{3,2,1,0:T(8,128)(2,1)S(1)}, bf16[2,2,512,128]{3,2,1,0:T(8,128)(2,1)S(1)}, u32[]{:S(2)}, u32[]{:S(2)}) collective-permute-start(bf16[2,2,512,128]{3,2,1,0:T(8,128)(2,1)S(1)} %get-tuple-element.71), channel_id=1, source_target_pairs={{0,96},{8,104},{16,112},{24,120},{32,0},{40,8},{48,16},{56,24},{64... | collective-permute-start | bytes 1572872 | tf_op jit(solution)/shard_map/documents/ppermute | solution.py:59
  89.5 13.7 %collective-permute-start.13 = (bf16[2,2,512,128]{3,2,1,0:T(8,128)(2,1)S(1)}, bf16[2,2,512,128]{3,2,1,0:T(8,128)(2,1)S(1)}, u32[]{:S(2)}, u32[]{:S(2)}) collective-permute-start(bf16[2,2,512,128]{3,2,1,0:T(8,128)(2,1)S(1)} %get-tuple-element.72), channel_id=1, source_target_pairs={{0,8},{8,16},{16,24},{24,0},{32,40},{40,48},{48,56},{56,32},{64,72... | collective-permute-start | bytes 1572872 | tf_op jit(solution)/shard_map/documents/ppermute | solution.py:59
  89.5 13.7 %collective-permute-start.14 = (bf16[2,2,512,128]{3,2,1,0:T(8,128)(2,1)S(1)}, bf16[2,2,512,128]{3,2,1,0:T(8,128)(2,1)S(1)}, u32[]{:S(2)}, u32[]{:S(2)}) collective-permute-start(bf16[2,2,512,128]{3,2,1,0:T(8,128)(2,1)S(1)} %get-tuple-element.73), channel_id=1, source_target_pairs={{0,24},{8,0},{16,8},{24,16},{32,56},{40,32},{48,40},{56,48},{64,88... | collective-permute-start | bytes 1572872 | tf_op jit(solution)/shard_map/documents/ppermute | solution.py:59
  91.9 11.4 %collective-permute-start.11 = (bf16[2,2,512,128]{3,2,1,0:T(8,128)(2,1)S(1)}, bf16[2,2,512,128]{3,2,1,0:T(8,128)(2,1)S(1)}, u32[]{:S(2)}, u32[]{:S(2)}) collective-permute-start(bf16[2,2,512,128]{3,2,1,0:T(8,128)(2,1)S(1)} %get-tuple-element.70), channel_id=1, source_target_pairs={{0,32},{8,40},{16,48},{24,56},{32,64},{40,72},{48,80},{56,88},{64,... | collective-permute-start | bytes 1572872 | tf_op jit(solution)/shard_map/documents/ppermute | solution.py:59
  110.8 13.0 %collective-permute-start.15 = (bf16[640,512]{1,0:T(8,128)(2,1)S(1)}, bf16[640,512]{1,0:T(8,128)(2,1)S(1)}, u32[]{:S(2)}, u32[]{:S(2)}) collective-permute-start(bf16[640,512]{1,0:T(8,128)(2,1)S(1)} %get-tuple-element.74.refs_0_), channel_id=1, source_target_pairs={{0,2},{1,3},{2,4},{3,5},{4,6},{5,7},{6,0},{7,1},{8,10},{9,11},{10,... | collective-permute-start | bytes 1966088 | tf_op jit(solution)/shard_map/output/ppermute | solution.py:350
  112.4 17.8 %collective-permute-start.17 = (bf16[640,512]{1,0:T(8,128)(2,1)S(1)}, bf16[640,512]{1,0:T(8,128)(2,1)S(1)}, u32[]{:S(2)}, u32[]{:S(2)}) collective-permute-start(bf16[640,512]{1,0:T(8,128)(2,1)S(1)} %get-tuple-element.74.refs_0_), channel_id=1, source_target_pairs={{0,6},{1,7},{2,0},{3,1},{4,2},{5,3},{6,4},{7,5},{8,14},{9,15},{10,... | collective-permute-start | bytes 1966088 | tf_op jit(solution)/shard_map/output/ppermute | solution.py:350
  114.6 18.7 %collective-permute-start.19 = (bf16[640,512]{1,0:T(8,128)(2,1)S(1)}, bf16[640,512]{1,0:T(8,128)(2,1)}, u32[]{:S(2)}, u32[]{:S(2)}) collective-permute-start(bf16[640,512]{1,0:T(8,128)(2,1)S(1)} %get-tuple-element.74.refs_0_), channel_id=1, source_target_pairs={{0,1},{1,0},{2,3},{3,2},{4,5},{5,4},{6,7},{7,6},{8,9},{9,8},{10,11... | collective-permute-start | bytes 1966088 | tf_op jit(solution)/shard_map/output/ppermute | solution.py:354
  123.8 9.5 %collective-permute-start.20 = (bf16[640,512]{1,0:T(8,128)(2,1)S(1)}, bf16[640,512]{1,0:T(8,128)(2,1)}, u32[]{:S(2)}, u32[]{:S(2)}) collective-permute-start(bf16[640,512]{1,0:T(8,128)(2,1)S(1)} %collective-permute-done.15.refs_2_), channel_id=1, source_target_pairs={{0,1},{1,0},{2,3},{3,2},{4,5},{5,4},{6,7},{7,6},{8,9},{9,8},{10,11... | collective-permute-start | bytes 1966088 | tf_op jit(solution)/shard_map/output/ppermute | solution.py:354
  130.2 3.1 %collective-permute-start.21 = (bf16[640,512]{1,0:T(8,128)(2,1)S(1)}, bf16[640,512]{1,0:T(8,128)(2,1)}, u32[]{:S(2)}, u32[]{:S(2)}) collective-permute-start(bf16[640,512]{1,0:T(8,128)(2,1)S(1)} %collective-permute-done.17.refs_3_), channel_id=1, source_target_pairs={{0,1},{1,0},{2,3},{3,2},{4,5},{5,4},{6,7},{7,6},{8,9},{9,8},{10,11... | collective-permute-start | bytes 1966088 | tf_op jit(solution)/shard_map/output/ppermute | solution.py:354
  130.3 10.2 %collective-permute-start.16 = (bf16[320,512]{1,0:T(8,128)(2,1)S(1)}, bf16[320,512]{1,0:T(8,128)(2,1)S(1)}, u32[]{:S(2)}, u32[]{:S(2)}) collective-permute-start(bf16[320,512]{1,0:T(8,128)(2,1)S(1)} %slice.28), channel_id=1, source_target_pairs={{0,2},{1,3},{2,4},{3,5},{4,6},{5,7},{6,0},{7,1},{8,10},{9,11},{10,... | collective-permute-start | bytes 983048 | tf_op jit(solution)/shard_map/output/ppermute | solution.py:350
  131.4 9.1 %collective-permute-start.18 = (bf16[320,512]{1,0:T(8,128)(2,1)S(1)}, bf16[320,512]{1,0:T(8,128)(2,1)S(1)}, u32[]{:S(2)}, u32[]{:S(2)}) collective-permute-start(bf16[320,512]{1,0:T(8,128)(2,1)S(1)} %slice.29), channel_id=1, source_target_pairs={{0,6},{1,7},{2,0},{3,1},{4,2},{5,3},{6,4},{7,5},{8,14},{9,15},{10,... | collective-permute-start | bytes 983048 | tf_op jit(solution)/shard_map/output/ppermute | solution.py:350
  140.5 2.5 %collective-permute-start.22 = (bf16[320,512]{1,0:T(8,128)(2,1)S(1)}, bf16[320,512]{1,0:T(8,128)(2,1)S(1)}, u32[]{:S(2)}, u32[]{:S(2)}) collective-permute-start(bf16[320,512]{1,0:T(8,128)(2,1)S(1)} %collective-permute-done.16.refs_0_), channel_id=1, source_target_pairs={{0,1},{1,0},{2,3},{3,2},{4,5},{5,4},{6,7},{7,6},{8,9},{9,8},{10,11... | collective-permute-start | bytes 983048 | tf_op jit(solution)/shard_map/output/ppermute | solution.py:354
  141.8 1.7 %collective-permute-start.23 = (bf16[320,512]{1,0:T(8,128)(2,1)S(1)}, bf16[320,512]{1,0:T(8,128)(2,1)S(1)}, u32[]{:S(2)}, u32[]{:S(2)}) collective-permute-start(bf16[320,512]{1,0:T(8,128)(2,1)S(1)} %collective-permute-done.18.refs_1_), channel_id=1, source_target_pairs={{0,1},{1,0},{2,3},{3,2},{4,5},{5,4},{6,7},{7,6},{8,9},{9,8},{10,11... | collective-permute-start | bytes 983048 | tf_op jit(solution)/shard_map/output/ppermute | solution.py:354
  (15 other events, 257.9 us)

commit v7 on v6

--- a/solution.py
+++ b/solution.py
@@ -38,7 +38,7 @@
 EARLY = [CARRIED[s] for s in TWO]
 LATE = [[s] for s in DIAGONAL + NEAR + OPPOSITE]
 CHOSEN = GROUPS * CAP + 2 * SLOTS
-STAGES = [[(0, 0)], TWO, DIAGONAL, NEAR + OPPOSITE, KNIGHT]
+STAGES = [[(0, 0)], DIAGONAL, TWO + NEAR + OPPOSITE, KNIGHT]
 JOINED = []
 ROOM = 24 << 20
 ALL_ROOM = 56 << 20
@@ -428,16 +428,15 @@
     state = attention(0, [new_index, key_new, value_new])
     now = NEAR + OPPOSITE
     send(now, after([packed[s] for s in now], [arrived[s] for s in TWO], state), now)
-    state = attention(1, state)
     blocks = []
     for s in KNIGHT:
         through = (0, 2) if s[1] == 2 else (2, 0)
         at = CAP * CARRIED[through].index(s)
         blocks.append(arrived[through][at : at + CAP])
     send(KNIGHT[:1], after(blocks[:1], [arrived[s] for s in DIAGONAL], state), NEAR[:1])
+    state = attention(1, state)
+    send(KNIGHT[1:], after(blocks[1:], state), NEAR[1:])
     state = attention(2, state)
-    send(KNIGHT[1:], after(blocks[1:], state), NEAR[1:])
-    state = attention(3, state)
     own = attention(len(STAGES) - 1, state)[-1]
 
     with jax.named_scope("output"):

time: 148 us -> 148 us (level)
  the two profiles are of different devices: /device:TPU:17 before, /device:TPU:1 now
where the time goes in v7:
time: 148 us; the launch traced here: 150 us
  waiting for transfers between devices  49.5 us (33%)
  starting transfers between devices  40.9 us (28%)
  Pallas kernels  39.4 us (27%)
  matrix products  9.36 us (6%)
  local copies, waits for them, and re-layouts  6.76 us (5%)
  other arithmetic  3.18 us (2%)
    ppermute x15, waiting for transfers between devices, shift(): return lax.ppermute(block, 'grp', pairs)  37.5 us
    ppermute x15, starting transfers between devices, shift(): return lax.ppermute(block, 'grp', pairs)  27.3 us
    pallas_call x4, Pallas kernels, attend(): pl.pallas_call(functools.partial(attend_kernel, shifts, count, first, las...  24.8 us
    ppermute x4, waiting for transfers between devices, ring(): lax.ppermute(block, 'tp', [(i, (i + 2 * by) % KVH) for i in range(KVH)])  10.3 us
    dot_general x3, matrix products, dot(): out = jnp.dot(normed_rows, w, preferred_element_type=jnp.float32)  9.36 us
    pallas_call x2, Pallas kernels, pack(): pl.pallas_call(kernel, out_shape=[jax.ShapeDtypeStruct(s, jnp.bfloat16) f...  8.54 us
    ppermute x5, starting transfers between devices, other_core(): return lax.ppermute(block, 'tp', [(i, i ^ 1) for i in range(KVH)])  8.07 us
    pallas_call x2, Pallas kernels, project(): pl.pallas_call(functools.partial(project_kernel, spans, last), out_shape=...  6.06 us
  transfers between devices with their start and end apart: 24, of which 12 were waited for; matrix products, arithmetic and copies ran while one was open for 11% of the time, Pallas kernels for 16%

profile of v7, /device:TPU:1, one launch (start us, length us, event | category | flops | bytes accessed | tf_op | source)
XLA Modules:
  0.0 149.5 jit_solution(3983169975936896663)
XLA Ops:
  0.0 4.6 %pack.2 = (bf16[6,2,512,128]{3,2,1,0:T(8,128)(2,1)}, bf16[6,2,512,128]{3,2,1,0:T(8,128)(2,1)}, s32[97]{0:T(128)}) custom-call(s32[1]{0:T(128)} %bitcast.4.me_ref, s32[256]{0:T(256)} %home_ref.1, s32[8,32]{1,0:T(8,128)} %bitcast.26, s32[256]{0:T(256)} %len_ref.1, bf16[16,2,512,128]{3,2,1,0:T(8,128)(2,1)} %cache_ref.3), custom_call_target="tpu_custom_call" | custom-call | bytes 5242880 | tf_op jit(solution)/shard_map/pack/pack/pallas_call | solution.py:142
  4.6 3.6 %collective-permute-start.4 = (bf16[6,2,512,128]{3,2,1,0:T(8,128)(2,1)}, bf16[6,2,512,128]{3,2,1,0:T(8,128)(2,1)}, u32[]{:S(2)}, u32[]{:S(2)}) collective-permute-start(bf16[6,2,512,128]{3,2,1,0:T(8,128)(2,1)} %get-tuple-element.49), channel_id=1, source_target_pairs={{0,64},{8,72},{16,80},{24,88},{32,96},{40,104},{48,112},{56,120},{... | collective-permute-start | bytes 4718600 | tf_op jit(solution)/shard_map/documents/ppermute | solution.py:59
  8.1 2.9 %collective-permute-start.5 = (bf16[6,2,512,128]{3,2,1,0:T(8,128)(2,1)}, bf16[6,2,512,128]{3,2,1,0:T(8,128)(2,1)}, u32[]{:S(2)}, u32[]{:S(2)}) collective-permute-start(bf16[6,2,512,128]{3,2,1,0:T(8,128)(2,1)} %get-tuple-element.50), channel_id=1, source_target_pairs={{0,16},{8,24},{16,0},{24,8},{32,48},{40,56},{48,32},{56,40},{64,80... | collective-permute-start | bytes 4718600 | tf_op jit(solution)/shard_map/documents/ppermute | solution.py:59
  11.1 4.0 %pack.3 = (bf16[2,2,512,128]{3,2,1,0:T(8,128)(2,1)}, bf16[2,2,512,128]{3,2,1,0:T(8,128)(2,1)}, bf16[2,2,512,128]{3,2,1,0:T(8,128)(2,1)}, bf16[2,2,512,128]{3,2,1...) custom-call(s32[97]{0:T(128)} %get-tuple-element.38.refs_0_.table_re, ...), custom_call_target="tpu_custom_call" | custom-call | bytes 5242880 | tf_op jit(solution)/shard_map/pack/pack/pallas_call | solution.py:142
  15.4 4.5 %collective-permute-start.1 = (bf16[2,2,512,128]{3,2,1,0:T(8,128)(2,1)}, bf16[2,2,512,128]{3,2,1,0:T(8,128)(2,1)}, u32[]{:S(2)}, u32[]{:S(2)}) collective-permute-start(bf16[2,2,512,128]{3,2,1,0:T(8,128)(2,1)} %get-tuple-element.43), channel_id=1, source_target_pairs={{0,120},{8,96},{16,104},{24,112},{32,24},{40,0},{48,8},{56,16},{64... | collective-permute-start | bytes 1572872 | tf_op jit(solution)/shard_map/documents/ppermute | solution.py:59
  23.2 2.9 %convolution_convert_fusion = bf16[640,512]{1,0:T(8,128)(2,1)S(1)} fusion(bf16[640,4096]{1,0:T(8,128)(2,1)S(1)} %bitcast.21, bf16[4096,512]{1,0:T(8,128)(2,1)S(1)} %copy-done.10), kind=kOutput, calls=%fused_computation.5 | convolution fusion | flops 2684682240 | bytes 10092544 | tf_op jit(solution)/shard_map/projections/dot_general | solution.py:395
  30.0 12.0 %collective-permute-done.4.refs_6_ = bf16[6,2,512,128]{3,2,1,0:T(8,128)(2,1)} collective-permute-done((bf16[6,2,512,128]{3,2,1,0:T(8,128)(2,1)}, bf16[6,2,512,128]{3,2,1,0:T(8,128)(2,1)}, u32[]{:S(2)}, u32[]{:S(2)}) %collective-permute-start.4) | collective-permute-done | bytes 1572896 | tf_op jit(solution)/shard_map/documents/ppermute | solution.py:59
  42.0 4.1 %collective-permute-start.3 = (bf16[2,2,512,128]{3,2,1,0:T(8,128)(2,1)}, bf16[2,2,512,128]{3,2,1,0:T(8,128)(2,1)S(1)}, u32[]{:S(2)}, u32[]{:S(2)}) collective-permute-start(bf16[2,2,512,128]{3,2,1,0:T(8,128)(2,1)} %get-tuple-element.45), channel_id=1, source_target_pairs={{0,104},{8,112},{16,120},{24,96},{32,8},{40,16},{48,24},{56,0},{64... | collective-permute-start | bytes 1572872 | tf_op jit(solution)/shard_map/documents/ppermute | solution.py:59
  46.1 4.3 %convolution_convert_fusion.1 = bf16[640,128]{1,0:T(8,128)(2,1)S(1)} fusion(bf16[640,4096]{1,0:T(8,128)(2,1)} %bitcast.23, bf16[4096,128]{1,0:T(8,128)(2,1)} %param.15), kind=kOutput, calls=%fused_computation.6 | convolution fusion | flops 671170560 | bytes 6455296 | tf_op jit(solution)/shard_map/projections/dot_general | solution.py:395
  50.6 4.9 %attend.4 = (f32[2,4,320,128]{3,2,1,0:T(8,128)S(1)}, f32[2,4,320,128]{3,2,1,0:T(8,128)S(1)}, f32[2,4,320,128]{3,2,1,0:T(8,128)S(1)}) custom-call(s32[97]{0:T(128)S(1)} %copy-done.4, bf16[2,320,512]{2,1,0:T(8,128)(2,1)S(1)} %bitcast.17, s32[2,4,320,1]{3,2,1,0:T(8,128)S(1)} %reshape.43.refs_2_, s32[2,1,384]{2,1,0:T(1,128)S(1)} %reshape.39.refs_3_, ...), custom_call_target="tpu_custom_call" | custom-call | flops 335544320 | bytes 8650752 | tf_op jit(solution)/shard_map/attention/attend/pallas_call | solution.py:289
  58.4 2.3 %collective-permute-start.6 = (bf16[2,2,512,128]{3,2,1,0:T(8,128)(2,1)S(1)}, bf16[2,2,512,128]{3,2,1,0:T(8,128)(2,1)S(1)}, u32[]{:S(2)}, u32[]{:S(2)}) collective-permute-start(bf16[2,2,512,128]{3,2,1,0:T(8,128)(2,1)S(1)} %copy-done.14), channel_id=1, source_target_pairs={{0,32},{8,40},{16,48},{24,56},{32,64},{40,72},{48,80},{56,88},{64,... | collective-permute-start | bytes 1572872 | tf_op jit(solution)/shard_map/documents/ppermute | solution.py:59
  61.1 6.6 %collective-permute-done.2.refs_8_ = bf16[2,2,512,128]{3,2,1,0:T(8,128)(2,1)} collective-permute-done((bf16[2,2,512,128]{3,2,1,0:T(8,128)(2,1)}, bf16[2,2,512,128]{3,2,1,0:T(8,128)(2,1)}, u32[]{:S(2)}, u32[]{:S(2)}) %collective-permute-start.2) | collective-permute-done | bytes 524320 | tf_op jit(solution)/shard_map/documents/ppermute | solution.py:59
  70.8 8.4 %collective-permute-done.3.refs_9_ = bf16[2,2,512,128]{3,2,1,0:T(8,128)(2,1)S(1)} collective-permute-done((bf16[2,2,512,128]{3,2,1,0:T(8,128)(2,1)}, bf16[2,2,512,128]{3,2,1,0:T(8,128)(2,1)S(1)}, u32[]{:S(2)}, u32[]{:S(2)}) %collective-permute-start.3) | collective-permute-done | bytes 524320 | tf_op jit(solution)/shard_map/documents/ppermute | solution.py:59
  79.2 6.4 %attend.5 = (f32[2,4,320,128]{3,2,1,0:T(8,128)S(1)}, f32[2,4,320,128]{3,2,1,0:T(8,128)S(1)}, f32[2,4,320,128]{3,2,1,0:T(8,128)S(1)}) custom-call(s32[97]{0:T(128)S(1)} %copy-done.4, bf16[2,320,512]{2,1,0:T(8,128)(2,1)S(1)} %bitcast.18, s32[2,4,320,1]{3,2,1,0:T(8,128)S(1)} %reshape.43.refs_2_, ...), custom_call_target="tpu_custom_call", output_to_operand_aliasing={{0}: (3, {}), {1}: (4, {}), {2}: (5, {})} | custom-call | flops 1342177280 | bytes 9437184 | tf_op jit(solution)/shard_map/attention/attend/pallas_call | solution.py:289
  89.8 3.5 %collective-permute-start.11 = (bf16[2,2,512,128]{3,2,1,0:T(8,128)(2,1)S(1)}, bf16[2,2,512,128]{3,2,1,0:T(8,128)(2,1)S(1)}, u32[]{:S(2)}, u32[]{:S(2)}) collective-permute-start(bf16[2,2,512,128]{3,2,1,0:T(8,128)(2,1)S(1)} %get-tuple-element.64), channel_id=1, source_target_pairs={{0,32},{8,40},{16,48},{24,56},{32,64},{40,72},{48,80},{56,88},{64,... | collective-permute-start | bytes 1572872 | tf_op jit(solution)/shard_map/documents/ppermute | solution.py:59
  95.3 4.7 %attend.6 = (f32[2,4,320,128]{3,2,1,0:T(8,128)S(1)}, f32[2,4,320,128]{3,2,1,0:T(8,128)S(1)}, f32[2,4,320,128]{3,2,1,0:T(8,128)S(1)}) custom-call(s32[97]{0:T(128)S(1)} %copy-done.4, bf16[2,320,512]{2,1,0:T(8,128)(2,1)S(1)} %bitcast.19, s32[2,4,320,1]{3,2,1,0:T(8,128)S(1)} %reshape.43.refs_2_, ...), custom_call_target="tpu_custom_call", output_to_operand_aliasing={{0}: (3, {}), {1}: (4, {}), {2}: (5, {})} | custom-call | flops 2348810240 | bytes 10223616 | tf_op jit(solution)/shard_map/attention/attend/pallas_call | solution.py:289
  100.1 6.4 %collective-permute-done.14.refs_9_ = bf16[2,2,512,128]{3,2,1,0:T(8,128)(2,1)S(1)} collective-permute-done((bf16[2,2,512,128]{3,2,1,0:T(8,128)(2,1)S(1)}, bf16[2,2,512,128]{3,2,1,0:T(8,128)(2,1)S(1)}, u32[]{:S(2)}, u32[]{:S(2)}) %collective-permute-start.14) | collective-permute-done | bytes 524320 | tf_op jit(solution)/shard_map/documents/ppermute | solution.py:59
  106.6 8.8 %attend.7 = (f32[2,4,320,128]{3,2,1,0:T(8,128)S(1)}, f32[2,4,320,128]{3,2,1,0:T(8,128)S(1)}, f32[2,4,320,128]{3,2,1,0:T(8,128)S(1)}, bf16[640,512]{1,0:T(8,128)(2,1)}) custom-call(s32[97]{0:T(128)S(1)} %copy-done.4, bf16[2,320,512]{2,1,0:T(8,128)(2,1)S(1)} %bitcast.20, ...), custom_call_target="tpu_custom_call", output_to_operand_aliasing={{0}: (3, {}), {1}: (4, {}), {2}: (5, {})} | custom-call | flops 1342177280 | bytes 9437184 | tf_op jit(solution)/shard_map/attention/attend/pallas_call | solution.py:289
  115.9 2.2 %collective-permute-start.17 = (bf16[640,512]{1,0:T(8,128)(2,1)}, bf16[640,512]{1,0:T(8,128)(2,1)S(1)}, u32[]{:S(2)}, u32[]{:S(2)}) collective-permute-start(bf16[640,512]{1,0:T(8,128)(2,1)} %get-tuple-element.68.refs_0_), channel_id=1, source_target_pairs={{0,6},{1,7},{2,0},{3,1},{4,2},{5,3},{6,4},{7,5},{8,14},{9,15},{10,... | collective-permute-start | bytes 1966088 | tf_op jit(solution)/shard_map/output/ppermute | solution.py:350
  118.1 3.2 %collective-permute-start.19 = (bf16[640,512]{1,0:T(8,128)(2,1)}, bf16[640,512]{1,0:T(8,128)(2,1)S(1)}, u32[]{:S(2)}, u32[]{:S(2)}) collective-permute-start(bf16[640,512]{1,0:T(8,128)(2,1)} %get-tuple-element.68.refs_0_), channel_id=1, source_target_pairs={{0,1},{1,0},{2,3},{3,2},{4,5},{5,4},{6,7},{7,6},{8,9},{9,8},{10,11... | collective-permute-start | bytes 1966088 | tf_op jit(solution)/shard_map/output/ppermute | solution.py:354
  121.3 9.2 %collective-permute-done.15.refs_2_ = bf16[640,512]{1,0:T(8,128)(2,1)S(1)} collective-permute-done((bf16[640,512]{1,0:T(8,128)(2,1)}, bf16[640,512]{1,0:T(8,128)(2,1)S(1)}, u32[]{:S(2)}, u32[]{:S(2)}) %collective-permute-start.15) | collective-permute-done | bytes 655392 | tf_op jit(solution)/shard_map/output/ppermute | solution.py:350
  130.5 3.5 %collective-permute-start.20 = (bf16[640,512]{1,0:T(8,128)(2,1)S(1)}, bf16[640,512]{1,0:T(8,128)(2,1)}, u32[]{:S(2)}, u32[]{:S(2)}) collective-permute-start(bf16[640,512]{1,0:T(8,128)(2,1)S(1)} %collective-permute-done.15.refs_2_), channel_id=1, source_target_pairs={{0,1},{1,0},{2,3},{3,2},{4,5},{5,4},{6,7},{7,6},{8,9},{9,8},{10,11... | collective-permute-start | bytes 1966088 | tf_op jit(solution)/shard_map/output/ppermute | solution.py:354
  139.3 3.8 %project.2.refs_4_ = f32[640,512]{1,0:T(8,128)S(1)} custom-call(s32[8]{0:T(128)S(1)} %pad_add_fusion.place_ref, bf16[4096,512]{1,0:T(8,128)(2,1)S(1)} %copy-done.2, bf16[640,512]{1,0:T(8,128)(2,1)} %get-tuple-element.68.refs_0_, bf16[640,512]{1,0:T(8,128)(2,1)S(1)} %collective-permute-done.19.refs_1_, bf16[640,512]{1,0:T(8,128)(2,1)S(1)} %collective-permute-done.15.refs_2_, ...), custom_call_target="tpu_custom_call" | custom-call | flops 2013265920 | bytes 6291456 | tf_op jit(solution)/shard_map/output/project/pallas_call | solution.py:336
  147.3 2.2 %project.3 = bf16[640,512]{1,0:T(8,128)(2,1)} custom-call(s32[8]{0:T(128)S(1)} %pad_add_fusion.place_ref, bf16[4096,512]{1,0:T(8,128)(2,1)S(1)} %copy-done.3, bf16[320,512]{1,0:T(8,128)(2,1)S(1)} %collective-permute-done.16.refs_0_, bf16[320,512]{1,0:T(8,128)(2,1)S(1)} %collective-permute-done.18.refs_1_, ...), custom_call_target="tpu_custom_call" | custom-call | flops 671088640 | bytes 2097152 | tf_op jit(solution)/shard_map/output/project/pallas_call | solution.py:336
  (84 shorter events, 30.1 us)
Async XLA Ops:
  4.6 37.5 %collective-permute-start.4 = (bf16[6,2,512,128]{3,2,1,0:T(8,128)(2,1)}, bf16[6,2,512,128]{3,2,1,0:T(8,128)(2,1)}, u32[]{:S(2)}, u32[]{:S(2)}) collective-permute-start(bf16[6,2,512,128]{3,2,1,0:T(8,128)(2,1)} %get-tuple-element.49), channel_id=1, source_target_pairs={{0,64},{8,72},{16,80},{24,88},{32,96},{40,104},{48,112},{56,120},{... | collective-permute-start | bytes 4718600 | tf_op jit(solution)/shard_map/documents/ppermute | solution.py:59
  8.1 48.2 %collective-permute-start.5 = (bf16[6,2,512,128]{3,2,1,0:T(8,128)(2,1)}, bf16[6,2,512,128]{3,2,1,0:T(8,128)(2,1)}, u32[]{:S(2)}, u32[]{:S(2)}) collective-permute-start(bf16[6,2,512,128]{3,2,1,0:T(8,128)(2,1)} %get-tuple-element.50), channel_id=1, source_target_pairs={{0,16},{8,24},{16,0},{24,8},{32,48},{40,56},{48,32},{56,40},{64,80... | collective-permute-start | bytes 4718600 | tf_op jit(solution)/shard_map/documents/ppermute | solution.py:59
  15.1 43.3 %collective-permute-start = (bf16[2,2,512,128]{3,2,1,0:T(8,128)(2,1)}, bf16[2,2,512,128]{3,2,1,0:T(8,128)(2,1)S(1)}, u32[]{:S(2)}, u32[]{:S(2)}) collective-permute-start(bf16[2,2,512,128]{3,2,1,0:T(8,128)(2,1)} %get-tuple-element.42), channel_id=1, source_target_pairs={{0,40},{8,48},{16,56},{24,32},{32,72},{40,80},{48,88},{56,64},{64,... | collective-permute-start | bytes 1572872 | tf_op jit(solution)/shard_map/documents/ppermute | solution.py:59
  15.4 45.3 %collective-permute-start.1 = (bf16[2,2,512,128]{3,2,1,0:T(8,128)(2,1)}, bf16[2,2,512,128]{3,2,1,0:T(8,128)(2,1)}, u32[]{:S(2)}, u32[]{:S(2)}) collective-permute-start(bf16[2,2,512,128]{3,2,1,0:T(8,128)(2,1)} %get-tuple-element.43), channel_id=1, source_target_pairs={{0,120},{8,96},{16,104},{24,112},{32,24},{40,0},{48,8},{56,16},{64... | collective-permute-start | bytes 1572872 | tf_op jit(solution)/shard_map/documents/ppermute | solution.py:59
  19.9 47.8 %collective-permute-start.2 = (bf16[2,2,512,128]{3,2,1,0:T(8,128)(2,1)}, bf16[2,2,512,128]{3,2,1,0:T(8,128)(2,1)}, u32[]{:S(2)}, u32[]{:S(2)}) collective-permute-start(bf16[2,2,512,128]{3,2,1,0:T(8,128)(2,1)} %get-tuple-element.44), channel_id=1, source_target_pairs={{0,56},{8,32},{16,40},{24,48},{32,88},{40,64},{48,72},{56,80},{64,... | collective-permute-start | bytes 1572872 | tf_op jit(solution)/shard_map/documents/ppermute | solution.py:59
  42.0 37.1 %collective-permute-start.3 = (bf16[2,2,512,128]{3,2,1,0:T(8,128)(2,1)}, bf16[2,2,512,128]{3,2,1,0:T(8,128)(2,1)S(1)}, u32[]{:S(2)}, u32[]{:S(2)}) collective-permute-start(bf16[2,2,512,128]{3,2,1,0:T(8,128)(2,1)} %get-tuple-element.45), channel_id=1, source_target_pairs={{0,104},{8,112},{16,120},{24,96},{32,8},{40,16},{48,24},{56,0},{64... | collective-permute-start | bytes 1572872 | tf_op jit(solution)/shard_map/documents/ppermute | solution.py:59
  56.3 30.6 %collective-permute-start.10 = (bf16[2,2,512,128]{3,2,1,0:T(8,128)(2,1)S(1)}, bf16[2,2,512,128]{3,2,1,0:T(8,128)(2,1)S(1)}, u32[]{:S(2)}, u32[]{:S(2)}) collective-permute-start(bf16[2,2,512,128]{3,2,1,0:T(8,128)(2,1)S(1)} %copy-done.15), channel_id=1, source_target_pairs={{0,80},{8,88},{16,64},{24,72},{32,112},{40,120},{48,96},{56,104},{... | collective-permute-start | bytes 1572872 | tf_op jit(solution)/shard_map/documents/ppermute | solution.py:59
  58.4 28.6 %collective-permute-start.6 = (bf16[2,2,512,128]{3,2,1,0:T(8,128)(2,1)S(1)}, bf16[2,2,512,128]{3,2,1,0:T(8,128)(2,1)S(1)}, u32[]{:S(2)}, u32[]{:S(2)}) collective-permute-start(bf16[2,2,512,128]{3,2,1,0:T(8,128)(2,1)S(1)} %copy-done.14), channel_id=1, source_target_pairs={{0,32},{8,40},{16,48},{24,56},{32,64},{40,72},{48,80},{56,88},{64,... | collective-permute-start | bytes 1572872 | tf_op jit(solution)/shard_map/documents/ppermute | solution.py:59
  60.7 28.4 %collective-permute-start.7 = (bf16[2,2,512,128]{3,2,1,0:T(8,128)(2,1)S(1)}, bf16[2,2,512,128]{3,2,1,0:T(8,128)(2,1)S(1)}, u32[]{:S(2)}, u32[]{:S(2)}) collective-permute-start(bf16[2,2,512,128]{3,2,1,0:T(8,128)(2,1)S(1)} %copy-done.13), channel_id=1, source_target_pairs={{0,96},{8,104},{16,112},{24,120},{32,0},{40,8},{48,16},{56,24},{64... | collective-permute-start | bytes 1572872 | tf_op jit(solution)/shard_map/documents/ppermute | solution.py:59
  67.7 22.1 %collective-permute-start.8 = (bf16[2,2,512,128]{3,2,1,0:T(8,128)(2,1)S(1)}, bf16[2,2,512,128]{3,2,1,0:T(8,128)(2,1)S(1)}, u32[]{:S(2)}, u32[]{:S(2)}) collective-permute-start(bf16[2,2,512,128]{3,2,1,0:T(8,128)(2,1)S(1)} %copy-done.12), channel_id=1, source_target_pairs={{0,8},{8,16},{16,24},{24,0},{32,40},{40,48},{48,56},{56,32},{64,72... | collective-permute-start | bytes 1572872 | tf_op jit(solution)/shard_map/documents/ppermute | solution.py:59
  79.2 16.2 %collective-permute-start.9 = (bf16[2,2,512,128]{3,2,1,0:T(8,128)(2,1)S(1)}, bf16[2,2,512,128]{3,2,1,0:T(8,128)(2,1)S(1)}, u32[]{:S(2)}, u32[]{:S(2)}) collective-permute-start(bf16[2,2,512,128]{3,2,1,0:T(8,128)(2,1)S(1)} %copy-done.11), channel_id=1, source_target_pairs={{0,24},{8,0},{16,8},{24,16},{32,56},{40,32},{48,40},{56,48},{64,88... | collective-permute-start | bytes 1572872 | tf_op jit(solution)/shard_map/documents/ppermute | solution.py:59
  86.9 13.1 %collective-permute-start.12 = (bf16[2,2,512,128]{3,2,1,0:T(8,128)(2,1)S(1)}, bf16[2,2,512,128]{3,2,1,0:T(8,128)(2,1)S(1)}, u32[]{:S(2)}, u32[]{:S(2)}) collective-permute-start(bf16[2,2,512,128]{3,2,1,0:T(8,128)(2,1)S(1)} %get-tuple-element.65), channel_id=1, source_target_pairs={{0,96},{8,104},{16,112},{24,120},{32,0},{40,8},{48,16},{56,24},{64... | collective-permute-start | bytes 1572872 | tf_op jit(solution)/shard_map/documents/ppermute | solution.py:59
  87.0 13.1 %collective-permute-start.13 = (bf16[2,2,512,128]{3,2,1,0:T(8,128)(2,1)S(1)}, bf16[2,2,512,128]{3,2,1,0:T(8,128)(2,1)S(1)}, u32[]{:S(2)}, u32[]{:S(2)}) collective-permute-start(bf16[2,2,512,128]{3,2,1,0:T(8,128)(2,1)S(1)} %get-tuple-element.66), channel_id=1, source_target_pairs={{0,8},{8,16},{16,24},{24,0},{32,40},{40,48},{48,56},{56,32},{64,72... | collective-permute-start | bytes 1572872 | tf_op jit(solution)/shard_map/documents/ppermute | solution.py:59
  89.1 17.4 %collective-permute-start.14 = (bf16[2,2,512,128]{3,2,1,0:T(8,128)(2,1)S(1)}, bf16[2,2,512,128]{3,2,1,0:T(8,128)(2,1)S(1)}, u32[]{:S(2)}, u32[]{:S(2)}) collective-permute-start(bf16[2,2,512,128]{3,2,1,0:T(8,128)(2,1)S(1)} %get-tuple-element.67), channel_id=1, source_target_pairs={{0,24},{8,0},{16,8},{24,16},{32,56},{40,32},{48,40},{56,48},{64,88... | collective-permute-start | bytes 1572872 | tf_op jit(solution)/shard_map/documents/ppermute | solution.py:59
  89.8 16.8 %collective-permute-start.11 = (bf16[2,2,512,128]{3,2,1,0:T(8,128)(2,1)S(1)}, bf16[2,2,512,128]{3,2,1,0:T(8,128)(2,1)S(1)}, u32[]{:S(2)}, u32[]{:S(2)}) collective-permute-start(bf16[2,2,512,128]{3,2,1,0:T(8,128)(2,1)S(1)} %get-tuple-element.64), channel_id=1, source_target_pairs={{0,32},{8,40},{16,48},{24,56},{32,64},{40,72},{48,80},{56,88},{64,... | collective-permute-start | bytes 1572872 | tf_op jit(solution)/shard_map/documents/ppermute | solution.py:59
  115.4 15.1 %collective-permute-start.15 = (bf16[640,512]{1,0:T(8,128)(2,1)}, bf16[640,512]{1,0:T(8,128)(2,1)S(1)}, u32[]{:S(2)}, u32[]{:S(2)}) collective-permute-start(bf16[640,512]{1,0:T(8,128)(2,1)} %get-tuple-element.68.refs_0_), channel_id=1, source_target_pairs={{0,2},{1,3},{2,4},{3,5},{4,6},{5,7},{6,0},{7,1},{8,10},{9,11},{10,... | collective-permute-start | bytes 1966088 | tf_op jit(solution)/shard_map/output/ppermute | solution.py:350
  115.9 18.1 %collective-permute-start.17 = (bf16[640,512]{1,0:T(8,128)(2,1)}, bf16[640,512]{1,0:T(8,128)(2,1)S(1)}, u32[]{:S(2)}, u32[]{:S(2)}) collective-permute-start(bf16[640,512]{1,0:T(8,128)(2,1)} %get-tuple-element.68.refs_0_), channel_id=1, source_target_pairs={{0,6},{1,7},{2,0},{3,1},{4,2},{5,3},{6,4},{7,5},{8,14},{9,15},{10,... | collective-permute-start | bytes 1966088 | tf_op jit(solution)/shard_map/output/ppermute | solution.py:350
  118.1 18.9 %collective-permute-start.19 = (bf16[640,512]{1,0:T(8,128)(2,1)}, bf16[640,512]{1,0:T(8,128)(2,1)S(1)}, u32[]{:S(2)}, u32[]{:S(2)}) collective-permute-start(bf16[640,512]{1,0:T(8,128)(2,1)} %get-tuple-element.68.refs_0_), channel_id=1, source_target_pairs={{0,1},{1,0},{2,3},{3,2},{4,5},{5,4},{6,7},{7,6},{8,9},{9,8},{10,11... | collective-permute-start | bytes 1966088 | tf_op jit(solution)/shard_map/output/ppermute | solution.py:354
  130.5 6.6 %collective-permute-start.20 = (bf16[640,512]{1,0:T(8,128)(2,1)S(1)}, bf16[640,512]{1,0:T(8,128)(2,1)}, u32[]{:S(2)}, u32[]{:S(2)}) collective-permute-start(bf16[640,512]{1,0:T(8,128)(2,1)S(1)} %collective-permute-done.15.refs_2_), channel_id=1, source_target_pairs={{0,1},{1,0},{2,3},{3,2},{4,5},{5,4},{6,7},{7,6},{8,9},{9,8},{10,11... | collective-permute-start | bytes 1966088 | tf_op jit(solution)/shard_map/output/ppermute | solution.py:354
  134.0 3.1 %collective-permute-start.21 = (bf16[640,512]{1,0:T(8,128)(2,1)S(1)}, bf16[640,512]{1,0:T(8,128)(2,1)}, u32[]{:S(2)}, u32[]{:S(2)}) collective-permute-start(bf16[640,512]{1,0:T(8,128)(2,1)S(1)} %collective-permute-done.17.refs_3_), channel_id=1, source_target_pairs={{0,1},{1,0},{2,3},{3,2},{4,5},{5,4},{6,7},{7,6},{8,9},{9,8},{10,11... | collective-permute-start | bytes 1966088 | tf_op jit(solution)/shard_map/output/ppermute | solution.py:354
  134.1 10.0 %collective-permute-start.16 = (bf16[320,512]{1,0:T(8,128)(2,1)S(1)}, bf16[320,512]{1,0:T(8,128)(2,1)S(1)}, u32[]{:S(2)}, u32[]{:S(2)}) collective-permute-start(bf16[320,512]{1,0:T(8,128)(2,1)S(1)} %slice.28), channel_id=1, source_target_pairs={{0,2},{1,3},{2,4},{3,5},{4,6},{5,7},{6,0},{7,1},{8,10},{9,11},{10,... | collective-permute-start | bytes 983048 | tf_op jit(solution)/shard_map/output/ppermute | solution.py:350
  135.1 9.1 %collective-permute-start.18 = (bf16[320,512]{1,0:T(8,128)(2,1)S(1)}, bf16[320,512]{1,0:T(8,128)(2,1)S(1)}, u32[]{:S(2)}, u32[]{:S(2)}) collective-permute-start(bf16[320,512]{1,0:T(8,128)(2,1)S(1)} %slice.29), channel_id=1, source_target_pairs={{0,6},{1,7},{2,0},{3,1},{4,2},{5,3},{6,4},{7,5},{8,14},{9,15},{10,... | collective-permute-start | bytes 983048 | tf_op jit(solution)/shard_map/output/ppermute | solution.py:350
  144.2 2.6 %collective-permute-start.22 = (bf16[320,512]{1,0:T(8,128)(2,1)S(1)}, bf16[320,512]{1,0:T(8,128)(2,1)S(1)}, u32[]{:S(2)}, u32[]{:S(2)}) collective-permute-start(bf16[320,512]{1,0:T(8,128)(2,1)S(1)} %collective-permute-done.16.refs_0_), channel_id=1, source_target_pairs={{0,1},{1,0},{2,3},{3,2},{4,5},{5,4},{6,7},{7,6},{8,9},{9,8},{10,11... | collective-permute-start | bytes 983048 | tf_op jit(solution)/shard_map/output/ppermute | solution.py:354
  145.5 1.7 %collective-permute-start.23 = (bf16[320,512]{1,0:T(8,128)(2,1)S(1)}, bf16[320,512]{1,0:T(8,128)(2,1)S(1)}, u32[]{:S(2)}, u32[]{:S(2)}) collective-permute-start(bf16[320,512]{1,0:T(8,128)(2,1)S(1)} %collective-permute-done.18.refs_1_), channel_id=1, source_target_pairs={{0,1},{1,0},{2,3},{3,2},{4,5},{5,4},{6,7},{7,6},{8,9},{9,8},{10,11... | collective-permute-start | bytes 983048 | tf_op jit(solution)/shard_map/output/ppermute | solution.py:354
  (16 other events, 205.3 us)
